TPU v7x, 128 devices: a whole 4x4x4 slice. The times are simulated.
128 devices in a mesh: dp: 32 (over x, z_lo, y), tensor: 4 (over z_hi, core).
Axes of the slice: x: 4, y: 4, z: 4 (z_hi: 2, z_lo: 2; z = z_hi * 2 + z_lo), core: 2. Of those that a mesh axis runs over, the one named last changes fastest.
Arguments:
- tokens: bfloat16 [8192, 1536], P(('dp', 'tensor')), may hold values from -6 to 6
- cotangent: bfloat16 [8192, 1536], P(('dp', 'tensor')), may hold values from -6 to 6
- segments: int32 [8192], P('dp'), may hold values from 0 to 7, as said below
- routes: int32 [8192, 6], P('dp'), may hold values from 0 to 7, all different within a row; in each aligned block of 256 rows (0 to 255, 256 to 511, ...) at most 256 rows name the same one
- gate_weights: float32 [8192, 6], P('dp'), may hold values from 0.1 to 0.3
- norm_gain: float32 [1536], replicated, may hold values from 0.5 to 1.5
- w_zx: bfloat16 [1536, 2, 3072], P('dp', None, 'tensor'), may hold values from -0.15625 to 0.15625
- w_bc: bfloat16 [1536, 2, 128], P('dp'), may hold values from -0.15625 to 0.15625
- w_dt: bfloat16 [1536, 48], P('dp', 'tensor'), may hold values from -0.15625 to 0.15625
- conv_x: float32 [4, 3072], replicated, may hold values from -3 to 3
- conv_bc: float32 [4, 2, 128], replicated, may hold values from -3 to 3
- dt_bias: float32 [48], replicated, may hold values from -4 to -1
- a_log: float32 [48], replicated, may hold values from -12 to 1
- d_skip: float32 [48], replicated, may hold values from 0.5 to 1.5
- mix_gain: float32 [3072], replicated, may hold values from 0.5 to 1.5
- w_out: bfloat16 [3072, 1536], P('tensor', 'dp'), may hold values from -0.109375 to 0.109375
- post_gain: float32 [1536], replicated, may hold values from 0.5 to 1.5
- exp_gate: bfloat16 [8, 1536, 512], P(None, 'dp', 'tensor'), may hold values from -0.15625 to 0.15625
- exp_up: bfloat16 [8, 1536, 512], P(None, 'dp', 'tensor'), may hold values from -0.15625 to 0.15625
- exp_down: bfloat16 [8, 512, 1536], P(None, 'tensor', 'dp'), may hold values from -0.25 to 0.25
- sh_gate: bfloat16 [1536, 1024], P('dp', 'tensor'), may hold values from -0.15625 to 0.15625
- sh_up: bfloat16 [1536, 1024], P('dp', 'tensor'), may hold values from -0.15625 to 0.15625
- sh_down: bfloat16 [1024, 1536], P('tensor', 'dp'), may hold values from -0.1875 to 0.1875
Outputs:
- block_out: float32 [8192, 1536], P(('dp', 'tensor'))
- grad_tokens: float32 [8192, 1536], P(('dp', 'tensor'))
- grad_norm_gain: float32 [1536], replicated
- grad_w_zx: float32 [1536, 2, 3072], P('dp', None, 'tensor')
- grad_w_bc: float32 [1536, 2, 128], P('dp')
- grad_w_dt: float32 [1536, 48], P('dp', 'tensor')
- grad_conv_x: float32 [4, 3072], replicated
- grad_conv_bc: float32 [4, 2, 128], replicated
- grad_dt_bias: float32 [48], replicated
- grad_a_log: float32 [48], replicated
- grad_d_skip: float32 [48], replicated
- grad_mix_gain: float32 [3072], replicated
- grad_w_out: float32 [3072, 1536], P('tensor', 'dp')
- grad_post_gain: float32 [1536], replicated
- grad_exp_gate: float32 [8, 1536, 512], P(None, 'dp', 'tensor')
- grad_exp_up: float32 [8, 1536, 512], P(None, 'dp', 'tensor')
- grad_exp_down: float32 [8, 512, 1536], P(None, 'tensor', 'dp')
- grad_sh_gate: float32 [1536, 1024], P('dp', 'tensor')
- grad_sh_up: float32 [1536, 1024], P('dp', 'tensor')
- grad_sh_down: float32 [1024, 1536], P('tensor', 'dp')
Inputs may be any that keep to these rules, and one draw needn't show every extreme that they name: `routes`: within the rows of one index of dp (aligned blocks of 256 rows) no expert is named by more than 256 rows, a bound that some block reaches; a row names 6 different experts. `segments`: document numbers never fall along the rows; every number from 0 to 7 has at least one row.
All inputs are finite; a program needn't handle non-finite values.
Results may differ from a plain program's by a relative error of at most 0.018.
Values may be sent and summed in bfloat16 or wider, within the bound.
No kernel may reach another device: no remote copies, remote signals or barrier semaphores. Data moves between devices by JAX's collectives and lax.ppermute only.
A program may use at most 192 MiB of HBM per device.

v0:
```python
import jax
import jax.numpy as jnp
from jax import lax
from jax.sharding import PartitionSpec as P

SCAN_BLOCK = 256
CAP = 256


eps = 1e-05
highest = lax.Precision.HIGHEST


def from_behind(value, axis, steps):
    count = lax.axis_size(axis)
    leading, last = (max(0, -steps), min(count, count - steps))
    return lax.ppermute(value, axis, [(source, source + steps) for source in range(leading, last)])


def carried_in(shard, axis, combine, identity, reverse):
    peers, here = (lax.axis_size(axis), lax.axis_index(axis))
    everything = jax.tree.map(lambda part: lax.all_gather(part, axis), shard)
    start = jax.tree.map(
        lambda part, zero: jnp.broadcast_to(jnp.asarray(zero, part.dtype), part.shape),
        shard,
        identity,
    )

    def turn(k, before):
        at = peers - 1 - k if reverse else k
        reached = at > here if reverse else at < here
        new = combine(before, jax.tree.map(lambda part: part[at], everything))
        return jax.tree.map(lambda a, b: jnp.where(reached, a, b), new, before)

    return lax.fori_loop(0, peers, turn, start)


def silu_slope(value):
    sigma = jax.nn.sigmoid(value)
    return sigma * (1.0 + value * (1.0 - sigma))


def block_scan(values, b_rows, c_rows, steps_dt, log_decay, resets, skip_gain, carry_start):
    total_rows = values.shape[0]
    head_count = values.shape[1]
    head_dim = values.shape[2]
    state_dim = b_rows.shape[1]
    block_count = total_rows // SCAN_BLOCK

    def block_step(carried, pieces):
        x_blk, b_blk, c_blk, dt_blk, ld_blk, rs_blk = pieces
        cum_log = jnp.cumsum(ld_blk, 0)
        run_ids = jnp.cumsum(rs_blk)
        row_ids = lax.broadcasted_iota(jnp.int32, (SCAN_BLOCK, SCAN_BLOCK), 0)
        col_ids = lax.broadcasted_iota(jnp.int32, (SCAN_BLOCK, SCAN_BLOCK), 1)
        keep_mask = (row_ids >= col_ids) & (run_ids[:, None] == run_ids[None, :])
        gaps = cum_log[:, None, :] - cum_log[None, :, :]
        decays = jnp.exp(jnp.where(keep_mask[:, :, None], gaps, -jnp.inf))
        inner_cb = jnp.dot(c_blk, b_blk.T, precision=highest)
        weights = decays * inner_cb[:, :, None] * dt_blk[None, :, :]
        y_blk = jnp.einsum("ijh,jhp->ihp", weights, x_blk, precision=highest)
        opening = jnp.exp(cum_log) * (run_ids == 0).astype(jnp.float32)[:, None]
        y_blk = y_blk + opening[:, :, None] * jnp.einsum(
            "in,hpn->ihp", c_blk, carried, precision=highest
        )
        y_blk = y_blk + skip_gain[None, :, None] * x_blk
        last_run = run_ids[SCAN_BLOCK - 1]
        closing = (
            jnp.where(
                (run_ids == last_run)[:, None],
                jnp.exp(cum_log[SCAN_BLOCK - 1][None, :] - cum_log),
                0.0,
            )
            * dt_blk
        )
        keep_old = jnp.exp(cum_log[SCAN_BLOCK - 1]) * (last_run == 0).astype(jnp.float32)
        updated = carried * keep_old[:, None, None] + jnp.einsum(
            "jh,jhp,jn->hpn", closing, x_blk, b_blk, precision=highest
        )
        return (updated, y_blk)

    pieces = (
        values.reshape(block_count, SCAN_BLOCK, head_count, head_dim),
        b_rows.reshape(block_count, SCAN_BLOCK, state_dim),
        c_rows.reshape(block_count, SCAN_BLOCK, state_dim),
        steps_dt.reshape(block_count, SCAN_BLOCK, head_count),
        log_decay.reshape(block_count, SCAN_BLOCK, head_count),
        resets.reshape(block_count, SCAN_BLOCK),
    )
    final_state, y_blocks = lax.scan(jax.checkpoint(block_step), carry_start, pieces)
    return (y_blocks.reshape(total_rows, head_count, head_dim), final_state)


def fetch_weights(w_zx, w_bc, w_dt, w_out, exp_gate, exp_up, exp_down, sh_gate, sh_up, sh_down):
    return (
        lax.all_gather(w_zx, "dp", axis=0, tiled=True),
        lax.all_gather(w_bc, "dp", axis=0, tiled=True),
        lax.all_gather(w_dt, "dp", axis=0, tiled=True),
        lax.all_gather(w_out, "dp", axis=1, tiled=True),
        lax.all_gather(exp_gate, "dp", axis=1, tiled=True),
        lax.all_gather(exp_up, "dp", axis=1, tiled=True),
        lax.all_gather(exp_down, "dp", axis=2, tiled=True),
        lax.all_gather(sh_gate, "dp", axis=0, tiled=True),
        lax.all_gather(sh_up, "dp", axis=0, tiled=True),
        lax.all_gather(sh_down, "dp", axis=1, tiled=True),
    )


def link_states(earlier, later):
    return (later[1][:, None, None] * earlier[0] + later[0], earlier[1] * later[1])


def place_slice(piece, full_size, offset, along_dim):
    shape_out = piece.shape[:along_dim] + (full_size,) + piece.shape[along_dim + 1 :]
    return lax.dynamic_update_slice_in_dim(
        jnp.zeros(shape_out, jnp.float32), piece, offset, along_dim
    )


def body(
    tokens,
    cotangent,
    segments,
    routes,
    gate_weights,
    norm_gain,
    w_zx,
    w_bc,
    w_dt,
    conv_x,
    conv_bc,
    dt_bias,
    a_log,
    d_skip,
    mix_gain,
    w_out,
    post_gain,
    exp_gate,
    exp_up,
    exp_down,
    sh_gate,
    sh_up,
    sh_down,
):
    tensor_count = lax.axis_size("tensor")
    tensor_rank = lax.axis_index("tensor")
    block_rows = segments.shape[0]
    model_dim = tokens.shape[1]
    inner_local = w_zx.shape[2]
    heads_local = w_dt.shape[1]
    head_dim = inner_local // heads_local
    state_dim = w_bc.shape[2]
    bc_rows_local = w_bc.shape[0]
    conv_taps = conv_x.shape[0]
    edge_rows = conv_taps - 1
    inner_total = inner_local * tensor_count
    head_total = heads_local * tensor_count
    experts = exp_gate.shape[0]
    top_count = routes.shape[1]
    zx_full, bc_full, dt_full, out_full, eg_full, eu_full, ed_full, sg_full, su_full, sd_full = (
        fetch_weights(w_zx, w_bc, w_dt, w_out, exp_gate, exp_up, exp_down, sh_gate, sh_up, sh_down)
    )
    head_start = tensor_rank * heads_local
    chan_start = tensor_rank * inner_local
    bias_local = lax.dynamic_slice_in_dim(dt_bias, head_start, heads_local)
    alog_local = lax.dynamic_slice_in_dim(a_log, head_start, heads_local)
    skip_local = lax.dynamic_slice_in_dim(d_skip, head_start, heads_local)
    mixg_local = lax.dynamic_slice_in_dim(mix_gain, chan_start, inner_local)
    convx_local = lax.dynamic_slice_in_dim(conv_x, chan_start, inner_local, 1)
    conv_all = jnp.concatenate([convx_local, conv_bc.reshape(conv_taps, 2 * state_dim)], 1)
    x_own = tokens.astype(jnp.float32)
    scale_in = lax.rsqrt(jnp.mean(x_own * x_own, -1, keepdims=True) + eps)
    normed_own = (x_own * scale_in * norm_gain).astype(jnp.bfloat16)
    normed_in, grad_rows = (
        lax.all_gather(normed_own, "tensor", axis=0, tiled=True),
        lax.all_gather(cotangent, "tensor", axis=0, tiled=True),
    )
    proj_zx = jnp.dot(
        normed_in, zx_full.reshape(model_dim, 2 * inner_local), preferred_element_type=jnp.float32
    )
    proj_bc = jnp.dot(
        normed_in, bc_full.reshape(model_dim, 2 * state_dim), preferred_element_type=jnp.float32
    )
    proj_dt = jnp.dot(normed_in, dt_full, preferred_element_type=jnp.float32)
    gate_z = proj_zx[:, :inner_local]
    pre_conv = jnp.concatenate([proj_zx[:, inner_local:], proj_bc], 1)
    seg_float = segments.astype(jnp.float32)
    tail_vals, tail_ids = from_behind(
        (pre_conv[block_rows - edge_rows :], seg_float[block_rows - edge_rows :]), "dp", 1
    )
    pre_ext = jnp.concatenate([tail_vals, pre_conv], 0)
    ids_ext = jnp.concatenate([tail_ids, seg_float])
    global_rows = lax.axis_index("dp") * block_rows + jnp.arange(block_rows, dtype=jnp.int32)
    lag_masks = []
    for shift_back in range(conv_taps):
        start_row = edge_rows - shift_back
        same_doc = (ids_ext[start_row : start_row + block_rows] == seg_float) & (
            global_rows >= shift_back
        )
        lag_masks.append(same_doc.astype(jnp.float32))
    doc_resets = 1.0 - lag_masks[1]

    def front(ext_values, dt_raw, conv_weights, bias_vals, alog_vals, skip_vals):
        conv_sum = jnp.zeros((block_rows, conv_weights.shape[1]), jnp.float32)
        for shift_back in range(conv_taps):
            start_row = edge_rows - shift_back
            conv_sum = (
                conv_sum
                + conv_weights[conv_taps - 1 - shift_back][None, :]
                * ext_values[start_row : start_row + block_rows]
                * lag_masks[shift_back][:, None]
            )
        conv_act = jax.nn.silu(conv_sum)
        x_heads = conv_act[:, :inner_local].reshape(block_rows, heads_local, head_dim)
        b_rows = conv_act[:, inner_local : inner_local + state_dim]
        c_rows = conv_act[:, inner_local + state_dim :]
        steps_dt = jax.nn.softplus(dt_raw + bias_vals)
        log_decay = -steps_dt * jnp.exp(alog_vals)
        y_heads, final_state = block_scan(
            x_heads,
            b_rows,
            c_rows,
            steps_dt,
            log_decay,
            doc_resets,
            skip_vals,
            jnp.zeros((heads_local, head_dim, state_dim), jnp.float32),
        )
        decay_all = jnp.exp(jnp.sum(log_decay, 0)) * (jnp.sum(doc_resets) == 0.0).astype(
            jnp.float32
        )
        return (y_heads, c_rows, log_decay, final_state, decay_all)

    front_out, front_pull = jax.vjp(
        front, pre_ext, proj_dt, conv_all, bias_local, alog_local, skip_local
    )
    y_heads, c_rows, log_decay, final_state, decay_all = front_out
    identity_pair = (jnp.zeros_like(final_state), jnp.ones_like(decay_all))
    incoming, ignored_decay = carried_in(
        (final_state, decay_all), "dp", link_states, identity_pair, False
    )

    def back_half(y_vals, c_vals, log_vals, enter_state, z_vals):
        run_count = jnp.cumsum(doc_resets)
        opening = jnp.exp(jnp.cumsum(log_vals, 0)) * (run_count == 0.0).astype(jnp.float32)[:, None]
        y_all = y_vals + opening[:, :, None] * jnp.einsum(
            "in,hpn->ihp", c_vals, enter_state, precision=highest
        )
        return y_all.reshape(block_rows, inner_local) * jax.nn.silu(z_vals)

    gated, back_pull = jax.vjp(back_half, y_heads, c_rows, log_decay, incoming, gate_z)
    squares = jnp.sum(gated * gated, -1)
    mixer_in = (gated * mixg_local).astype(jnp.bfloat16)
    partial_out = jnp.dot(mixer_in, out_full, preferred_element_type=jnp.float32)
    projected, squares_own = (
        lax.psum_scatter(partial_out, "tensor", scatter_dimension=0, tiled=True),
        lax.psum_scatter(squares, "tensor", scatter_dimension=0, tiled=True),
    )
    scale_mix = lax.rsqrt(squares_own / inner_total + eps)
    middle = x_own + scale_mix[:, None] * projected
    scale_post = lax.rsqrt(jnp.mean(middle * middle, -1, keepdims=True) + eps)
    post_own = (middle * scale_post * post_gain).astype(jnp.bfloat16)
    normed_post = lax.all_gather(post_own, "tensor", axis=0, tiled=True)
    flat_routes = routes.reshape(-1)
    pair_count = flat_routes.shape[0]
    route_hot = (flat_routes[:, None] == jnp.arange(experts, dtype=jnp.int32)[None, :]).astype(
        jnp.int32
    )
    slot_index = jnp.sum((jnp.cumsum(route_hot, 0) - route_hot) * route_hot, 1)
    dest_rows = flat_routes * CAP + slot_index
    pair_ids = jnp.arange(pair_count, dtype=jnp.int32)
    source_rows = (
        jnp.full((experts * CAP,), block_rows, jnp.int32).at[dest_rows].set(pair_ids // top_count)
    )
    padded_post = jnp.concatenate([normed_post, jnp.zeros((1, model_dim), jnp.bfloat16)], 0)
    buffer = padded_post[source_rows].reshape(experts, CAP, model_dim)
    pre_gate = jnp.einsum("ecd,edf->ecf", buffer, eg_full, preferred_element_type=jnp.float32)
    pre_up = jnp.einsum("ecd,edf->ecf", buffer, eu_full, preferred_element_type=jnp.float32)
    expert_act = (jax.nn.silu(pre_gate) * pre_up).astype(jnp.bfloat16)
    expert_out = jnp.einsum("ecf,efd->ecd", expert_act, ed_full, preferred_element_type=jnp.float32)
    picked = expert_out.reshape(experts * CAP, model_dim)[dest_rows].reshape(
        block_rows, top_count, model_dim
    )
    routed = jnp.sum(picked * gate_weights[:, :, None], 1)
    sh_pre_g = jnp.dot(normed_post, sg_full, preferred_element_type=jnp.float32)
    sh_pre_u = jnp.dot(normed_post, su_full, preferred_element_type=jnp.float32)
    sh_act = (jax.nn.silu(sh_pre_g) * sh_pre_u).astype(jnp.bfloat16)
    shared_out = jnp.dot(sh_act, sd_full, preferred_element_type=jnp.float32)
    ffn_own = lax.psum_scatter(routed + shared_out, "tensor", scatter_dimension=0, tiled=True)
    block_out = middle + ffn_own
    held = lax.optimization_barrier(
        (grad_rows, w_zx, w_bc, w_dt, w_out, exp_gate, exp_up, exp_down, sh_gate, sh_up, sh_down)
    )
    grad_rows = held[0]
    zx_full, bc_full, dt_full, out_full, eg_full, eu_full, ed_full, sg_full, su_full, sd_full = (
        fetch_weights(
            held[1],
            held[2],
            held[3],
            held[4],
            held[5],
            held[6],
            held[7],
            held[8],
            held[9],
            held[10],
        )
    )
    grad_sd = jnp.einsum("tf,td->fd", sh_act, grad_rows, preferred_element_type=jnp.float32)
    d_sh_act = jnp.einsum("td,fd->tf", grad_rows, sd_full, preferred_element_type=jnp.float32)
    d_sh_g = (d_sh_act * sh_pre_u * silu_slope(sh_pre_g)).astype(jnp.bfloat16)
    d_sh_u = (d_sh_act * jax.nn.silu(sh_pre_g)).astype(jnp.bfloat16)
    grad_sg = jnp.einsum("td,tf->df", normed_post, d_sh_g, preferred_element_type=jnp.float32)
    grad_su = jnp.einsum("td,tf->df", normed_post, d_sh_u, preferred_element_type=jnp.float32)
    d_post = jnp.einsum("tf,df->td", d_sh_g, sg_full, preferred_element_type=jnp.float32)
    d_post = d_post + jnp.einsum("tf,df->td", d_sh_u, su_full, preferred_element_type=jnp.float32)
    weighted = (grad_rows.astype(jnp.float32)[:, None, :] * gate_weights[:, :, None]).astype(
        jnp.bfloat16
    )
    weighted = weighted.reshape(pair_count, model_dim)
    slot_source = jnp.full((experts * CAP,), pair_count, jnp.int32).at[dest_rows].set(pair_ids)
    padded_grad = jnp.concatenate([weighted, jnp.zeros((1, model_dim), jnp.bfloat16)], 0)
    d_buffer = padded_grad[slot_source].reshape(experts, CAP, model_dim)
    grad_ed = jnp.einsum("ecf,ecd->efd", expert_act, d_buffer, preferred_element_type=jnp.float32)
    d_act = jnp.einsum("ecd,efd->ecf", d_buffer, ed_full, preferred_element_type=jnp.float32)
    d_pre_g = (d_act * pre_up * silu_slope(pre_gate)).astype(jnp.bfloat16)
    d_pre_u = (d_act * jax.nn.silu(pre_gate)).astype(jnp.bfloat16)
    grad_eg = jnp.einsum("ecd,ecf->edf", buffer, d_pre_g, preferred_element_type=jnp.float32)
    grad_eu = jnp.einsum("ecd,ecf->edf", buffer, d_pre_u, preferred_element_type=jnp.float32)
    d_slots = jnp.einsum("ecf,edf->ecd", d_pre_g, eg_full, preferred_element_type=jnp.float32)
    d_slots = d_slots + jnp.einsum(
        "ecf,edf->ecd", d_pre_u, eu_full, preferred_element_type=jnp.float32
    )
    d_pairs = d_slots.reshape(experts * CAP, model_dim)[dest_rows].reshape(
        block_rows, top_count, model_dim
    )
    d_post = d_post + jnp.sum(d_pairs, 1)
    d_post_own = lax.psum_scatter(d_post, "tensor", scatter_dimension=0, tiled=True)
    grad_post_gain = jnp.sum(d_post_own * middle * scale_post, 0)
    d_scaled = d_post_own * post_gain
    d_middle = (
        cotangent.astype(jnp.float32)
        + scale_post * d_scaled
        - middle * scale_post**3 * jnp.mean(d_scaled * middle, -1, keepdims=True)
    )
    d_mix = lax.optimization_barrier(d_middle.astype(jnp.bfloat16)).astype(jnp.float32)
    d_scale = jnp.sum(d_mix * projected, -1)
    norm_coeff = -d_scale * scale_mix**3 / inner_total
    d_proj_own = lax.optimization_barrier((d_mix * scale_mix[:, None]).astype(jnp.bfloat16)).astype(
        jnp.float32
    )
    d_proj_all, coeff_all = (
        lax.all_gather(d_proj_own, "tensor", axis=0, tiled=True),
        lax.all_gather(norm_coeff, "tensor", axis=0, tiled=True),
    )
    d_proj = d_proj_all.astype(jnp.bfloat16)
    grad_out = jnp.einsum("ti,td->id", mixer_in, d_proj, preferred_element_type=jnp.float32)
    d_mixer_in = jnp.einsum("td,id->ti", d_proj, out_full, preferred_element_type=jnp.float32)
    grad_mixg_local = jnp.sum(d_mixer_in * gated, 0)
    d_gated = d_mixer_in * mixg_local + coeff_all[:, None] * gated
    grad_y, grad_c, grad_logs, grad_enter, grad_z = back_pull(d_gated)
    later_grad, ignored_back = carried_in(
        (grad_enter, decay_all), "dp", link_states, identity_pair, True
    )
    grad_decay = jnp.sum(later_grad * incoming, (1, 2))
    grad_ext, grad_dt_raw, grad_conv, grad_bias, grad_alog, grad_skip = front_pull(
        (grad_y, grad_c, grad_logs, later_grad, grad_decay)
    )
    tail_grad = from_behind(grad_ext[:edge_rows], "dp", -1)
    grad_pre = grad_ext[edge_rows:].at[block_rows - edge_rows :].add(tail_grad)
    d_zx = jnp.concatenate([grad_z, grad_pre[:, :inner_local]], 1).astype(jnp.bfloat16)
    d_bc = grad_pre[:, inner_local:].astype(jnp.bfloat16)
    d_dt = grad_dt_raw.astype(jnp.bfloat16)
    grad_zx = jnp.einsum("td,tc->dc", normed_in, d_zx, preferred_element_type=jnp.float32).reshape(
        model_dim, 2, inner_local
    )
    grad_bc = jnp.einsum("td,tc->dc", normed_in, d_bc, preferred_element_type=jnp.float32).reshape(
        model_dim, 2, state_dim
    )
    grad_dt = jnp.einsum("td,tc->dc", normed_in, d_dt, preferred_element_type=jnp.float32)
    d_in = jnp.einsum(
        "tc,dc->td",
        d_zx,
        zx_full.reshape(model_dim, 2 * inner_local),
        preferred_element_type=jnp.float32,
    )
    d_in = d_in + jnp.einsum(
        "tc,dc->td",
        d_bc,
        bc_full.reshape(model_dim, 2 * state_dim),
        preferred_element_type=jnp.float32,
    )
    d_in = d_in + jnp.einsum("tc,dc->td", d_dt, dt_full, preferred_element_type=jnp.float32)
    d_in_own = lax.psum_scatter(d_in, "tensor", scatter_dimension=0, tiled=True)
    grad_norm = jnp.sum(d_in_own * x_own * scale_in, 0)
    d_scaled_in = d_in_own * norm_gain
    grad_tokens = (
        d_middle
        + scale_in * d_scaled_in
        - x_own * scale_in**3 * jnp.mean(d_scaled_in * x_own, -1, keepdims=True)
    )
    sharded = (
        lax.psum_scatter(grad_zx, "dp", scatter_dimension=0, tiled=True),
        lax.psum_scatter(grad_dt, "dp", scatter_dimension=0, tiled=True),
        lax.psum_scatter(grad_out, "dp", scatter_dimension=1, tiled=True),
        lax.psum_scatter(grad_eg, "dp", scatter_dimension=1, tiled=True),
        lax.psum_scatter(grad_eu, "dp", scatter_dimension=1, tiled=True),
        lax.psum_scatter(grad_ed, "dp", scatter_dimension=2, tiled=True),
        lax.psum_scatter(grad_sg, "dp", scatter_dimension=0, tiled=True),
        lax.psum_scatter(grad_su, "dp", scatter_dimension=0, tiled=True),
        lax.psum_scatter(grad_sd, "dp", scatter_dimension=1, tiled=True),
    )
    summed = lax.psum(
        (
            grad_norm,
            grad_post_gain,
            grad_bc,
            place_slice(grad_conv[:, :inner_local], inner_total, chan_start, 1),
            grad_conv[:, inner_local:].reshape(conv_taps, 2, state_dim),
            place_slice(grad_bias, head_total, head_start, 0),
            place_slice(grad_alog, head_total, head_start, 0),
            place_slice(grad_skip, head_total, head_start, 0),
            place_slice(grad_mixg_local, inner_total, chan_start, 0),
        ),
        ("dp", "tensor"),
    )
    grad_bc_own = lax.dynamic_slice_in_dim(
        summed[2], lax.axis_index("dp") * bc_rows_local, bc_rows_local, 0
    )
    return (
        block_out,
        grad_tokens,
        summed[0],
        sharded[0],
        grad_bc_own,
        sharded[1],
        summed[3],
        summed[4],
        summed[5],
        summed[6],
        summed[7],
        summed[8],
        sharded[2],
        summed[1],
        sharded[3],
        sharded[4],
        sharded[5],
        sharded[6],
        sharded[7],
        sharded[8],
    )


def solution(mesh):
    in_specs = (
        P(("dp", "tensor"), None),
        P(("dp", "tensor"), None),
        P("dp"),
        P("dp", None),
        P("dp", None),
        P(),
        P("dp", None, "tensor"),
        P("dp", None, None),
        P("dp", "tensor"),
        P(),
        P(),
        P(),
        P(),
        P(),
        P(),
        P("tensor", "dp"),
        P(),
        P(None, "dp", "tensor"),
        P(None, "dp", "tensor"),
        P(None, "tensor", "dp"),
        P("dp", "tensor"),
        P("dp", "tensor"),
        P("tensor", "dp"),
    )
    out_specs = (
        P(("dp", "tensor"), None),
        P(("dp", "tensor"), None),
        P(),
        P("dp", None, "tensor"),
        P("dp", None, None),
        P("dp", "tensor"),
        P(),
        P(),
        P(),
        P(),
        P(),
        P(),
        P("tensor", "dp"),
        P(),
        P(None, "dp", "tensor"),
        P(None, "dp", "tensor"),
        P(None, "tensor", "dp"),
        P("dp", "tensor"),
        P("dp", "tensor"),
        P("tensor", "dp"),
    )
    return jax.shard_map(body, mesh=mesh, in_specs=in_specs, out_specs=out_specs, check_vma=False)
```

profile of v0, /device:TPU:1, one launch (start us, length us, event | category | flops | bytes accessed | tf_op | source)
XLA Modules:
  0.0 4235.5 jit_solution(11556995421140598915)
XLA Ops:
  12.8 69.5 %all-gather.3 = bf16[32,48,12]{1,2,0:T(8,128)(2,1)S(1)} all-gather(bf16[1,48,12]{1,2,0:T(8,128)(2,1)} %bitcast.349), channel_id=1, replica_groups=mesh['dp'=32,'tensor'=4] {'dp'}, dimensions={0}, use_global_device_ids=true | all-gather | bytes 38016 | tf_op jit(solution)/shard_map/all_gather | solution.py:98
  113.4 68.8 %all_gather.95 = bf16[1536,2,128]{2,1,0:T(2,128)(2,1)S(1)} all-gather(bf16[48,2,128]{2,1,0:T(2,128)(2,1)S(1)} %copy-done.73), channel_id=1, replica_groups=mesh['dp'=32,'tensor'=4] {'dp'}, dimensions={0}, use_global_device_ids=true | all-gather | bytes 811008 | tf_op jit(solution)/shard_map/all_gather | solution.py:97
  203.9 68.7 %all-reduce.15 = f32[384]{0:T(512)S(1)} all-reduce(f32[384]{0:T(512)S(1)} %multiply_dynamic-update-slice_fusion.2), channel_id=2, replica_groups=mesh['dp'=32,'tensor'=4] {'dp'}, use_global_device_ids=true, to_apply=%add.15 | all-reduce | flops 384 | bytes 3072
  274.8 94.4 %all-gather.38.cloned.1.call-done = f32[384,64,128]{2,1,0:T(8,128)} async-done(((f32[12,64,128]{2,1,0:T(8,128)}), f32[384,64,128]{2,1,0:T(8,128)}) %all-gather.38.cloned.1.call-update) | async-done | bytes 12582928 | tf_op jit(solution)/shard_map/all_gather | solution.py:22
  369.2 36.9 while.21
  414.7 103.4 %all-gather.20.cloned.1.call-done = bf16[768,1536]{0,1:T(8,128)(2,1)} async-done(((bf16[768,48]{0,1:T(8,128)(2,1)}), bf16[768,1536]{0,1:T(8,128)(2,1)}) %all-gather.20.cloned.1.call-update) | async-done | bytes 2359312 | tf_op jit(solution)/shard_map/all_gather | solution.py:99
  556.9 78.1 %all_gather.105 = bf16[1536,256]{1,0:T(8,128)(2,1)} all-gather(bf16[48,256]{1,0:T(8,128)(2,1)S(1)} %copy-done.70), channel_id=1, replica_groups=mesh['dp'=32,'tensor'=4] {'dp'}, dimensions={0}, use_global_device_ids=true | all-gather | bytes 811008 | tf_op jit(solution)/shard_map/all_gather | solution.py:103
  635.0 73.6 %all_gather.106 = bf16[1536,256]{1,0:T(8,128)(2,1)} all-gather(bf16[48,256]{1,0:T(8,128)(2,1)S(1)} %copy-done.71), channel_id=1, replica_groups=mesh['dp'=32,'tensor'=4] {'dp'}, dimensions={0}, use_global_device_ids=true | all-gather | bytes 811008 | tf_op jit(solution)/shard_map/all_gather | solution.py:104
  742.6 77.4 %all_gather.109 = bf16[256,1536]{0,1:T(8,128)(2,1)} all-gather(bf16[256,48]{0,1:T(8,128)(2,1)S(1)} %copy-done.72), channel_id=1, replica_groups=mesh['dp'=32,'tensor'=4] {'dp'}, dimensions={1}, use_global_device_ids=true | all-gather | bytes 811008 | tf_op jit(solution)/shard_map/all_gather | solution.py:105
  820.0 75.7 %all_gather.110 = bf16[1536,256]{1,0:T(8,128)(2,1)} all-gather(bf16[48,256]{1,0:T(8,128)(2,1)S(1)} %copy-done.70), channel_id=1, replica_groups=mesh['dp'=32,'tensor'=4] {'dp'}, dimensions={0}, use_global_device_ids=true | all-gather | bytes 811008 | tf_op jit(solution)/shard_map/all_gather | solution.py:103
  895.7 74.7 %all_gather.111 = bf16[1536,256]{1,0:T(8,128)(2,1)} all-gather(bf16[48,256]{1,0:T(8,128)(2,1)S(1)} %copy-done.71), channel_id=1, replica_groups=mesh['dp'=32,'tensor'=4] {'dp'}, dimensions={0}, use_global_device_ids=true | all-gather | bytes 811008 | tf_op jit(solution)/shard_map/all_gather | solution.py:104
  994.1 63.0 %all-reduce.17 = f32[256]{0:T(256)S(1)} all-reduce(f32[256]{0:T(256)S(1)} %get-tuple-element.484), channel_id=5, replica_groups=mesh['dp'=32,'tensor'=4] {'tensor'}, use_global_device_ids=true, to_apply=%region_10.11.clone | all-reduce | flops 256 | bytes 2048
  1100.9 87.6 %all-gather.30.cloned.1.call-done = bf16[8,1536,128]{2,1,0:T(8,128)(2,1)} async-done(((bf16[8,48,128]{2,1,0:T(8,128)(2,1)}), bf16[8,1536,128]{2,1,0:T(8,128)(2,1)}) %all-gather.30.cloned.1.call-update) | async-done | bytes 3145744 | tf_op jit(solution)/shard_map/all_gather | solution.py:100
  1196.9 148.9 %all-gather.32.cloned.1.call-done = bf16[8,1536,128]{2,1,0:T(8,128)(2,1)} async-done(((bf16[8,48,128]{2,1,0:T(8,128)(2,1)}), bf16[8,1536,128]{2,1,0:T(8,128)(2,1)}) %all-gather.32.cloned.1.call-update) | async-done | bytes 3145744 | tf_op jit(solution)/shard_map/all_gather | solution.py:101
  1399.3 78.2 %all_gather.107 = bf16[256,1536]{0,1:T(8,128)(2,1)} all-gather(bf16[256,48]{0,1:T(8,128)(2,1)S(1)} %copy-done.72), channel_id=1, replica_groups=mesh['dp'=32,'tensor'=4] {'dp'}, dimensions={1}, use_global_device_ids=true | all-gather | bytes 811008 | tf_op jit(solution)/shard_map/all_gather | solution.py:105
  1563.4 43.2 %reduce-scatter.17.cloned.1.call-done = f32[64,1536]{1,0:T(8,128)} async-done(((f32[256,1536]{1,0:T(8,128)}), f32[64,1536]{1,0:T(8,128)}) %reduce-scatter.17.cloned.1.call-update) | async-done | bytes 393232 | tf_op jit(solution)/shard_map/reduce_scatter | solution.py:289
  1628.7 112.3 %all-gather.34.cloned.1.call-done = bf16[768,1536]{0,1:T(8,128)(2,1)} async-done(((bf16[768,48]{0,1:T(8,128)(2,1)}), bf16[768,1536]{0,1:T(8,128)(2,1)}) %all-gather.34.cloned.1.call-update) | async-done | bytes 2359312 | tf_op jit(solution)/shard_map/all_gather | solution.py:99
  1748.4 69.1 %all-gather.4 = bf16[32,48,12]{1,2,0:T(8,128)(2,1)S(1)} all-gather(bf16[1,48,12]{1,2,0:T(8,128)(2,1)S(1)} %bitcast.350), channel_id=1, replica_groups=mesh['dp'=32,'tensor'=4] {'dp'}, dimensions={0}, use_global_device_ids=true | all-gather | bytes 38016 | tf_op jit(solution)/shard_map/all_gather | solution.py:98
  1817.7 76.2 %all_gather.121 = bf16[1536,2,128]{2,1,0:T(2,128)(2,1)} all-gather(bf16[48,2,128]{2,1,0:T(2,128)(2,1)S(1)} %copy-done.74), channel_id=1, replica_groups=mesh['dp'=32,'tensor'=4] {'dp'}, dimensions={0}, use_global_device_ids=true | all-gather | bytes 811008 | tf_op jit(solution)/shard_map/all_gather | solution.py:97
  1917.9 165.0 %all-gather.40.cloned.1.call-done = f32[384,64,128]{2,1,0:T(8,128)} async-done(((f32[12,64,128]{2,1,0:T(8,128)}), f32[384,64,128]{2,1,0:T(8,128)}) %all-gather.40.cloned.1.call-update) | async-done | bytes 12582928 | tf_op jit(solution)/shard_map/all_gather | solution.py:22
  2082.8 58.6 %while.22 = (s32[]{:T(128)}, f32[12,64,128]{2,1,0:T(8,128)S(1)}, s32[]{:T(128)}, f32[32,12]{1,0:T(8,128)}, f32[32,12,64,128]{3,2,1,0:T(8,128)}, /*index=5*/s32[]{:T(128)}, s32[]{:T(128)}, s32[]{:T(128)}, s32[]{:T(128)}) while((s32[]{:T(128)}, f32[12,64,128]{2,1,0:T(8,128)S(1)}, s32[]{:T(128)}, f32[32,12]{1,0:T(8,128)}, ...), condition=%wide.region_25.26_spmd.clone, body=%wide.region_24.25_spmd.clone.sunk | while | flops 393224 | bytes 1179959 | solution.py:35
  2256.9 81.0 %reduce-scatter.37.cloned.1.call-done = f32[48,12]{1,0:T(8,128)} async-done(((f32[1536,12]{1,0:T(8,128)}), f32[48,12]{1,0:T(8,128)}) %reduce-scatter.37.cloned.1.call-update) | async-done | bytes 2320
  2339.3 173.4 %all-reduce.24.cloned.1.call-done = f32[1536,2,128]{2,1,0:T(2,128)} async-done(((f32[1536,2,128]{2,1,0:T(2,128)}), f32[1536,2,128]{2,1,0:T(2,128)}) %all-reduce.24.cloned.1.call-update) | async-done | bytes 1572880 | tf_op jit(solution)/shard_map/psum | solution.py:413
  2552.4 326.0 %all-reduce.26.cloned.1.call-done = f32[1536,2,768]{2,1,0:T(2,128)} async-done(((f32[1536,2,768]{2,1,0:T(2,128)}), f32[1536,2,768]{2,1,0:T(2,128)}) %all-reduce.26.cloned.1.call-update) | async-done | bytes 9437200
  2880.1 158.8 %reduce-scatter.31.cloned.1.call-done = f32[48,256]{1,0:T(8,128)} async-done(((f32[1536,256]{1,0:T(8,128)}), f32[48,256]{1,0:T(8,128)}) %reduce-scatter.31.cloned.1.call-update) | async-done | bytes 49168 | tf_op jit(solution)/shard_map/reduce_scatter | solution.py:409
  3038.9 161.1 %reduce-scatter.33.cloned.1.call-done = f32[48,256]{1,0:T(8,128)} async-done(((f32[1536,256]{1,0:T(8,128)}), f32[48,256]{1,0:T(8,128)}) %reduce-scatter.33.cloned.1.call-update) | async-done | bytes 49168 | tf_op jit(solution)/shard_map/reduce_scatter | solution.py:410
  3200.0 161.2 %reduce-scatter.35.cloned.1.call-done = f32[256,48]{0,1:T(8,128)} async-done(((f32[256,1536]{0,1:T(8,128)}), f32[256,48]{0,1:T(8,128)}) %reduce-scatter.35.cloned.1.call-update) | async-done | bytes 49168 | tf_op jit(solution)/shard_map/reduce_scatter | solution.py:411
  3361.2 175.6 %reduce-scatter.29.cloned.1.call-done = f32[8,128,48]{1,2,0:T(8,128)} async-done(((f32[8,128,1536]{1,2,0:T(8,128)}), f32[8,128,48]{1,2,0:T(8,128)}) %reduce-scatter.29.cloned.1.call-update) | async-done | bytes 196624 | tf_op jit(solution)/shard_map/reduce_scatter | solution.py:408
  3536.7 174.1 %reduce-scatter.25.cloned.1.call-done = f32[8,48,128]{2,1,0:T(8,128)} async-done(((f32[8,1536,128]{2,1,0:T(8,128)}), f32[8,48,128]{2,1,0:T(8,128)}) %reduce-scatter.25.cloned.1.call-update) | async-done | bytes 196624 | tf_op jit(solution)/shard_map/reduce_scatter | solution.py:406
  3710.8 173.5 %reduce-scatter.27.cloned.1.call-done = f32[8,48,128]{2,1,0:T(8,128)} async-done(((f32[8,1536,128]{2,1,0:T(8,128)}), f32[8,48,128]{2,1,0:T(8,128)}) %reduce-scatter.27.cloned.1.call-update) | async-done | bytes 196624 | tf_op jit(solution)/shard_map/reduce_scatter | solution.py:407
  3884.3 167.4 %reduce-scatter.23.cloned.1.call-done = f32[768,48]{0,1:T(8,128)} async-done(((f32[768,1536]{0,1:T(8,128)}), f32[768,48]{0,1:T(8,128)}) %reduce-scatter.23.cloned.1.call-update) | async-done | bytes 147472 | tf_op jit(solution)/shard_map/reduce_scatter | solution.py:405
  4051.7 166.5 %all-reduce.28.cloned.1.call-done = (f32[1536]{0:T(1024)}, f32[4,3072]{1,0:T(4,128)}, f32[4,2,128]{2,1,0:T(2,128)}, f32[48]{0:T(128)}, f32[48]{0:T(128)}, /*index=5*/f32[48]{0:T(128)}, f32[3072]{0:T(1024)}, f32[1536]{0:T(1024)}) async-done(((f32[1536]{0:T(1024)}, f32[4,3072]{1,0:T(4,128)}, f32[4,2,128]{2,1,0:T(2,128)}, f32[48]{0:T(128)}, f32[48]{0:T(128)}, /*index=5*/f32[48]{0:T(128)}, f32[3072]{0:T(1024)}, ...) | async-done | bytes 78416 | tf_op jit(solution)/shard_map/psum | solution.py:413
  (707 shorter events, 665.6 us)
Async XLA Ops:
  7.2 180.1 %all-gather.18.cloned.1.call-start = ((), (), s32[]{:S(2)}) async-start(), calls=%async_computation.12 | async-start | bytes 4866048 | tf_op jit(solution)/shard_map/all_gather | solution.py:96
  8.0 361.2 %all-gather.38.cloned.1.call-start = ((), (), s32[]{:S(2)}) async-start(), calls=%async_computation.34 | async-start | bytes 12976128 | tf_op jit(solution)/shard_map/all_gather | solution.py:22
  8.8 173.8 %collective-permute-start.1 = (f32[3]{0:T(128)S(1)}, f32[3]{0:T(128)S(1)}, u32[]{:S(2)}, u32[]{:S(2)}) collective-permute-start(f32[3]{0:T(128)S(1)} %slice.163), channel_id=1, source_target_pairs={{0,4},{4,8},{8,12},{12,16},{16,20},{20,24},{24,28},{28,32},{32,36}... | collective-permute-start | bytes 44 | tf_op jit(solution)/shard_map/ppermute | solution.py:17
  192.1 3.9 collective-permute-start
  200.0 318.1 %all-gather.20.cloned.1.call-start = ((), (), s32[]{:S(2)}) async-start(), calls=%async_computation.13 | async-start | bytes 2433024 | tf_op jit(solution)/shard_map/all_gather | solution.py:99
  200.7 856.4 %reduce-scatter.15.cloned.1.call-start = ((), (), s32[]{:S(2)}) async-start(), calls=%async_computation.14 | async-start | bytes 1966080 | tf_op jit(solution)/shard_map/reduce_scatter | solution.py:256
  521.9 559.0 %all-gather.22.cloned.1.call-start = ((), (), s32[]{:S(2)}) async-start(), calls=%async_computation.15 | async-start | bytes 3244032 | tf_op jit(solution)/shard_map/all_gather | solution.py:100
  522.5 564.9 %all-gather.24.cloned.1.call-start = ((), (), s32[]{:S(2)}) async-start(), calls=%async_computation.16 | async-start | bytes 3244032 | tf_op jit(solution)/shard_map/all_gather | solution.py:101
  523.0 570.8 %all-gather.28.cloned.1.call-start = ((), (), s32[]{:S(2)}) async-start(), calls=%async_computation.19 | async-start | bytes 3244032 | tf_op jit(solution)/shard_map/all_gather | solution.py:102
  554.3 841.5 %copy-start.19 = (bf16[256,1536]{1,0:T(8,128)(2,1)}, bf16[256,1536]{1,0:T(8,128)(2,1)S(1)}, u32[]{:S(2)}) copy-start(bf16[256,1536]{1,0:T(8,128)(2,1)S(1)} %all_gather.108) | copy-start | bytes 2359300
  554.4 634.1 %all-gather.30.cloned.1.call-start = ((), (), s32[]{:S(2)}) async-start(), calls=%async_computation.20 | async-start | bytes 3244032 | tf_op jit(solution)/shard_map/all_gather | solution.py:100
  555.1 790.7 %all-gather.32.cloned.1.call-start = ((), (), s32[]{:S(2)}) async-start(), calls=%async_computation.21 | async-start | bytes 3244032 | tf_op jit(solution)/shard_map/all_gather | solution.py:101
  555.8 948.1 %all-gather.26.cloned.1.call-start = ((), (), s32[]{:S(2)}) async-start(), calls=%async_computation.17 | async-start | bytes 3244032 | tf_op jit(solution)/shard_map/all_gather | solution.py:102
  556.4 1005.2 %reduce-scatter.19.cloned.1.call-start = ((), (), s32[]{:S(2)}) async-start(), calls=%async_computation.22 | async-start | bytes 1966080 | tf_op jit(solution)/shard_map/reduce_scatter | solution.py:338
  1399.2 207.3 %reduce-scatter.17.cloned.1.call-start = ((), (), s32[]{:S(2)}) async-start(), calls=%async_computation.18 | async-start | bytes 1966080 | tf_op jit(solution)/shard_map/reduce_scatter | solution.py:289
  1551.5 189.6 %all-gather.34.cloned.1.call-start = ((), (), s32[]{:S(2)}) async-start(), calls=%async_computation.23 | async-start | bytes 2433024 | tf_op jit(solution)/shard_map/all_gather | solution.py:99
  1552.2 353.3 %all-gather.36.cloned.1.call-start = ((), (), s32[]{:S(2)}) async-start(), calls=%async_computation.24 | async-start | bytes 4866048 | tf_op jit(solution)/shard_map/all_gather | solution.py:96
  1552.8 530.1 %all-gather.40.cloned.1.call-start = ((), (), s32[]{:S(2)}) async-start(), calls=%async_computation.35 | async-start | bytes 12976128 | tf_op jit(solution)/shard_map/all_gather | solution.py:22
  1748.3 589.6 %reduce-scatter.37.cloned.1.call-start = ((), (), s32[]{:S(2)}) async-start(), calls=%async_computation.36 | async-start | bytes 811008
  2177.5 8.3 collective-permute-start.2
  2185.7 326.9 %all-reduce.24.cloned.1.call-start = ((), (), s32[]{:S(2)}) async-start(), calls=%async_computation.26 | async-start | bytes 3145728 | tf_op jit(solution)/shard_map/psum | solution.py:413
  2192.8 355.9 %reduce-scatter.21.cloned.1.call-start = ((), (), s32[]{:S(2)}) async-start(), calls=%async_computation.25 | async-start | bytes 1966080 | tf_op jit(solution)/shard_map/reduce_scatter | solution.py:394
  2198.9 679.4 %all-reduce.26.cloned.1.call-start = ((), (), s32[]{:S(2)}) async-start(), calls=%async_computation.37 | async-start | bytes 18874368
  2218.9 819.9 %reduce-scatter.31.cloned.1.call-start = ((), (), s32[]{:S(2)}) async-start(), calls=%async_computation.31 | async-start | bytes 1622016 | tf_op jit(solution)/shard_map/reduce_scatter | solution.py:409
  2221.4 978.6 %reduce-scatter.33.cloned.1.call-start = ((), (), s32[]{:S(2)}) async-start(), calls=%async_computation.32 | async-start | bytes 1622016 | tf_op jit(solution)/shard_map/reduce_scatter | solution.py:410
  2223.1 1138.1 %reduce-scatter.35.cloned.1.call-start = ((), (), s32[]{:S(2)}) async-start(), calls=%async_computation.33 | async-start | bytes 1622016 | tf_op jit(solution)/shard_map/reduce_scatter | solution.py:411
  2224.8 1311.9 %reduce-scatter.29.cloned.1.call-start = ((), (), s32[]{:S(2)}) async-start(), calls=%async_computation.30 | async-start | bytes 6488064 | tf_op jit(solution)/shard_map/reduce_scatter | solution.py:408
  2232.7 1478.1 %reduce-scatter.25.cloned.1.call-start = ((), (), s32[]{:S(2)}) async-start(), calls=%async_computation.28 | async-start | bytes 6488064 | tf_op jit(solution)/shard_map/reduce_scatter | solution.py:406
  2241.3 1643.0 %reduce-scatter.27.cloned.1.call-start = ((), (), s32[]{:S(2)}) async-start(), calls=%async_computation.29 | async-start | bytes 6488064 | tf_op jit(solution)/shard_map/reduce_scatter | solution.py:407
  2249.9 1801.8 %reduce-scatter.23.cloned.1.call-start = ((), (), s32[]{:S(2)}) async-start(), calls=%async_computation.27 | async-start | bytes 4866048 | tf_op jit(solution)/shard_map/reduce_scatter | solution.py:405
  2254.3 1973.9 %copy-start.1 = (f32[4,3072]{1,0:T(4,128)S(1)}, f32[4,3072]{1,0:T(4,128)}, u32[]{:S(2)}) copy-start(f32[4,3072]{1,0:T(4,128)} %param.38) | copy-start | bytes 147460
  2254.3 1963.9 %all-reduce.28.cloned.1.call-start = ((), (), s32[]{:S(2)}) async-start(), calls=%async_computation.38 | async-start | bytes 166912 | tf_op jit(solution)/shard_map/psum | solution.py:413
  (131 other events, 8763.6 us)
Sparse Core Ops, SparseCore 0:
  9.7 144.8 all-gather.17
  200.1 169.0 all-gather.37
  370.9 147.2 all-gather.19
  522.0 56.9 reduce-scatter.14
  580.5 134.7 all-gather.21
  716.9 158.2 all-gather.23
  877.0 154.5 all-gather.27
  1033.3 155.0 all-gather.29
  1190.2 155.4 all-gather.31
  1347.4 156.5 all-gather.25
  1506.8 54.7 reduce-scatter.18
  1564.1 42.3 reduce-scatter.16
  1608.3 132.6 all-gather.33
  1742.6 162.8 all-gather.35
  1907.1 175.7 all-gather.39
  2185.9 151.9 reduce-scatter.36
  2342.4 170.2 all-reduce.23
  2515.2 33.4 reduce-scatter.20
  2551.4 326.9 all-reduce.25
  2881.3 157.5 reduce-scatter.30
  3041.8 158.1 reduce-scatter.32
  3203.0 158.0 reduce-scatter.34
  3364.2 172.5 reduce-scatter.28
  3539.6 171.2 reduce-scatter.24
  3713.8 170.4 reduce-scatter.26
  3887.1 164.5 reduce-scatter.22
  4058.8 159.4 all-reduce.27
where the time goes:
time: 4250 us; the launch traced here: 4240 us
  waiting for transfers between devices  2760 us (65%)
  blocking collectives  961 us (23%)
  local copies, waits for them, and re-layouts  200 us (5%)
  matrix products  147 us (3%)
  other arithmetic  134 us (3%)
    unnamed x29, waiting for transfers between devices  412 us
    psum x2, waiting for transfers between devices, body(): lax.psum((grad_norm, grad_post_gain, grad_bc, place_slice(grad_conv[:, :i...  340 us
    all_gather x2, waiting for transfers between devices, carried_in(): everything = jax.tree.map(lambda part: lax.all_gather(part, axis), shard)  259 us
    all_gather x2, waiting for transfers between devices, fetch_weights(): lax.all_gather(w_out, 'dp', axis=1, tiled=True)  216 us
    reduce_scatter x1, waiting for transfers between devices, body(): lax.psum_scatter(grad_ed, 'dp', scatter_dimension=2, tiled=True)  176 us
    reduce_scatter x1, waiting for transfers between devices, body(): lax.psum_scatter(grad_eg, 'dp', scatter_dimension=1, tiled=True)  174 us
    reduce_scatter x1, waiting for transfers between devices, body(): lax.psum_scatter(grad_eu, 'dp', scatter_dimension=1, tiled=True)  173 us
    reduce_scatter x1, waiting for transfers between devices, body(): lax.psum_scatter(grad_out, 'dp', scatter_dimension=1, tiled=True)  167 us
  transfers between devices with their start and end apart: 30, of which 23 were waited for; matrix products, arithmetic and copies ran while one was open for 9% of the time, Pallas kernels for 0%

commit v1 on v0

v1 whole, which is shorter than its diff:
```python
import math

import jax
import jax.numpy as jnp
from jax import lax
from jax.experimental import pallas as pl
from jax.experimental.pallas import tpu as pltpu
from jax.sharding import PartitionSpec as P

f32 = jnp.float32
bf16 = jnp.bfloat16
eps = 1e-05
highest = lax.Precision.HIGHEST
LANES = 128
DP_SHAPE = (4, 2, 4)
EDGE = 16
SUB = 8
RAW_LIMIT = 48 * 1024 * 1024
VMEM_SPARE = 12 * 1024 * 1024

NN = (((1,), (0,)), ((), ()))
NT = (((1,), (1,)), ((), ()))
TN = (((0,), (0,)), ((), ()))


def dot(a, b, dims=NN):
    return lax.dot_general(a.astype(bf16), b.astype(bf16), dims, preferred_element_type=f32)


def dot_exact(a, b, dims=NN):
    return lax.dot_general(a, b, dims, precision=highest, preferred_element_type=f32)


def halves(value):
    high = value.astype(bf16)
    return high, (value - high.astype(f32)).astype(bf16)


def dot_left(a, b, dims=NN):
    high, low = halves(a)
    return dot(high, b, dims) + dot(low, b, dims)


def dot_both(a, b, dims=NN):
    a_high, a_low = halves(a)
    b_high, b_low = halves(b)
    return dot(a_high, b_high, dims) + (dot(a_low, b_high, dims) + dot(a_high, b_low, dims))


def from_behind(value, axis, steps):
    count = lax.axis_size(axis)
    leading, last = (max(0, -steps), min(count, count - steps))
    return lax.ppermute(value, axis, [(source, source + steps) for source in range(leading, last)])


def kernel_call(kernel, out_shapes, *args, flops=0, scratch=(), small=(), raw=()):
    moved = sum(a.size * a.dtype.itemsize for a in args)
    moved += sum(s.size * s.dtype.itemsize for s in out_shapes)
    kept = [a for i, a in enumerate(args) if i not in raw and i not in small] + list(out_shapes)
    kept += [s for s in scratch if s.dtype in (f32, bf16)]
    held = sum(math.prod(a.shape) * (4 if a.dtype == f32 else 2) for a in kept)
    spaces = [
        pltpu.SMEM if i in small else pl.ANY if i in raw else pltpu.VMEM for i in range(len(args))
    ]
    return pl.pallas_call(
        kernel,
        out_shape=out_shapes,
        in_specs=[pl.BlockSpec(memory_space=space) for space in spaces],
        scratch_shapes=scratch,
        compiler_params=pltpu.CompilerParams(vmem_limit_bytes=max(held + VMEM_SPARE, RAW_LIMIT if len(raw) > 1 else 0)),
        cost_estimate=pl.CostEstimate(flops=flops, bytes_accessed=moved, transcendentals=0),
    )(*args)


def shape_of(shape, dtype=f32):
    return jax.ShapeDtypeStruct(shape, dtype)


def ids(shape, dim):
    return lax.broadcasted_iota(jnp.int32, shape, dim)


def per_head(columns, pair, rows):
    left = ids((rows, LANES), 1) < LANES // 2
    return jnp.where(left, columns[:, 2 * pair : 2 * pair + 1], columns[:, 2 * pair + 1 : 2 * pair + 2])


def run_info(cum, heads):
    rows = cum.shape[0]
    turned = cum.T
    run_col = cum[:, heads : heads + 1]
    run_row = turned[heads : heads + 1, :]
    keep = (ids((rows, rows), 0) >= ids((rows, rows), 1)) & (run_col == run_row)
    return turned, run_col, run_col[rows - 1 : rows, :], keep


PIECES = 10


def load_blocks(pieces, target, done, here, ranges, shard):
    x_size, z_size, y_size = DP_SHAPE
    x, z, y = here[0], here[1], here[2]
    copies = []
    for half, start, at, width in ranges:
        for index, far in enumerate((0, -1, 1, 2, 2)):
            for block in range(4 if far == 2 else 8):
                place_in = block + 4 * (index == 4)
                near = RING[place_in // 2]
                to_x, to_y = (far, near) if half == 0 else (near, far)
                to_x = lax.rem(x + (to_x + x_size), x_size)
                to_y = lax.rem(y + (to_y + y_size), y_size)
                to_z = lax.rem(z + place_in % 2, z_size)
                row = pl.multiple_of(((to_x * z_size + to_z) * y_size + to_y) * shard, 16)
                copy = pltpu.make_async_copy(
                    pieces[half * 5 + index].at[block, :, pl.ds(start, width)],
                    target.at[pl.ds(row, shard), pl.ds(at, width)],
                    done.at[len(copies)],
                )
                copy.start()
                copies.append(copy)
    return copies


def wait_all(copies):
    for copy in copies:
        copy.wait()


def column_ranges(split, first, last):
    ranges = []
    if first < split:
        ranges.append((0, first, 0, min(last, split) - first))
    if last > split:
        begin = max(first, split)
        ranges.append((1, begin - split, begin - first, last - begin))
    return ranges


def rows_at(index, quarter):
    return pl.ds(pl.multiple_of(index * quarter, quarter), quarter)


def silu_slope(value, sigma):
    return sigma * (1.0 + value * (1.0 - sigma))


def input_rows(quarter, width):
    def kernel(here, own, across, core_own, core_across, gain, rows_out, normed_out, own_out):
        core, pair = here[3], here[4]
        places = (pair * 2 + core, (1 - pair) * 2 + core, pair * 2 + 1 - core, (1 - pair) * 2 + 1 - core)
        for ref, place_at in zip((own, across, core_own, core_across), places, strict=True):
            rows = ref[0:quarter, :]
            value = rows.astype(f32)
            scale = lax.rsqrt(jnp.mean(value * value, -1, keepdims=True) + eps)
            rows_out[rows_at(place_at, quarter), :] = rows
            normed = (value * scale * gain[...]).astype(bf16)
            normed_out[rows_at(place_at, quarter), :] = normed
            if ref is own:
                own_out[...] = normed

    return kernel


def scan_front(heads, inner, state, shard, ranges):
    pairs = heads // 2
    tiles = (inner + 2 * state) // LANES

    def kernel(here, normed, tail, taps, lags, bias, alog, skip, *refs):
        pieces, refs = refs[:PIECES], refs[PIECES:]
        weights_in, proj, y_out, conv_out, cum_out, steps_out, state_out, act, sums, done = refs
        copies = load_blocks(pieces, weights_in, done, here, ranges, shard)
        wait_all(copies)
        columns = weights_in.shape[1]
        wide = 3 * LANES
        for at in range(0, columns, wide):
            part = weights_in[:, at : at + wide]
            proj[0:EDGE, at : at + wide] = dot(tail[...], part)
            proj[EDGE:, at : at + wide] = dot(normed[...], part)
        rows = y_out.shape[0]
        count = taps.shape[0] // 2
        for tile in range(tiles):
            at = tile * LANES
            total = jnp.zeros((rows, LANES), f32)
            for back in range(count):
                source = proj[EDGE - back : EDGE - back + rows, inner + at : inner + at + LANES]
                weight = taps[count - 1 - back : count - back, at : at + LANES]
                total = total + weight * source * lags[:, back : back + 1]
            conv_out[:, at : at + LANES] = total
            act[:, at : at + LANES] = total * jax.nn.sigmoid(total)
        b_rows = act[:, inner : inner + state]
        c_rows = act[:, inner + state : inner + 2 * state]
        raw = proj[EDGE : EDGE + rows, 2 * inner + 2 * state :] + bias[...]
        steps = jnp.maximum(raw, 0.0) + jnp.log1p(jnp.exp(-jnp.abs(raw)))
        lane = ids((rows, LANES), 1)
        reset = 1.0 - lags[:, 1:2]
        logs = jnp.where(lane < heads, -steps * jnp.exp(alog[...]), jnp.where(lane == heads, reset, 0.0))
        lower = (ids((rows, rows), 0) >= ids((rows, rows), 1)).astype(f32)
        cum = dot_exact(lower, logs)
        steps_out[...] = steps
        cum_out[...] = cum
        turned, run_col, last_run, keep = run_info(cum, heads)
        inner_cb = dot_exact(c_rows, b_rows, NT)
        closing = jnp.where(run_col == last_run, jnp.exp(cum[rows - 1 : rows, :] - cum), 0.0)
        left = ids((rows, LANES), 1) < LANES // 2
        for pair in range(pairs):
            at = pair * LANES
            x_pair = act[:, at : at + LANES]
            scaled = x_pair * per_head(steps, pair, rows)
            parts = []
            for head in (2 * pair, 2 * pair + 1):
                gaps = cum[:, head : head + 1] - turned[head : head + 1, :]
                weights = jnp.exp(jnp.where(keep, gaps, -jnp.inf)) * inner_cb
                parts.append(dot_both(weights, scaled))
            y_out[:, at : at + LANES] = (
                jnp.where(left, parts[0], parts[1]) + skip[:, at : at + LANES] * x_pair
            )
            sums[at : at + LANES, :] = dot_both(scaled * per_head(closing, pair, rows), b_rows, TN)
        last = cum[rows - 1 : rows, :]
        fill_states(state_out, sums, jnp.where(last_run == 0.0, jnp.exp(last), 0.0), heads)

    return kernel


def fill_states(out, sums, keep, heads):
    blocks, size = out.shape[0], sums.shape[0] // out.shape[0]
    head_rows = sums.shape[0] // heads
    row_head = (ids((blocks, LANES), 0) * size + ids((blocks, LANES), 1)) // head_rows
    table = jnp.zeros((blocks, LANES), f32)
    for head in range(heads):
        table = jnp.where(row_head == head, keep[:, head : head + 1], table)
    for block in range(blocks):
        out[block, 0:size, :] = sums[block * size : (block + 1) * size, :]
        out[block, size : size + SUB, :] = jnp.broadcast_to(table[block : block + 1, :], (SUB, LANES))


def gate_front(heads, inner, state, shard, ranges):
    pairs = heads // 2

    def kernel(here, y_in, proj, conv, cum_in, entering, gain, *refs):
        pieces, refs = refs[:PIECES], refs[PIECES:]
        w_back, y_out, mixed_out, mine_out, theirs_out, mixed_low, partial, done = refs
        copies = load_blocks(pieces, w_back, done, here, ranges, shard)
        rows = y_in.shape[0]
        quarter = rows // 4
        width = partial.shape[1] - LANES
        core = here[3]
        cum = cum_in[...]
        opening = jnp.where(cum[:, heads : heads + 1] == 0.0, jnp.exp(cum), 0.0)
        c_conv = conv[:, inner + state : inner + 2 * state]
        c_rows = c_conv * jax.nn.sigmoid(c_conv)
        squares = jnp.zeros((rows, LANES), f32)
        for pair in range(pairs):
            at = pair * LANES
            y_pair = y_in[:, at : at + LANES] + per_head(opening, pair, rows) * dot_both(
                c_rows, entering[at : at + LANES, :], NT
            )
            z_pair = proj[EDGE : EDGE + rows, at : at + LANES]
            gated = y_pair * z_pair * jax.nn.sigmoid(z_pair)
            y_out[:, at : at + LANES] = y_pair
            high, low = halves(gated * gain[:, at : at + LANES])
            mixed_out[:, at : at + LANES] = high
            mixed_low[:, at : at + LANES] = low
            squares = squares + gated * gated
        total = jnp.sum(squares, 1, keepdims=True)
        partial[:, width:] = jnp.broadcast_to(total, (rows, LANES))
        wait_all(copies)
        wide = 2 * LANES
        for at in range(0, width, wide):
            part = w_back[at : at + wide, :]
            partial[:, at : at + wide] = dot(mixed_out[...], part, NT) + dot(mixed_low[...], part, NT)
        for half in range(2):
            to = slice(half * quarter, (half + 1) * quarter)
            mine_out[to, :] = partial[rows_at(2 * half + core, quarter), :]
            theirs_out[to, :] = partial[rows_at(2 * half + 1 - core, quarter), :]

    return kernel


def core_sum(width):
    def kernel(mine, theirs, sum_out, sent_out):
        total = mine[...] + theirs[...]
        sum_out[...] = total[:, :width]
        sent_out[:, :width] = total[:, :width].astype(bf16)
        squares = total[:, width : width + 1]
        high = squares.astype(bf16).astype(f32)
        lane = ids((total.shape[0], LANES), 1)
        sent_out[:, width:] = jnp.where(lane == 0, high, jnp.where(lane == 1, squares - high, 0.0)).astype(bf16)

    return kernel


def middle_rows(quarter, width, inner_total):
    def kernel(here, sent, got, own, across, gain, middle_out, post_out, scales_out):
        pair = here[4]
        total = sent[...].astype(f32) + got[...].astype(f32)
        squares = total[:, width : width + 1] + total[:, width + 1 : width + 2]
        scale_mix = lax.rsqrt(squares / inner_total + eps)
        middle_out[rows_at(pair, quarter), :] = own[0:quarter, :].astype(f32)
        middle_out[rows_at(1 - pair, quarter), :] = across[0:quarter, :].astype(f32)
        middle = middle_out[...] + scale_mix * total[:, :width]
        middle_out[...] = middle
        scale = lax.rsqrt(jnp.mean(middle * middle, -1, keepdims=True) + eps)
        post_out[...] = (middle * scale * gain[...]).astype(bf16)
        lane = ids((2 * quarter, LANES), 1)
        scales_out[...] = jnp.where(lane == 0, scale_mix, scale)

    return kernel


def experts_both(quarter, hidden, ffe, experts, shard, ranges):
    def kernel(here, post_mine, post_theirs, own, across, core_own, core_across, share, *refs):
        pieces, refs = refs[:PIECES], refs[PIECES:]
        (
            post, cot, act_out, dpre_out, out_mine, out_theirs, dpost_mine, dpost_theirs,
            weights, shares, done,
        ) = refs
        copies = load_blocks(pieces, weights, done, here, ranges, shard)
        core, pair = here[3], here[4]
        half = 2 * quarter
        width = post.shape[1]
        post[0:half, :] = post_mine[...]
        post[half:, :] = post_theirs[...]
        cot[rows_at(pair, quarter), :] = own[quarter:, :]
        cot[rows_at(1 - pair, quarter), :] = across[quarter:, :]
        cot[rows_at(2 + pair, quarter), :] = core_own[quarter:, :]
        cot[rows_at(3 - pair, quarter), :] = core_across[quarter:, :]
        for index in range(2):
            shares[index * quarter : (index + 1) * quarter, :] = share[rows_at(2 * index + core, quarter), :]
            shares[half + index * quarter : half + (index + 1) * quarter, :] = share[
                rows_at(2 * index + 1 - core, quarter), :
            ]
        wait_all(copies)
        wide = 2 * LANES
        left = ids((2 * half, wide), 1) < ffe
        for at in range(0, hidden, wide):
            gate = dot(post[...], weights[:, at : at + wide])
            up = dot(post[...], weights[:, hidden + at : hidden + at + wide])
            d_act = dot(cot[...], weights[:, 2 * hidden + at : 2 * hidden + at + wide])
            sigma = jax.nn.sigmoid(gate)
            silu = gate * sigma
            act = silu * up
            expert = at // ffe
            if expert < experts:
                by = jnp.where(left, shares[:, expert : expert + 1], shares[:, expert + 1 : expert + 2])
                act = act * by
                d_act = d_act * by
            act_out[:, at : at + wide] = act.astype(bf16)
            dpre_out[:, at : at + wide] = (d_act * up * silu_slope(gate, sigma)).astype(bf16)
            dpre_out[:, hidden + at : hidden + at + wide] = (d_act * silu).astype(bf16)
        for at in range(0, width, wide):
            d_post = dot(dpre_out[...], weights[at : at + wide, : 2 * hidden], NT)
            dpost_mine[:, at : at + wide] = d_post[:half]
            dpost_theirs[:, at : at + wide] = d_post[half:].astype(bf16)
        for at in range(0, width, wide):
            out = dot(act_out[...], weights[at : at + wide, 2 * hidden :], NT)
            out_mine[:, at : at + wide] = out[:half]
            out_theirs[:, at : at + wide] = out[half:].astype(bf16)

    return kernel


def add_round():
    def kernel(mine, theirs, sent_out):
        sent_out[...] = (mine[...] + theirs[...].astype(f32)).astype(bf16)

    return kernel


def add_split(quarter):
    def kernel(here, mine, theirs, own_out, sent_out):
        pair = here[4]
        own = rows_at(pair, quarter)
        away = rows_at(1 - pair, quarter)
        own_out[...] = mine[own, :] + theirs[own, :].astype(f32)
        sent_out[...] = (mine[away, :] + theirs[away, :].astype(f32)).astype(sent_out.dtype)

    return kernel


def middle_back(quarter, width, inner_total):
    def kernel(
        here, sent, got, own, across, middle_in, scales, core_total, pair_sent, gain,
        dmiddle_out, back_out, gain_out,
    ):
        pair = here[4]
        d_post = sent[...].astype(f32) + got[...].astype(f32)
        middle = middle_in[...]
        scale_mix, scale = scales[:, 0:1], scales[:, 1:2]
        gain_out[...] = 0.5 * jnp.sum(d_post * middle * scale, 0, keepdims=True)
        scaled = d_post * gain[...]
        dmiddle_out[rows_at(pair, quarter), :] = own[quarter:, :].astype(f32)
        dmiddle_out[rows_at(1 - pair, quarter), :] = across[quarter:, :].astype(f32)
        d_middle = (
            dmiddle_out[...]
            + scale * scaled
            - middle * (scale * scale * scale) * jnp.mean(scaled * middle, -1, keepdims=True)
        )
        dmiddle_out[...] = d_middle
        d_proj = (scale_mix * d_middle.astype(bf16).astype(f32)).astype(bf16)
        back_out[:, :width] = d_proj
        projected = core_total[...] + pair_sent[:, :width].astype(f32)
        d_scale = jnp.sum(d_proj.astype(f32) * projected, -1, keepdims=True)
        coeff = -d_scale * scale_mix * scale_mix / inner_total
        high = coeff.astype(bf16).astype(f32)
        lane = ids((2 * quarter, LANES), 1)
        back_out[:, width:] = jnp.where(lane == 0, high, jnp.where(lane == 1, coeff - high, 0.0)).astype(bf16)

    return kernel


def gate_back(heads, inner, state):
    pairs = heads // 2

    def kernel(
        here, back_mine, back_theirs, w_back, y_in, proj, conv, cum_in, gain,
        dproj_out, dy_out, dz_out, gain_out, enter_out, sums, factors, d_mixed,
    ):
        rows = y_in.shape[0]
        quarter = rows // 4
        width = dproj_out.shape[1]
        core = here[3]
        for index in range(2):
            part = slice(index * quarter, (index + 1) * quarter)
            for ref, at in ((back_mine, 2 * index + core), (back_theirs, 2 * index + 1 - core)):
                dproj_out[rows_at(at, quarter), :] = ref[part, :width]
                factors[rows_at(at, quarter), :] = ref[part, width:].astype(f32)
        d_mixed[...] = dot(dproj_out[...], w_back[...])
        cum = cum_in[...]
        opening = jnp.where(cum[:, heads : heads + 1] == 0.0, jnp.exp(cum), 0.0)
        c_conv = conv[:, inner + state : inner + 2 * state]
        c_rows = c_conv * jax.nn.sigmoid(c_conv)
        factor = factors[:, 0:1] + factors[:, 1:2]
        for pair in range(pairs):
            at = pair * LANES
            y_pair = y_in[:, at : at + LANES]
            z_pair = proj[EDGE : EDGE + rows, at : at + LANES]
            sigma = jax.nn.sigmoid(z_pair)
            silu = z_pair * sigma
            gated = y_pair * silu
            d_mix = d_mixed[:, at : at + LANES]
            gain_out[:, at : at + LANES] = jnp.sum(d_mix * gated, 0, keepdims=True)
            d_gated = d_mix * gain[:, at : at + LANES] + factor * gated
            dz_out[:, at : at + LANES] = (d_gated * y_pair * silu_slope(z_pair, sigma)).astype(bf16)
            d_y = d_gated * silu
            dy_out[:, at : at + LANES] = d_y
            sums[at : at + LANES, :] = dot_both(d_y * per_head(opening, pair, rows), c_rows, TN)
        last = cum[rows - 1 : rows, :]
        last_run = last[:, heads : heads + 1]
        fill_states(enter_out, sums, jnp.where(last_run == 0.0, jnp.exp(last), 0.0), heads)

    return kernel


def bc_split(quarter, inner):
    def kernel(here, d_bc, tail, mine_out, theirs_out, whole):
        core = here[3]
        last = d_bc.shape[0] - EDGE
        whole[0:last, :] = d_bc[0:last, :]
        whole[last:, :] = d_bc[last:, :] + tail[:, inner:]
        for index in range(2):
            part = slice(index * quarter, (index + 1) * quarter)
            mine_out[part, :] = whole[rows_at(2 * index + core, quarter), :]
            theirs_out[part, :] = whole[rows_at(2 * index + 1 - core, quarter), :]

    return kernel


def bc_back(first, state):
    def kernel(own_sum, got, tokens, win, own_out, rows_out, gain_out, weights, done):
        copy = pltpu.make_async_copy(win.at[:, pl.ds(first, 2 * state)], weights, done)
        copy.start()
        total = (own_sum[...] + got[...]).astype(bf16)
        own_out[...] = total
        value = tokens[...].astype(f32)
        scale = lax.rsqrt(jnp.mean(value * value, -1, keepdims=True) + eps)
        copy.wait()
        rows = dot(total, weights[...], NT)
        rows_out[...] = rows
        gain_out[...] = jnp.sum(rows * value * scale, 0, keepdims=True)

    return kernel


def input_back(quarter, inner, state):
    def kernel(here, d_z, d_x, tail, d_dt, win, rows_in, dall_out, mine_out, theirs_out, gain_out, d_in):
        core = here[3]
        rows, width = rows_in.shape
        dall_out[:, :inner] = d_z[...]
        dall_out[:, inner : 2 * inner] = d_x[...].astype(bf16)
        dall_out[rows - EDGE :, inner : 2 * inner] = (d_x[rows - EDGE :, :] + tail[:, :inner]).astype(bf16)
        dall_out[:, 2 * inner :] = d_dt[...]
        wide = 2 * LANES
        for at in range(0, width, wide):
            d_in[:, at : at + wide] = dot(dall_out[:, : 2 * inner], win[at : at + wide, : 2 * inner], NT) + dot(
                d_dt[...], win[at : at + wide, 2 * inner + 2 * state :], NT
            )
        value = rows_in[...].astype(f32)
        scale = lax.rsqrt(jnp.mean(value * value, -1, keepdims=True) + eps)
        gain_out[...] = jnp.sum(d_in[...] * value * scale, 0, keepdims=True)
        for index in range(2):
            part = slice(index * quarter, (index + 1) * quarter)
            mine_out[part, :] = d_in[rows_at(2 * index + core, quarter), :]
            theirs_out[part, :] = d_in[rows_at(2 * index + 1 - core, quarter), :].astype(bf16)

    return kernel


def input_grad(quarter):
    def kernel(here, own_sum, got, bc_part, tokens, d_middle, gain, grad_out):
        pair = here[4]
        value = tokens[...].astype(f32)
        scale = lax.rsqrt(jnp.mean(value * value, -1, keepdims=True) + eps)
        scaled = (own_sum[...] + got[...].astype(f32) + bc_part[...]) * gain[...]
        grad_out[...] = (
            d_middle[rows_at(pair, quarter), :]
            + scale * scaled
            - value * (scale * scale * scale) * jnp.mean(scaled * value, -1, keepdims=True)
        )

    return kernel


def layer_out(quarter):
    def kernel(here, own_sum, got, middle, out):
        out[...] = middle[rows_at(here[4], quarter), :] + own_sum[...] + got[...].astype(f32)

    return kernel


def scan_back(heads, inner, state):
    pairs = heads // 2
    tiles = (inner + 2 * state) // LANES

    def kernel(
        proj, taps, lags, bias, alog, skip, conv, cum_in, steps_in, dy_in, entering, leaving,
        dx_out, dbc_out, tail_out, ddt_out, conv_grad, head_grad, skip_grad, dact, rowsums, dpre_out,
    ):
        rows = dy_in.shape[0]
        count = taps.shape[0] // 2
        cum = cum_in[...]
        steps = steps_in[...]
        lane = ids((rows, LANES), 1)
        left = lane < LANES // 2
        turned, run_col, last_run, keep = run_info(cum, heads)
        b_conv = conv[:, inner : inner + state]
        c_conv = conv[:, inner + state : inner + 2 * state]
        b_rows = b_conv * jax.nn.sigmoid(b_conv)
        c_rows = c_conv * jax.nn.sigmoid(c_conv)
        inner_cb = dot_exact(c_rows, b_rows, NT)
        last_cum = cum[rows - 1 : rows, :]
        closing = jnp.where(run_col == last_run, jnp.exp(last_cum - cum), 0.0)
        opening = jnp.where(run_col == 0.0, jnp.exp(cum), 0.0)
        keep_old = jnp.where(last_run == 0.0, jnp.exp(last_cum), 0.0)
        d_cb = jnp.zeros((rows, rows), f32)
        d_b = jnp.zeros((rows, state), f32)
        d_c = jnp.zeros((rows, state), f32)
        d_cum = jnp.zeros((rows, LANES), f32)
        d_steps = jnp.zeros((rows, LANES), f32)
        d_open = jnp.zeros((rows, LANES), f32)
        d_close = jnp.zeros((rows, LANES), f32)
        d_keep = jnp.zeros((1, LANES), f32)
        lane_row = ids((1, LANES), 1)
        rowsums[...] = jnp.zeros_like(rowsums)
        for pair in range(pairs):
            at = pair * LANES
            x_conv = conv[:, at : at + LANES]
            x_pair = x_conv * jax.nn.sigmoid(x_conv)
            d_y = dy_in[:, at : at + LANES]
            step_pair = per_head(steps, pair, rows)
            scaled = x_pair * step_pair
            enter_pair = entering[at : at + LANES, :]
            leave_pair = leaving[at : at + LANES, :]
            close_pair = per_head(closing, pair, rows)
            b_leave = dot(b_rows, leave_pair, NT)
            c_enter = dot(c_rows, enter_pair, NT)
            d_b = d_b + dot_both(scaled * close_pair, leave_pair)
            d_c = d_c + dot_both(d_y * per_head(opening, pair, rows), enter_pair)
            close_prod = b_leave * scaled
            open_prod = d_y * c_enter
            keep_prod = enter_pair * leave_pair
            parts = []
            for side, head in ((0, 2 * pair), (1, 2 * pair + 1)):
                mine = left if side == 0 else ~left
                gaps = cum[:, head : head + 1] - turned[head : head + 1, :]
                decay = jnp.exp(jnp.where(keep, gaps, -jnp.inf))
                weights = decay * inner_cb
                d_weights = dot_both(jnp.where(mine, d_y, 0.0), scaled, NT)
                d_cb = d_cb + d_weights * decay
                flow = d_weights * weights
                d_cum = d_cum + jnp.where(lane == head, jnp.sum(flow, 1, keepdims=True), 0.0)
                rowsums[head : head + 1, :] = jnp.sum(flow, 0, keepdims=True)
                parts.append(dot(weights, d_y, TN))
                half = LANES // 2
                kept = jnp.sum(
                    jnp.sum(keep_prod[side * half : side * half + half, :], 0, keepdims=True), 1, keepdims=True
                )
                d_keep = d_keep + jnp.where(lane_row == head, kept, 0.0)
                d_open = d_open + jnp.where(
                    lane == head, jnp.sum(jnp.where(mine, open_prod, 0.0), 1, keepdims=True), 0.0
                )
                d_close = d_close + jnp.where(
                    lane == head, jnp.sum(jnp.where(mine, close_prod, 0.0), 1, keepdims=True), 0.0
                )
            d_scaled = jnp.where(left, parts[0], parts[1]) + close_pair * b_leave
            skip_grad[:, at : at + LANES] = jnp.sum(d_y * x_pair, 0, keepdims=True)
            dact[:, at : at + LANES] = step_pair * d_scaled + skip[:, at : at + LANES] * d_y
            step_prod = d_scaled * x_pair
            for side, head in ((0, 2 * pair), (1, 2 * pair + 1)):
                mine = left if side == 0 else ~left
                d_steps = d_steps + jnp.where(
                    lane == head, jnp.sum(jnp.where(mine, step_prod, 0.0), 1, keepdims=True), 0.0
                )
        dact[:, inner : inner + state] = d_b + dot_both(d_cb, c_rows, TN)
        dact[:, inner + state : inner + 2 * state] = d_c + dot_both(d_cb, b_rows)
        ended = closing * d_close
        d_last = jnp.sum(ended, 0, keepdims=True) + keep_old * d_keep
        d_cum = d_cum - rowsums[...].T + opening * d_open - ended
        d_cum = d_cum + jnp.where(ids((rows, LANES), 0) == rows - 1, d_last, 0.0)
        upper = (ids((rows, rows), 0) <= ids((rows, rows), 1)).astype(f32)
        d_logs = jnp.where(lane < heads, dot_exact(upper, d_cum), 0.0)
        rate = jnp.exp(alog[...])
        raw = proj[EDGE : EDGE + rows, 2 * inner + 2 * state :] + bias[...]
        d_raw = (d_steps - rate * d_logs) * jax.nn.sigmoid(raw)
        ddt_out[...] = d_raw.astype(bf16)
        head_grad[...] = jnp.zeros_like(head_grad)
        head_grad[0:1, :] = jnp.sum(d_raw, 0, keepdims=True)
        head_grad[1:2, :] = -jnp.sum(d_logs * steps, 0, keepdims=True) * rate
        dpre_out[...] = jnp.zeros_like(dpre_out)
        conv_grad[...] = jnp.zeros_like(conv_grad)
        for tile in range(tiles):
            at = tile * LANES
            value = conv[:, at : at + LANES]
            sigma = jax.nn.sigmoid(value)
            d_conv = dact[:, at : at + LANES] * (sigma * (1.0 + value * (1.0 - sigma)))
            for back in range(count):
                tap = count - 1 - back
                masked = d_conv * lags[:, back : back + 1]
                source = proj[EDGE - back : EDGE - back + rows, inner + at : inner + at + LANES]
                conv_grad[tap : tap + 1, at : at + LANES] = jnp.sum(masked * source, 0, keepdims=True)
                dpre_out[EDGE - back : EDGE - back + rows, at : at + LANES] += (
                    taps[tap : tap + 1, at : at + LANES] * masked
                )
        dx_out[...] = dpre_out[EDGE:, :inner]
        dbc_out[...] = dpre_out[EDGE:, inner:]
        tail_out[...] = dpre_out[0:EDGE, :]

    return kernel


def chain_states(reverse, blocks, size):
    def kernel(parts, carried_out):
        factors = parts[:, size, :].T
        carried = jnp.zeros((size, LANES), f32)
        for turn in range(blocks):
            k = blocks - 1 - turn if reverse else turn
            carried_out[k] = carried
            carried = factors[0:size, k : k + 1] * carried + parts[k, 0:size, :]

    return kernel


def exchange_states(sent, size, axis, reverse, wait=()):
    blocks = lax.axis_size(axis)
    parts = after(wait, lax.all_to_all(sent, axis, 0, 0, tiled=True))
    carried = kernel_call(
        chain_states(reverse, blocks, size), [shape_of((blocks, size, LANES))], parts
    )[0]
    back = lax.all_to_all(carried, axis, 0, 0, tiled=True)
    return back.reshape(blocks * size, LANES), carried


def other(value, bit):
    count = lax.axis_size("tensor")
    return lax.ppermute(value, "tensor", [(rank, rank ^ bit) for rank in range(count)])


def after(first, value):
    return lax.optimization_barrier((first, value))[1]


def place():
    x_size, z_size, y_size = DP_SHAPE
    index = lax.axis_index("dp")
    return index // (z_size * y_size), index // y_size % z_size, index % y_size


def shift(value, axis, step):
    x_size, z_size, y_size = DP_SHAPE
    pairs = []
    for x in range(x_size):
        for z in range(z_size):
            for y in range(y_size):
                to_x = (x + step) % x_size if axis == "x" else x
                to_z = (z + step) % z_size if axis == "z" else z
                to_y = (y + step) % y_size if axis == "y" else y
                pairs.append(((x * z_size + z) * y_size + y, (to_x * z_size + to_z) * y_size + to_y))
    return lax.ppermute(value, "dp", pairs)


RING = (0, -1, 1, 2)


def spread(pack, near, split):
    mids = []
    for columns, axis in ((slice(0, split), "y"), (slice(split, None), "x")):
        own = jnp.stack([pack[:, columns], near[:, columns]])
        back, ahead = shift(own, axis, 1), shift(own, axis, -1)
        far = [shift(back[:1], axis, 1), shift(ahead[1:], axis, -1)]
        mids.append((own, back, ahead, *far))
    return mids


def finish(mids):
    return [(mid, shift(mid, axis, 1), shift(mid, axis, -1)) for mid, axis in zip(mids, "xy", strict=True)]


def finish_far(rings):
    pieces = []
    for (mid, back, ahead), axis in zip(rings, "xy", strict=True):
        pieces += [mid, back, ahead, shift(back[:4], axis, 1), shift(ahead[4:], axis, -1)]
    return pieces


SENT = 5


def cut_chunks(outs, rows_of, part):
    own, to_ahead, to_back, ahead_first, back_second = outs
    own[0:part, :] = rows_of(0, 0)
    own[part:, :] = rows_of(0, 1)
    to_ahead[0:part, :] = rows_of(2, 0)
    to_ahead[part:, :] = rows_of(1, 1)
    to_back[0:part, :] = rows_of(2, 1)
    to_back[part:, :] = rows_of(-1, 0)
    ahead_first[...] = rows_of(1, 0)
    back_second[...] = rows_of(-1, 1)


def chunk_shapes(part, widths):
    shapes = []
    for width in widths:
        shapes += [shape_of((2 * part, width), bf16)] * 3 + [shape_of((part, width), bf16)] * 2
    return shapes


def wrapped(index, step):
    return lax.rem(index + (step + 4), 4)


def term_products(plan, shard):
    x_size, z_size, y_size = DP_SHAPE
    part = 4 * shard

    def kernel(here, *refs):
        count = 1 + max(max(lhs, rhs) for terms in plan for lhs, rhs, _, _ in terms)
        arrays, outs, scratch = refs[:count], refs[count : count + 2 * SENT], refs[count + 2 * SENT :]
        x, y = here[0], here[2]
        for half, terms in enumerate(plan):
            product = scratch[half]
            at = 0
            for lhs, rhs, first, last in terms:
                for start in range(first, last, 2 * LANES):
                    stop = min(start + 2 * LANES, last)
                    product[:, at : at + stop - start] = dot(
                        arrays[lhs][...], arrays[rhs][:, start:stop], TN
                    ).astype(bf16)
                    at += stop - start

            def along_x(step, side, product=product):
                row = (wrapped(x, step) * 2 + side) * part
                return product[pl.ds(pl.multiple_of(row, part), part), :]

            def along_y(step, side, product=product):
                groups = range(side * 4, side * 4 + 4)
                rows = [(group * y_size + wrapped(y, step)) * shard for group in groups]
                return jnp.concatenate([product[pl.ds(pl.multiple_of(row, 16), shard), :] for row in rows], 0)

            cut_chunks(outs[half * SENT : (half + 1) * SENT], along_x if half == 0 else along_y, part)

    return kernel


def ring_add(part):
    def kernel(*refs):
        for half in range(2):
            from_back, from_ahead, ahead_first, back_second = refs[4 * half : 4 * half + 4]
            ahead_out, back_out = refs[8 + 2 * half : 10 + 2 * half]
            ahead_out[...] = (ahead_first[...].astype(f32) + from_back[0:part, :].astype(f32)).astype(bf16)
            back_out[...] = (back_second[...].astype(f32) + from_ahead[0:part, :].astype(f32)).astype(bf16)

    return kernel


def ring_totals(refs, part):
    own, from_back, from_ahead, from_back_last, from_ahead_last = refs
    first = own[0:part, :].astype(f32) + from_ahead[part:, :].astype(f32) + from_back_last[...].astype(f32)
    second = own[part:, :].astype(f32) + from_back[part:, :].astype(f32) + from_ahead_last[...].astype(f32)
    return first, second


def ring_fold(shard):
    part = 4 * shard

    def kernel(here, *refs):
        x, y = here[0], here[2]
        outs, scratch = refs[2 * SENT : 4 * SENT], refs[4 * SENT :]
        for half in range(2):
            total = scratch[half]
            total[0:part, :], total[part:, :] = ring_totals(refs[half * SENT : (half + 1) * SENT], part)

            def along_y(step, side, total=total):
                row = side * part + wrapped(y, step) * shard
                return total[pl.ds(pl.multiple_of(row, 16), shard), :].astype(bf16)

            def along_x(step, side, total=total):
                row = (wrapped(x, step) * 2 + side) * shard
                return total[pl.ds(pl.multiple_of(row, 16), shard), :].astype(bf16)

            cut_chunks(outs[half * SENT : (half + 1) * SENT], along_y if half == 0 else along_x, shard)

    return kernel


def ring_end(shard, widths):
    def kernel(here, *refs):
        z = here[1]
        mine_out, sent_out = refs[2 * SENT :]
        at = 0
        for half in range(2):
            first, second = ring_totals(refs[half * SENT : (half + 1) * SENT], shard)
            columns = slice(at, at + widths[half])
            mine_out[:, columns] = jnp.where(z == 0, first, second)
            sent_out[:, columns] = jnp.where(z == 0, second, first).astype(bf16)
            at += widths[half]

    return kernel


def ring_send(chunks, axes):
    arrived, stays = [], []
    for half, axis in enumerate(axes):
        own, to_ahead, to_back, ahead_first, back_second = chunks[half * SENT : (half + 1) * SENT]
        arrived += [shift(to_ahead, axis, 1), shift(to_back, axis, -1)]
        stays.append((own, ahead_first, back_second))
    return arrived, stays


def ring_pass(arrived, stays, plan, axes, part, wait=None):
    terms = []
    for half in range(2):
        terms += [*arrived[2 * half : 2 * half + 2], *stays[half][1:]]
    if wait is not None:
        terms = after(wait, terms)
    shapes = [shape_of((part, width), bf16) for width in widths_of(plan) for _ in range(2)]
    sent = kernel_call(ring_add(part), shapes, *terms)
    results = []
    for half, axis in enumerate(axes):
        last = [shift(sent[2 * half], axis, 1), shift(sent[2 * half + 1], axis, -1)]
        results += [stays[half][0], *arrived[2 * half : 2 * half + 2], *last]
    return results


def widths_of(plan):
    return [sum(last - first for _, _, first, last in terms) for terms in plan]


def scatter_begin(here, plan, arrays, shard):
    part = 4 * shard
    widths = widths_of(plan)
    return kernel_call(
        term_products(plan, shard), chunk_shapes(part, widths), here, *arrays,
        flops=sum(2 * arrays[0].shape[0] * 8 * part * width for width in widths),
        small=(0,),
        scratch=[pltpu.VMEM((8 * part, width), bf16) for width in widths],
    )


def scatter_fold(here, results, plan, shard):
    widths = widths_of(plan)
    return kernel_call(
        ring_fold(shard), chunk_shapes(shard, widths), here, *results,
        small=(0,),
        scratch=[pltpu.VMEM((8 * shard, width), f32) for width in widths],
    )


def scatter_last(here, results, plan, shard):
    widths = widths_of(plan)
    shape = (shard, sum(widths))
    mine, sent = kernel_call(
        ring_end(shard, widths), [shape_of(shape), shape_of(shape, bf16)], here, *results,
        small=(0,),
    )
    return mine + shift(sent, "z", 1).astype(f32)


EACH = 6


def small_rows(model_dim, inner, state, taps, ranks):
    wide, share = model_dim // LANES, inner // LANES
    sizes = {
        "norm": wide,
        "post": wide,
        "taps": taps * ranks * share,
        "bc": taps * 2 * state // LANES,
        "gain": ranks * share,
        "skip": ranks * share,
        "heads": 2 * ranks,
    }
    rows, at = {}, 0
    for name, size in sizes.items():
        rows[name] = at
        at += size
    return rows


def small_table(layout, inner, state, taps, heads):
    share = inner // LANES

    def kernel(here, norm, norm_bc, post, conv, gain, head, skip, out, table):
        rank = here[4] * 2 + here[3]
        ranks = (layout["skip"] - layout["gain"]) // share

        def lanes(i):
            return slice(i * LANES, (i + 1) * LANES)

        table[...] = jnp.zeros_like(table)
        for i in range(layout["post"] - layout["norm"]):
            table[layout["norm"] + i : layout["norm"] + i + 1, :] = norm[:, lanes(i)] + norm_bc[:, lanes(i)]
            table[layout["post"] + i : layout["post"] + i + 1, :] = post[:, lanes(i)]
        for i in range(share):
            for tap in range(taps):
                row = layout["taps"] + tap * ranks * share + rank * share + i
                table[pl.ds(row, 1), :] = conv[tap : tap + 1, lanes(i)]
            table[pl.ds(layout["gain"] + rank * share + i, 1), :] = gain[:, lanes(i)]
            table[pl.ds(layout["skip"] + rank * share + i, 1), :] = skip[:, lanes(i)]
        wide = 2 * state // LANES
        for tap in range(taps):
            for i in range(wide):
                row = layout["bc"] + tap * wide + i
                table[row : row + 1, :] = conv[tap : tap + 1, lanes(share + i)]
        for i in range(2):
            table[pl.ds(layout["heads"] + i * ranks + rank, 1), :] = head[i : i + 1, :]
        out[...] = jnp.zeros_like(out)
        for block in range(out.shape[0]):
            out[block, 0:EACH, :] = table[block * EACH : (block + 1) * EACH, :]

    return kernel


def small_sum():
    def kernel(parts, out):
        out[...] = jnp.broadcast_to(jnp.sum(parts[...], 0, keepdims=True), out.shape)

    return kernel


def small_out(layout, ranks, inner, state, taps):
    def kernel(parts, norm, post, conv_x, conv_bc, gain, skip, head, table):
        for block in range(parts.shape[0] // ranks):
            total = jnp.sum(parts[block * ranks : (block + 1) * ranks], 0)
            table[block * EACH : (block + 1) * EACH, :] = total[0:EACH, :]

        def spread_out(ref, line, first):
            for i in range(ref.shape[1] // LANES):
                ref[line : line + 1, i * LANES : (i + 1) * LANES] = table[first + i : first + i + 1, :]

        spread_out(norm, 0, layout["norm"])
        spread_out(post, 0, layout["post"])
        spread_out(gain, 0, layout["gain"])
        spread_out(skip, 0, layout["skip"])
        for tap in range(taps):
            spread_out(conv_x, tap, layout["taps"] + tap * (conv_x.shape[1] // LANES))
            spread_out(conv_bc, tap, layout["bc"] + tap * (conv_bc.shape[1] // LANES))
        head[...] = table[layout["heads"] : layout["heads"] + 2 * ranks, :]

    return kernel


def body(
    tokens,
    cotangent,
    segments,
    routes,
    gate_weights,
    norm_gain,
    w_zx,
    w_bc,
    w_dt,
    conv_x,
    conv_bc,
    dt_bias,
    a_log,
    d_skip,
    mix_gain,
    w_out,
    post_gain,
    exp_gate,
    exp_up,
    exp_down,
    sh_gate,
    sh_up,
    sh_down,
):
    tensor_count = lax.axis_size("tensor")
    tensor_rank = lax.axis_index("tensor")
    pair, core = tensor_rank // 2, tensor_rank % 2
    dp_count = lax.axis_size("dp")
    here = jnp.stack([*place(), core, pair]).astype(jnp.int32)
    quarter = tokens.shape[0]
    block_rows = segments.shape[0]
    model_dim = tokens.shape[1]
    shard = w_zx.shape[0]
    inner = w_zx.shape[2]
    heads = w_dt.shape[1]
    head_dim = inner // heads
    state = w_bc.shape[2]
    conv_taps = conv_x.shape[0]
    inner_total = inner * tensor_count
    head_total = heads * tensor_count
    experts = exp_gate.shape[0]
    ffe = exp_gate.shape[2]
    ffs = sh_gate.shape[1]
    hidden = experts * ffe + ffs
    wide_in = 2 * inner + 2 * state + LANES

    own_rows = jnp.concatenate([tokens, cotangent], 0)
    pack_in = jnp.concatenate(
        [
            w_zx.reshape(shard, 2 * inner),
            w_bc.reshape(shard, 2 * state),
            jnp.pad(w_dt, ((0, 0), (0, LANES - heads))),
            w_out.T,
        ],
        1,
    )
    pack_rest = jnp.concatenate(
        [
            exp_gate.transpose(1, 0, 2).reshape(shard, experts * ffe),
            sh_gate,
            exp_up.transpose(1, 0, 2).reshape(shard, experts * ffe),
            sh_up,
            exp_down.transpose(2, 0, 1).reshape(shard, experts * ffe),
            sh_down.T,
        ],
        1,
    )
    in_columns, rest_columns = wide_in, pack_rest.shape[1]
    in_split, rest_split = pack_in.shape[1] // 256 * LANES, rest_columns // 256 * LANES
    in_near, rest_near = shift(pack_in, "z", 1), shift(pack_rest, "z", 1)
    both_splits = zip((pack_in, pack_rest), (in_split, rest_split), strict=True)
    pack = [[part[:, :split], part[:, split:]] for part, split in both_splits]
    both_splits = zip((in_near, rest_near), (in_split, rest_split), strict=True)
    near = [[part[:, :split], part[:, split:]] for part, split in both_splits]
    mids = spread(
        jnp.concatenate([pack[0][0], pack[1][0], pack[0][1], pack[1][1]], 1),
        jnp.concatenate([near[0][0], near[1][0], near[0][1], near[1][1]], 1),
        in_split + rest_split,
    )
    cuts = (in_split, pack_in.shape[1] - in_split)
    in_mids = [
        jnp.concatenate([part[:, :, :cut] for part in parts], 0) for parts, cut in zip(mids, cuts, strict=True)
    ]
    rest_mids = [
        jnp.concatenate([part[:, :, cut:] for part in parts], 0) for parts, cut in zip(mids, cuts, strict=True)
    ]
    in_rings = finish(in_mids)
    core_rows = other(own_rows, 1)
    pair_rows = other(own_rows, 2)
    far_rows = other(pair_rows, 1)
    rows_all, normed_in, normed_own = kernel_call(
        input_rows(quarter, model_dim),
        [shape_of((block_rows, model_dim), bf16)] * 2 + [shape_of((quarter, model_dim), bf16)],
        here, own_rows, pair_rows, core_rows, far_rows, norm_gain[None, :],
        small=(0,),
    )
    tail_rows = from_behind(normed_in[block_rows - EDGE :], "dp", 1)
    in_pieces = finish_far(after(tail_rows, in_rings))
    rest_rings = finish(after(in_pieces, rest_mids))

    head_start = tensor_rank * heads
    chan_start = tensor_rank * inner
    bias_local = lax.dynamic_slice_in_dim(dt_bias, head_start, heads)
    alog_local = lax.dynamic_slice_in_dim(a_log, head_start, heads)
    skip_local = lax.dynamic_slice_in_dim(d_skip, head_start, heads)
    gain_row = lax.dynamic_slice_in_dim(mix_gain, chan_start, inner)[None, :]
    convx_local = lax.dynamic_slice_in_dim(conv_x, chan_start, inner, 1)
    taps = jnp.concatenate([convx_local, conv_bc.reshape(conv_taps, 2 * state)], 1)
    taps = jnp.pad(taps, ((0, conv_taps), (0, 0)))
    bias_row = jnp.pad(bias_local, (0, LANES - heads))[None, :]
    alog_row = jnp.pad(alog_local, (0, LANES - heads))[None, :]
    skip_row = jnp.repeat(skip_local, head_dim)[None, :]

    seg_float = segments.astype(f32)
    tail_ids = from_behind(seg_float[block_rows - EDGE :], "dp", 1)
    ids_ext = jnp.concatenate([tail_ids, seg_float])
    global_rows = lax.axis_index("dp") * block_rows + jnp.arange(block_rows, dtype=jnp.int32)
    lags = [
        (
            (ids_ext[EDGE - back : EDGE - back + block_rows] == seg_float) & (global_rows >= back)
        ).astype(f32)
        for back in range(conv_taps)
    ]
    lags = jnp.pad(jnp.stack(lags, 1), ((0, 0), (0, LANES - conv_taps)))

    scan_flops = 2 * block_rows * block_rows * inner * 2
    size = inner // dp_count
    state_shape = shape_of((dp_count, size + SUB, state))
    win, proj, y_first, conv, cum, steps, state_sum = kernel_call(
        scan_front(heads, inner, state, shard, column_ranges(in_split, 0, in_columns)),
        [
            shape_of((model_dim, in_columns), bf16),
            shape_of((block_rows + EDGE, in_columns)),
            shape_of((block_rows, inner)),
            shape_of((block_rows, inner + 2 * state)),
            shape_of((block_rows, LANES)),
            shape_of((block_rows, LANES)),
            state_shape,
        ],
        here, normed_in, tail_rows, taps, lags, bias_row, alog_row, skip_row, *in_pieces,
        flops=scan_flops + 2 * block_rows * model_dim * in_columns,
        small=(0,),
        raw=range(8, 8 + PIECES),
        scratch=[
            pltpu.VMEM((block_rows, inner + 2 * state), f32),
            pltpu.VMEM((inner, state), f32),
            pltpu.SemaphoreType.DMA((64,)),
        ],
    )
    entering, carried = exchange_states(state_sum, size, "dp", False, [ring[1:] for ring in rest_rings])
    rest_pieces = finish_far(after(carried, rest_rings))
    entering = after(rest_pieces, entering)
    w_back, y_all, mixer_in, mine, theirs = kernel_call(
        gate_front(heads, inner, state, shard, column_ranges(in_split, in_columns, in_columns + inner)),
        [
            shape_of((model_dim, inner), bf16),
            shape_of((block_rows, inner)),
            shape_of((block_rows, inner), bf16),
            shape_of((2 * quarter, model_dim + LANES)),
            shape_of((2 * quarter, model_dim + LANES)),
        ],
        here, y_first, proj, conv, cum, entering, gain_row, *in_pieces,
        flops=scan_flops,
        small=(0,),
        raw=range(7, 7 + PIECES),
        scratch=[
            pltpu.VMEM((block_rows, inner), bf16),
            pltpu.VMEM((block_rows, model_dim + LANES), f32),
            pltpu.SemaphoreType.DMA((64,)),
        ],
    )
    core_total, sent = kernel_call(
        core_sum(model_dim),
        [shape_of((2 * quarter, model_dim)), shape_of((2 * quarter, model_dim + LANES), bf16)],
        mine, other(theirs, 1),
    )
    from_pair = other(sent, 2)
    middle, post_mine, scales = kernel_call(
        middle_rows(quarter, model_dim, inner_total),
        [
            shape_of((2 * quarter, model_dim)),
            shape_of((2 * quarter, model_dim), bf16),
            shape_of((2 * quarter, LANES)),
        ],
        here, sent, from_pair, own_rows, pair_rows, post_gain[None, :],
        small=(0,),
    )
    post_theirs = other(post_mine, 1)
    hot = routes[:, :, None] == jnp.arange(LANES, dtype=jnp.int32)[None, None, :]
    share = jnp.sum(jnp.where(hot, gate_weights[:, :, None], 0.0), 1)
    half_shape = (2 * quarter, model_dim)
    post, cot, act, d_pre, ffn_mine, ffn_theirs, dpost_mine, dpost_theirs = kernel_call(
        experts_both(quarter, hidden, ffe, experts, shard, column_ranges(rest_split, 0, 3 * hidden)),
        [
            shape_of((block_rows, model_dim), bf16),
            shape_of((block_rows, model_dim), bf16),
            shape_of((block_rows, hidden), bf16),
            shape_of((block_rows, 2 * hidden), bf16),
            shape_of(half_shape),
            shape_of(half_shape, bf16),
            shape_of(half_shape),
            shape_of(half_shape, bf16),
        ],
        here, post_mine, post_theirs, own_rows, pair_rows, core_rows, far_rows, share, *rest_pieces,
        flops=12 * block_rows * model_dim * hidden,
        small=(0,),
        raw=range(8, 8 + PIECES),
        scratch=[
            pltpu.VMEM((model_dim, 3 * hidden), bf16),
            pltpu.VMEM((block_rows, LANES), f32),
            pltpu.SemaphoreType.DMA((128,)),
        ],
    )
    ffn_split = (3 * hidden) // 256 * LANES
    ffn_plan = (((0, 2, 0, ffn_split),), ((0, 2, ffn_split, 2 * hidden), (1, 3, 0, hidden)))
    ffn_chunks = scatter_begin(here, ffn_plan, (post, cot, d_pre, act), shard)
    ffn_sent, ffn_terms = ring_send(ffn_chunks, "xy")
    dpost_theirs = after(ffn_chunks, dpost_theirs)
    sent_post = kernel_call(add_round(), [shape_of(half_shape, bf16)], dpost_mine, other(dpost_theirs, 1))[0]
    d_middle, back_mine, grad_post_gain = kernel_call(
        middle_back(quarter, model_dim, inner_total),
        [
            shape_of(half_shape),
            shape_of((2 * quarter, model_dim + LANES), bf16),
            shape_of((1, model_dim)),
        ],
        here, sent_post, other(sent_post, 2), own_rows, pair_rows, middle, scales, core_total, from_pair,
        post_gain[None, :],
        small=(0,),
    )
    back_theirs = other(back_mine, 1)
    d_proj, d_y, d_z, grad_gain, d_enter = kernel_call(
        gate_back(heads, inner, state),
        [
            shape_of((block_rows, model_dim), bf16),
            shape_of((block_rows, inner)),
            shape_of((block_rows, inner), bf16),
            shape_of((1, inner)),
            state_shape,
        ],
        here, back_mine, back_theirs, w_back, y_all, proj, conv, cum, gain_row,
        flops=scan_flops,
        small=(0,),
        scratch=[
            pltpu.VMEM((inner, state), f32),
            pltpu.VMEM((block_rows, LANES), f32),
            pltpu.VMEM((block_rows, inner), f32),
        ],
    )

    ffn_own, ffn_away = kernel_call(
        add_split(quarter),
        [shape_of((quarter, model_dim)), shape_of((quarter, model_dim), bf16)],
        here, ffn_mine, other(ffn_theirs, 1),
        small=(0,),
    )
    block_out = kernel_call(
        layer_out(quarter),
        [shape_of((quarter, model_dim))],
        here, ffn_own, other(ffn_away, 2), middle,
        small=(0,),
    )[0]

    leaving, carried = exchange_states(d_enter, size, "dp", True, ffn_sent)
    ffn_rings = ring_pass(ffn_sent, ffn_terms, ffn_plan, "xy", 4 * shard, carried)
    leaving = after(ffn_rings, leaving)
    d_x, d_bc, tail, d_dt, grad_taps, grad_heads, grad_skip = kernel_call(
        scan_back(heads, inner, state),
        [
            shape_of((block_rows, inner)),
            shape_of((block_rows, 2 * state)),
            shape_of((EDGE, inner + 2 * state)),
            shape_of((block_rows, LANES), bf16),
            shape_of((SUB, inner + 2 * state)),
            shape_of((SUB, LANES)),
            shape_of((1, inner)),
        ],
        proj, taps, lags, bias_row, alog_row, skip_row, conv, cum, steps, d_y, entering, leaving,
        flops=3 * scan_flops,
        scratch=[
            pltpu.VMEM((block_rows, inner + 2 * state), f32),
            pltpu.VMEM((LANES, block_rows), f32),
            pltpu.VMEM((block_rows + EDGE, inner + 2 * state), f32),
        ],
    )
    ffn_chunks = scatter_fold(here, after(d_dt, ffn_rings), ffn_plan, shard)
    tail = after(ffn_chunks, from_behind(tail, "dp", -1))
    ffn_sent, ffn_terms = ring_send(after(tail, ffn_chunks), "yx")
    bc_half = (2 * quarter, 2 * state)
    bc_mine, bc_theirs = kernel_call(
        bc_split(quarter, inner),
        [shape_of(bc_half)] * 2,
        here, d_bc, tail,
        small=(0,),
        scratch=[pltpu.VMEM((block_rows, 2 * state), f32)],
    )
    bc_shape = (quarter, 2 * state)
    bc_sum, bc_sent = kernel_call(
        add_split(quarter), [shape_of(bc_shape)] * 2, here, bc_mine, other(bc_theirs, 1), small=(0,)
    )
    d_all, din_mine, din_theirs, grad_norm = kernel_call(
        input_back(quarter, inner, state),
        [
            shape_of((block_rows, 2 * inner + LANES), bf16),
            shape_of(half_shape),
            shape_of(half_shape, bf16),
            shape_of((1, model_dim)),
        ],
        here, d_z, d_x, tail, d_dt, win, rows_all,
        flops=2 * block_rows * model_dim * in_columns,
        small=(0,),
        scratch=[pltpu.VMEM((block_rows, model_dim), f32)],
    )
    bc_own, din_bc, norm_bc = kernel_call(
        bc_back(2 * inner, state),
        [shape_of(bc_shape, bf16), shape_of((quarter, model_dim)), shape_of((1, model_dim))],
        bc_sum, other(bc_sent, 2), tokens, win,
        raw=(3,),
        scratch=[pltpu.VMEM((model_dim, 2 * state), bf16), pltpu.SemaphoreType.DMA],
    )
    din_own, din_sent = kernel_call(
        add_split(quarter),
        [shape_of((quarter, model_dim)), shape_of((quarter, model_dim), bf16)],
        here, din_mine, other(din_theirs, 1),
        small=(0,),
    )
    grad_tokens = kernel_call(
        input_grad(quarter),
        [shape_of((quarter, model_dim))],
        here, din_own, other(din_sent, 2), din_bc, tokens, d_middle, norm_gain[None, :],
        small=(0,),
    )[0]

    dt_at = 2 * inner
    bc_at = dt_at + LANES
    out_at = bc_at + 2 * state
    mix_split = (out_at + inner) // 256 * LANES
    mix_plan = (
        ((0, 2, 0, mix_split),),
        ((0, 2, mix_split, bc_at), (4, 5, 0, 2 * state), (1, 3, 0, inner)),
    )
    mix_arrays = (normed_in, d_proj, d_all, mixer_in, normed_own, bc_own)
    mix_arrays = after(ffn_sent, (normed_in, d_proj, d_all, mixer_in, normed_own, bc_own))
    mix_chunks = scatter_begin(here, mix_plan, mix_arrays, shard)
    mix_sent, mix_terms = ring_send(mix_chunks, "xy")
    layout = small_rows(model_dim, inner, state, conv_taps, tensor_count)
    table_shape = shape_of((dp_count, SUB, LANES))
    table = kernel_call(
        small_table(layout, inner, state, conv_taps, heads),
        [table_shape],
        here, after(mix_chunks, grad_norm), norm_bc, grad_post_gain, grad_taps, grad_gain, grad_heads, grad_skip,
        small=(0,),
        scratch=[pltpu.VMEM((dp_count * EACH, LANES), f32)],
    )[0]
    table = lax.all_to_all(table, "dp", 0, 0, tiled=True)
    mix_rings = ring_pass(mix_sent, mix_terms, mix_plan, "xy", 4 * shard, table)
    devices = dp_count * tensor_count
    table = kernel_call(small_sum(), [shape_of((devices, SUB, LANES))], after(mix_rings[1], table))[0]
    table = lax.all_to_all(table, ("dp", "tensor"), 0, 0, tiled=True)
    mix_rings = after(table, mix_rings)
    small = kernel_call(
        small_out(layout, tensor_count, inner, state, conv_taps),
        [
            shape_of((1, model_dim)),
            shape_of((1, model_dim)),
            shape_of((conv_taps, inner_total)),
            shape_of((conv_taps, 2 * state)),
            shape_of((1, inner_total)),
            shape_of((1, inner_total)),
            shape_of((2 * tensor_count, LANES)),
        ],
        table,
        scratch=[pltpu.VMEM((dp_count * EACH, LANES), f32)],
    )
    norm_sum, post_sum, taps_x, taps_bc, gain_sum, skip_sum, head_sums = small
    head_sums = head_sums.reshape(2, tensor_count, LANES)[:, :, :heads].reshape(2, -1)
    ffn_rings = ring_pass(ffn_sent, ffn_terms, ffn_plan, "yx", shard, mix_chunks)
    grad_ffn = scatter_last(here, ffn_rings, ffn_plan, shard)
    mix_chunks_last = scatter_fold(here, mix_rings, mix_plan, shard)
    mix_sent, mix_terms = ring_send(mix_chunks_last, "yx")
    mix_rings_last = ring_pass(mix_sent, mix_terms, mix_plan, "yx", shard)
    grad_mix = scatter_last(here, mix_rings_last, mix_plan, shard)
    grad_bc = grad_mix[:, bc_at:out_at]
    grad_bc = grad_bc + other(grad_bc, 1)
    grad_bc = grad_bc + other(grad_bc, 2)
    def experts_of(columns):
        return columns.reshape(shard, experts, ffe)

    wide_e = experts * ffe
    g_gate, g_up, g_down = (
        grad_ffn[:, :hidden],
        grad_ffn[:, hidden : 2 * hidden],
        grad_ffn[:, 2 * hidden :],
    )
    return (
        block_out,
        grad_tokens,
        norm_sum[0],
        grad_mix[:, : 2 * inner].reshape(shard, 2, inner),
        grad_bc.reshape(shard, 2, state),
        grad_mix[:, dt_at : dt_at + heads],
        taps_x,
        taps_bc.reshape(conv_taps, 2, state),
        head_sums[0],
        head_sums[1],
        jnp.sum(skip_sum.reshape(head_total, head_dim), 1),
        gain_sum[0],
        grad_mix[:, out_at:].T,
        post_sum[0],
        experts_of(g_gate[:, :wide_e]).transpose(1, 0, 2),
        experts_of(g_up[:, :wide_e]).transpose(1, 0, 2),
        experts_of(g_down[:, :wide_e]).transpose(1, 2, 0),
        g_gate[:, wide_e:],
        g_up[:, wide_e:],
        g_down[:, wide_e:].T,
    )


def solution(mesh):
    in_specs = (
        P(("dp", "tensor"), None),
        P(("dp", "tensor"), None),
        P("dp"),
        P("dp", None),
        P("dp", None),
        P(),
        P("dp", None, "tensor"),
        P("dp", None, None),
        P("dp", "tensor"),
        P(),
        P(),
        P(),
        P(),
        P(),
        P(),
        P("tensor", "dp"),
        P(),
        P(None, "dp", "tensor"),
        P(None, "dp", "tensor"),
        P(None, "tensor", "dp"),
        P("dp", "tensor"),
        P("dp", "tensor"),
        P("tensor", "dp"),
    )
    out_specs = (
        P(("dp", "tensor"), None),
        P(("dp", "tensor"), None),
        P(),
        P("dp", None, "tensor"),
        P("dp", None, None),
        P("dp", "tensor"),
        P(),
        P(),
        P(),
        P(),
        P(),
        P(),
        P("tensor", "dp"),
        P(),
        P(None, "dp", "tensor"),
        P(None, "dp", "tensor"),
        P(None, "tensor", "dp"),
        P("dp", "tensor"),
        P("dp", "tensor"),
        P("tensor", "dp"),
    )
    return jax.shard_map(body, mesh=mesh, in_specs=in_specs, out_specs=out_specs, check_vma=False)
```

time: 4250 us -> 508 us (0.12)
  waiting for transfers between devices: 2760 us -> 110 us
  blocking collectives: 961 us -> 31.4 us
  starting transfers between devices: 10.2 us -> 164 us
  matrix products: 147 us -> 0 us
  other arithmetic: 134 us -> 7.15 us
  local copies, waits for them, and re-layouts: 200 us -> 87.8 us
  Pallas kernels: 0 us -> 98.4 us
    reduce_scatter x11 -> x0, waiting for transfers between devices: 1260 us -> none  [the longest x1 176 us: body(): lax.psum_scatter(grad_ed, 'dp', scatter_dimension=2, tiled=True)]
    all_gather x14 -> x0, blocking collectives: 822 us -> none  [the longest x2 156 us: fetch_weights(): lax.all_gather(sh_down, 'dp', axis=1, tiled=True)]
    all_gather x12 -> x0, waiting for transfers between devices: 750 us -> none  [the longest x2 259 us: carried_in(): everything = jax.tree.map(lambda part: lax.all_gather(part, axis), shard)]
    unnamed x29 -> x0, waiting for transfers between devices: 412 us -> none
    psum x2 -> x0, waiting for transfers between devices: 340 us -> none  [body(): lax.psum((grad_norm, grad_post_gain, grad_bc, place_slice(grad_conv[:, :i...]
    dot_general x45 -> x0, matrix products: 145 us -> none  [the longest x3 16.2 us: block_step(): y_blk = jnp.einsum('ijh,jhp->ihp', weights, x_blk, precision=highest)]
    unnamed x3 -> x0, blocking collectives: 139 us -> none
    ppermute x0 -> x77, starting transfers between devices: none -> 138 us  [the longest x60 82.3 us: shift(): return lax.ppermute(value, 'dp', pairs)]
  transfers between devices with their start and end apart: 30 -> 84, of which waited for: 23 -> 28; matrix products, arithmetic and copies ran while one was open for 9% -> 7% of each run, Pallas kernels for 0% -> 9%
where the time goes in v1:
time: 508 us; the launch traced here: 502 us
  starting transfers between devices  164 us (32%)
  waiting for transfers between devices  110 us (22%)
  Pallas kernels  98.4 us (19%)
  local copies, waits for them, and re-layouts  87.8 us (17%)
  blocking collectives  31.4 us (6%)
  other arithmetic  7.15 us (1%)
    pallas_call x33, Pallas kernels, kernel_call(): pl.pallas_call(kernel, out_shape=out_shapes, in_specs=[pl.BlockSpec(memor...  98.4 us
    ppermute x60, starting transfers between devices, shift(): return lax.ppermute(value, 'dp', pairs)  82.3 us
    unnamed x322, local copies, waits for them, and re-layouts  66.2 us
    ppermute x60, waiting for transfers between devices, shift(): return lax.ppermute(value, 'dp', pairs)  66 us
    ppermute x17, starting transfers between devices, other(): lax.ppermute(value, 'tensor', [(rank, rank ^ bit) for rank in range(count)])  56 us
    ppermute x17, waiting for transfers between devices, other(): lax.ppermute(value, 'tensor', [(rank, rank ^ bit) for rank in range(count)])  29.3 us
    all_to_all x1, blocking collectives, exchange_states(): back = lax.all_to_all(carried, axis, 0, 0, tiled=True)  17.1 us
    all_to_all x1, blocking collectives, exchange_states(): parts = after(wait, lax.all_to_all(sent, axis, 0, 0, tiled=True))  14.3 us
  transfers between devices with their start and end apart: 84, of which 28 were waited for; matrix products, arithmetic and copies ran while one was open for 7% of the time, Pallas kernels for 9%

profile of v1, /device:TPU:1, one launch (start us, length us, event | category | flops | bytes accessed | tf_op | source)
XLA Modules:
  0.0 501.8 jit_solution(12132616438629382355)
XLA Ops:
  2.8 4.5 collective-permute-start
  18.0 4.1 collective-permute-done.5
  22.1 7.9 %collective-permute-done.6 = bf16[48,3840]{1,0:T(8,128)(2,1)S(1)} collective-permute-done((bf16[48,3840]{1,0:T(8,128)(2,1)}, bf16[48,3840]{1,0:T(8,128)(2,1)S(1)}, u32[]{:S(2)}, u32[]{:S(2)}) %collective-permute-start.6) | collective-permute-done | bytes 368672 | tf_op jit(solution)/shard_map/ppermute | solution.py:697
  51.1 3.2 collective-permute-done.14
  69.3 12.1 %collective-permute-done.11.refs_1_ = bf16[8,48,1280]{2,1,0:T(8,128)(2,1)S(1)} collective-permute-done((bf16[8,48,1280]{2,1,0:T(8,128)(2,1)S(1)}, bf16[8,48,1280]{2,1,0:T(8,128)(2,1)S(1)}, u32[]{:S(2)}, u32[]{:S(2)}) %collective-permute-start.11) | collective-permute-done | bytes 983072 | tf_op jit(solution)/shard_map/ppermute | solution.py:697
  95.9 5.6 %collective-permute-done.19.refs_3_ = bf16[4,48,1280]{2,1,0:T(8,128)(2,1)S(1)} collective-permute-done((bf16[4,48,1280]{2,1,0:T(8,128)(2,1)S(1)}, bf16[4,48,1280]{2,1,0:T(8,128)(2,1)S(1)}, u32[]{:S(2)}, u32[]{:S(2)}) %collective-permute-start.19) | collective-permute-done | bytes 491552 | tf_op jit(solution)/shard_map/ppermute | solution.py:697
  112.3 13.4 %shard_map.375 = (bf16[1536,1920]{1,0:T(8,128)(2,1)}, f32[272,1920]{1,0:T(8,128)}, f32[256,768]{1,0:T(8,128)S(1)}, f32[256,1024]{1,0:T(8,128)}, f32[256,128]{1,0...) custom-call(s32[5]{0:T(128)S(1)} %stack.61.here, bf16[256,1536]{1,0:T(8,128)(2,1)S(1)} %copy-done.44, ...), custom_call_target="tpu_custom_call" | custom-call | flops 1711276032 | bytes 19869716 | tf_op jit(solution)/shard_map/pallas_call | solution.py:65
  125.8 14.3 %all_to_all.30.parts = f32[32,32,128]{2,1,0:T(8,128)S(1)} all-to-all(f32[32,32,128]{2,1,0:T(8,128)S(1)} %get-tuple-element.240), channel_id=1, replica_groups=mesh['dp'=32,'tensor'=4] {'dp'}, dimensions={0} | all-to-all | bytes 1048576 | tf_op jit(solution)/shard_map/all_to_all | solution.py:664
  154.7 3.9 all-to-all-start.1
  159.3 8.2 %all-to-all-done.1 = f32[32,24,128]{2,1,0:T(8,128)S(1)} async-done(((f32[32,24,128]{2,1,0:T(8,128)}), f32[32,24,128]{2,1,0:T(8,128)S(1)}, u32[]{:S(2)}, u32[]{:S(2)}) %all-to-all-start.1) | async-done | bytes 393248 | tf_op jit(solution)/shard_map/all_to_all | solution.py:668
  168.8 6.9 %shard_map.377 = (bf16[1536,768]{1,0:T(8,128)(2,1)}, f32[256,768]{1,0:T(8,128)S(1)}, bf16[256,768]{1,0:T(8,128)(2,1)S(1)}, f32[128,1664]{1,0:T(8,128)S(1)}, f32[128,1664]{1,0:T(8,128)}) custom-call(s32[5]{0:T(128)S(1)} %stack.61.here, f32[256,768]{1,0:T(8,128)S(1)} %copy-done.47, f32[272,1920]{1,0:T(8,128)} %get-tuple-element.235.proj, ...), custom_call_target="tpu_custom_call" | custom-call | flops 201326592 | bytes 17951764 | tf_op jit(solution)/shard_map/pallas_call | solution.py:65
  175.8 9.1 %collective-permute-start.31 = (f32[128,1664]{1,0:T(8,128)}, f32[128,1664]{1,0:T(8,128)S(1)}, u32[]{:S(2)}, u32[]{:S(2)}) collective-permute-start(f32[128,1664]{1,0:T(8,128)} %get-tuple-element.250), channel_id=1, source_target_pairs={{0,1},{1,0},{2,3},{3,2},{4,5},{5,4},{6,7},{7,6},{8,9},{9,8},{10,11... | collective-permute-start | bytes 2555912 | tf_op jit(solution)/shard_map/ppermute | solution.py:674
  188.3 11.6 %collective-permute-done.32.got.pair_sent = bf16[128,1664]{1,0:T(8,128)(2,1)S(1)} collective-permute-done((bf16[128,1664]{1,0:T(8,128)(2,1)S(1)}, bf16[128,1664]{1,0:T(8,128)(2,1)S(1)}, u32[]{:S(2)}, u32[]{:S(2)}) %collective-permute-start.32) | collective-permute-done | bytes 426016 | tf_op jit(solution)/shard_map/ppermute | solution.py:674
  200.9 10.0 %collective-permute-start.33 = (bf16[128,1536]{1,0:T(8,128)(2,1)S(1)}, bf16[128,1536]{1,0:T(8,128)(2,1)S(1)}, u32[]{:S(2)}, u32[]{:S(2)}) collective-permute-start(bf16[128,1536]{1,0:T(8,128)(2,1)S(1)} %get-tuple-element.252.post_mine), channel_id=1, source_target_pairs={{0,1},{1,0},{2,3},{3,2},{4,5},{5,4},{6,7},{7,6},{8,9},{9,8},{10,11... | collective-permute-start | bytes 1179656 | tf_op jit(solution)/shard_map/ppermute | solution.py:674
  212.3 14.0 %shard_map.380 = (bf16[256,1536]{1,0:T(8,128)(2,1)}, bf16[256,1536]{1,0:T(8,128)(2,1)}, bf16[256,1280]{1,0:T(8,128)(2,1)S(1)}, bf16[256,2560]{1,0:T(8,128)(2,1)}...) custom-call(s32[5]{0:T(128)S(1)} %stack.61.here, ...), custom_call_target="tpu_custom_call" | custom-call | flops 6039797760 | bytes 20185108 | tf_op jit(solution)/shard_map/pallas_call | solution.py:65
  229.9 8.0 %shard_map.383 = (bf16[384,1920]{1,0:T(8,128)(2,1)S(1)}, bf16[384,1920]{1,0:T(8,128)(2,1)}, bf16[384,1920]{1,0:T(8,128)(2,1)}, bf16[192,1920]{1,0:T(8,128)(2,1)S...) custom-call(s32[5]{0:T(128)S(1)} %stack.61.here, ...), custom_call_target="tpu_custom_call" | custom-call | flops 3019898880 | bytes 15335444 | tf_op jit(solution)/shard_map/pallas_call | solution.py:65
  245.9 10.5 %collective-permute-done.37.got = bf16[128,1536]{1,0:T(8,128)(2,1)S(1)} collective-permute-done((bf16[128,1536]{1,0:T(8,128)(2,1)S(1)}, bf16[128,1536]{1,0:T(8,128)(2,1)S(1)}, u32[]{:S(2)}, u32[]{:S(2)}) %collective-permute-start.37) | collective-permute-done | bytes 393248 | tf_op jit(solution)/shard_map/ppermute | solution.py:674
  269.0 4.6 all-to-all-start.2
  277.4 6.5 %all-to-all-done.2.parts = f32[32,32,128]{2,1,0:T(8,128)} async-done(((f32[32,32,128]{2,1,0:T(8,128)}), f32[32,32,128]{2,1,0:T(8,128)}, u32[]{:S(2)}, u32[]{:S(2)}) %all-to-all-start.2) | async-done | bytes 524320 | tf_op jit(solution)/shard_map/all_to_all | solution.py:664
  289.8 3.5 shard_map.388
  298.7 17.1 %all_to_all.31 = f32[32,24,128]{2,1,0:T(8,128)S(1)} all-to-all(f32[32,24,128]{2,1,0:T(8,128)S(1)} %shard_map.387), channel_id=1, replica_groups=mesh['dp'=32,'tensor'=4] {'dp'}, dimensions={0} | all-to-all | bytes 786432 | tf_op jit(solution)/shard_map/all_to_all | solution.py:668
  316.0 10.4 %shard_map.389 = (f32[256,768]{1,0:T(8,128)S(1)}, f32[256,256]{1,0:T(8,128)S(1)}, f32[16,1024]{1,0:T(8,128)S(1)}, bf16[256,128]{1,0:T(8,128)(2,1)S(1)}, f32[8,10...) custom-call(f32[272,1920]{1,0:T(8,128)S(1)} %copy-done.2, f32[8,1024]{1,0:T(8,128)S(1)} %copy-done.95, ...), custom_call_target="tpu_custom_call" | custom-call | flops 603979776 | bytes 6360064 | tf_op jit(solution)/shard_map/pallas_call | solution.py:65
  327.8 4.9 shard_map.390
  335.7 3.8 collective-permute-start.54
  340.7 6.5 %collective-permute-start.50 = (f32[128,256]{1,0:T(8,128)S(1)}, f32[128,256]{1,0:T(8,128)S(1)}, u32[]{:S(2)}, u32[]{:S(2)}) collective-permute-start(f32[128,256]{1,0:T(8,128)S(1)} %get-tuple-element.330), channel_id=1, source_target_pairs={{0,1},{1,0},{2,3},{3,2},{4,5},{5,4},{6,7},{7,6},{8,9},{9,8},{10,11... | collective-permute-start | bytes 393224 | tf_op jit(solution)/shard_map/ppermute | solution.py:674
  357.9 5.9 %shard_map.397 = (bf16[384,1280]{1,0:T(8,128)(2,1)S(1)}, bf16[384,1280]{1,0:T(8,128)(2,1)S(1)}, bf16[384,1280]{1,0:T(8,128)(2,1)}, bf16[192,1280]{1,0:T(8,128)(2...) custom-call(s32[5]{0:T(128)S(1)} %stack.61.here, ...), custom_call_target="tpu_custom_call" | custom-call | flops 2113929216 | bytes 11304980 | tf_op jit(solution)/shard_map/pallas_call | solution.py:65
  377.0 14.9 %collective-permute-done.56.refs_0_.refs_1_ = bf16[384,1280]{1,0:T(8,128)(2,1)S(1)} collective-permute-done((bf16[384,1280]{1,0:T(8,128)(2,1)S(1)}, bf16[384,1280]{1,0:T(8,128)(2,1)S(1)}, u32[]{:S(2)}, u32[]{:S(2)}) %collective-permute-start.56) | collective-permute-done | bytes 983072 | tf_op jit(solution)/shard_map/ppermute | solution.py:697
  395.6 4.2 all-to-all-start.4
  425.1 9.0 %all-to-all-start.5 = ((f32[128,8,128]{2,1,0:T(8,128)}), f32[128,8,128]{2,1,0:T(8,128)}, u32[]{:S(2)}, u32[]{:S(2)}) async-start(f32[128,8,128]{2,1,0:T(8,128)} %copy-done.12), calls=%async_computation.5 | async-start | bytes 1048576 | tf_op jit(solution)/shard_map/all_to_all | solution.py:1340
  444.8 3.1 collective-permute-start.35
  456.1 3.3 shard_map.402
  483.4 7.7 %collective-permute-start.73 = (f32[48,256]{1,0:T(8,128)S(1)}, f32[48,256]{1,0:T(8,128)S(1)}, u32[]{:S(2)}, u32[]{:S(2)}) collective-permute-start(f32[48,256]{1,0:T(8,128)S(1)} %slice.287), channel_id=1, source_target_pairs={{0,1},{1,0},{2,3},{3,2},{4,5},{5,4},{6,7},{7,6},{8,9},{9,8},{10,11... | collective-permute-start | bytes 147464 | tf_op jit(solution)/shard_map/ppermute | solution.py:674
  (580 shorter events, 246.5 us)
Async XLA Ops:
  2.8 31.6 %collective-permute-start = (bf16[128,1536]{1,0:T(8,128)(2,1)S(1)}, bf16[128,1536]{1,0:T(8,128)(2,1)S(1)}, u32[]{:S(2)}, u32[]{:S(2)}) collective-permute-start(bf16[128,1536]{1,0:T(8,128)(2,1)S(1)} %constant_dynamic-update-slice_fusion.own), channel_id=1, source_target_pairs={{0,2},{1,3},{2,0},{3,1},{4,6},{5,7},{6,4},{7,5},{8,10},{9,11},{10,... | collective-permute-start | bytes 1179656 | tf_op jit(solution)/shard_map/ppermute | solution.py:674
  7.3 31.0 %collective-permute-start.1 = (bf16[128,1536]{1,0:T(8,128)(2,1)S(1)}, bf16[128,1536]{1,0:T(8,128)(2,1)S(1)}, u32[]{:S(2)}, u32[]{:S(2)}) collective-permute-start(bf16[128,1536]{1,0:T(8,128)(2,1)S(1)} %constant_dynamic-update-slice_fusion.own), channel_id=1, source_target_pairs={{0,1},{1,0},{2,3},{3,2},{4,5},{5,4},{6,7},{7,6},{8,9},{9,8},{10,11... | collective-permute-start | bytes 1179656 | tf_op jit(solution)/shard_map/ppermute | solution.py:674
  41.4 26.7 %collective-permute-start.3 = (bf16[16,1536]{1,0:T(8,128)(2,1)S(1)}, bf16[16,1536]{1,0:T(8,128)(2,1)S(1)}, u32[]{:S(2)}, u32[]{:S(2)}) collective-permute-start(bf16[16,1536]{1,0:T(8,128)(2,1)S(1)} %slice.195), channel_id=1, source_target_pairs={{0,4},{4,8},{8,12},{12,16},{16,20},{20,24},{24,28},{28,32},{32,36}... | collective-permute-start | bytes 147464 | tf_op jit(solution)/shard_map/ppermute | solution.py:53
  57.9 23.4 %collective-permute-start.11 = (bf16[8,48,1280]{2,1,0:T(8,128)(2,1)S(1)}, bf16[8,48,1280]{2,1,0:T(8,128)(2,1)S(1)}, u32[]{:S(2)}, u32[]{:S(2)}) collective-permute-start(bf16[8,48,1280]{2,1,0:T(8,128)(2,1)S(1)} %slice_dynamic-update-slice_fusion.14.refs_0_), channel_id=1, source_target_pairs={{0,32},{4,36},{8,40},{12,44},{16,48},{20,52},{24,56},{28,60},{32,6... | collective-permute-start | bytes 2949128 | tf_op jit(solution)/shard_map/ppermute | solution.py:697
  58.0 26.2 %collective-permute-start.12 = (bf16[8,48,1280]{2,1,0:T(8,128)(2,1)S(1)}, bf16[8,48,1280]{2,1,0:T(8,128)(2,1)S(1)}, u32[]{:S(2)}, u32[]{:S(2)}) collective-permute-start(bf16[8,48,1280]{2,1,0:T(8,128)(2,1)S(1)} %slice_dynamic-update-slice_fusion.14.refs_0_), channel_id=1, source_target_pairs={{0,96},{4,100},{8,104},{12,108},{16,112},{20,116},{24,120},{28,124... | collective-permute-start | bytes 2949128 | tf_op jit(solution)/shard_map/ppermute | solution.py:697
  63.2 23.7 %collective-permute-start.17 = (bf16[8,48,1408]{2,1,0:T(8,128)(2,1)S(1)}, bf16[8,48,1408]{2,1,0:T(8,128)(2,1)S(1)}, u32[]{:S(2)}, u32[]{:S(2)}) collective-permute-start(bf16[8,48,1408]{2,1,0:T(8,128)(2,1)S(1)} %slice_dynamic-update-slice_fusion.12.refs_5_), channel_id=1, source_target_pairs={{0,4},{4,8},{8,12},{12,0},{16,20},{20,24},{24,28},{28,16},{32,36},... | collective-permute-start | bytes 3244040 | tf_op jit(solution)/shard_map/ppermute | solution.py:697
  63.3 23.5 %collective-permute-start.18 = (bf16[8,48,1408]{2,1,0:T(8,128)(2,1)S(1)}, bf16[8,48,1408]{2,1,0:T(8,128)(2,1)S(1)}, u32[]{:S(2)}, u32[]{:S(2)}) collective-permute-start(bf16[8,48,1408]{2,1,0:T(8,128)(2,1)S(1)} %slice_dynamic-update-slice_fusion.12.refs_5_), channel_id=1, source_target_pairs={{0,12},{4,0},{8,4},{12,8},{16,28},{20,16},{24,20},{28,24},{32,44},... | collective-permute-start | bytes 3244040 | tf_op jit(solution)/shard_map/ppermute | solution.py:697
  68.0 40.8 %collective-permute-start.4 = (f32[16]{0:T(128)}, f32[16]{0:T(128)S(1)}, u32[]{:S(2)}, u32[]{:S(2)}) collective-permute-start(f32[16]{0:T(128)} %slice.196), channel_id=1, source_target_pairs={{0,4},{4,8},{8,12},{12,16},{16,20},{20,24},{24,28},{28,32},{32,36}... | collective-permute-start | bytes 200 | tf_op jit(solution)/shard_map/ppermute | solution.py:53
  102.2 37.8 %collective-permute-start.23 = (bf16[8,48,1920]{2,1,0:T(8,128)(2,1)}, bf16[8,48,1920]{2,1,0:T(8,128)(2,1)}, u32[]{:S(2)}, u32[]{:S(2)}) collective-permute-start(bf16[8,48,1920]{2,1,0:T(8,128)(2,1)} %slice_dynamic-update-slice_fusion.10.refs_0_), channel_id=1, source_target_pairs={{0,32},{4,36},{8,40},{12,44},{16,48},{20,52},{24,56},{28,60},{32,6... | collective-permute-start | bytes 4423688 | tf_op jit(solution)/shard_map/ppermute | solution.py:697
  102.9 37.1 %collective-permute-start.24 = (bf16[8,48,1920]{2,1,0:T(8,128)(2,1)}, bf16[8,48,1920]{2,1,0:T(8,128)(2,1)}, u32[]{:S(2)}, u32[]{:S(2)}) collective-permute-start(bf16[8,48,1920]{2,1,0:T(8,128)(2,1)} %slice_dynamic-update-slice_fusion.10.refs_0_), channel_id=1, source_target_pairs={{0,96},{4,100},{8,104},{12,108},{16,112},{20,116},{24,120},{28,124... | collective-permute-start | bytes 4423688 | tf_op jit(solution)/shard_map/ppermute | solution.py:697
  104.9 35.2 %collective-permute-start.25 = (bf16[8,48,1920]{2,1,0:T(8,128)(2,1)}, bf16[8,48,1920]{2,1,0:T(8,128)(2,1)}, u32[]{:S(2)}, u32[]{:S(2)}) collective-permute-start(bf16[8,48,1920]{2,1,0:T(8,128)(2,1)} %slice_dynamic-update-slice_fusion.8.refs_5_), channel_id=1, source_target_pairs={{0,4},{4,8},{8,12},{12,0},{16,20},{20,24},{24,28},{28,16},{32,36},... | collective-permute-start | bytes 4423688 | tf_op jit(solution)/shard_map/ppermute | solution.py:697
  104.9 35.2 %collective-permute-start.26 = (bf16[8,48,1920]{2,1,0:T(8,128)(2,1)}, bf16[8,48,1920]{2,1,0:T(8,128)(2,1)}, u32[]{:S(2)}, u32[]{:S(2)}) collective-permute-start(bf16[8,48,1920]{2,1,0:T(8,128)(2,1)} %slice_dynamic-update-slice_fusion.8.refs_5_), channel_id=1, source_target_pairs={{0,12},{4,0},{8,4},{12,8},{16,28},{20,16},{24,20},{28,24},{32,44},... | collective-permute-start | bytes 4423688 | tf_op jit(solution)/shard_map/ppermute | solution.py:697
  143.2 24.4 %collective-permute-start.27 = (bf16[4,48,1920]{2,1,0:T(8,128)(2,1)}, bf16[4,48,1920]{2,1,0:T(8,128)(2,1)}, u32[]{:S(2)}, u32[]{:S(2)}) collective-permute-start(bf16[4,48,1920]{2,1,0:T(8,128)(2,1)} %slice.236), channel_id=1, source_target_pairs={{0,32},{4,36},{8,40},{12,44},{16,48},{20,52},{24,56},{28,60},{32,6... | collective-permute-start | bytes 2211848 | tf_op jit(solution)/shard_map/ppermute | solution.py:697
  145.6 22.0 %collective-permute-start.28 = (bf16[4,48,1920]{2,1,0:T(8,128)(2,1)}, bf16[4,48,1920]{2,1,0:T(8,128)(2,1)}, u32[]{:S(2)}, u32[]{:S(2)}) collective-permute-start(bf16[4,48,1920]{2,1,0:T(8,128)(2,1)} %slice.237), channel_id=1, source_target_pairs={{0,96},{4,100},{8,104},{12,108},{16,112},{20,116},{24,120},{28,124... | collective-permute-start | bytes 2211848 | tf_op jit(solution)/shard_map/ppermute | solution.py:697
  239.3 35.6 %collective-permute-start.39 = (bf16[384,1920]{1,0:T(8,128)(2,1)}, bf16[384,1920]{1,0:T(8,128)(2,1)}, u32[]{:S(2)}, u32[]{:S(2)}) collective-permute-start(bf16[384,1920]{1,0:T(8,128)(2,1)} %get-tuple-element.264), channel_id=1, source_target_pairs={{0,32},{4,36},{8,40},{12,44},{16,48},{20,52},{24,56},{28,60},{32,6... | collective-permute-start | bytes 4423688 | tf_op jit(solution)/shard_map/ppermute | solution.py:697
  239.7 35.1 %collective-permute-start.40 = (bf16[384,1920]{1,0:T(8,128)(2,1)}, bf16[384,1920]{1,0:T(8,128)(2,1)}, u32[]{:S(2)}, u32[]{:S(2)}) collective-permute-start(bf16[384,1920]{1,0:T(8,128)(2,1)} %get-tuple-element.265), channel_id=1, source_target_pairs={{0,96},{4,100},{8,104},{12,108},{16,112},{20,116},{24,120},{28,124... | collective-permute-start | bytes 4423688 | tf_op jit(solution)/shard_map/ppermute | solution.py:697
  242.1 35.2 %collective-permute-start.41 = (bf16[384,1920]{1,0:T(8,128)(2,1)}, bf16[384,1920]{1,0:T(8,128)(2,1)}, u32[]{:S(2)}, u32[]{:S(2)}) collective-permute-start(bf16[384,1920]{1,0:T(8,128)(2,1)} %get-tuple-element.269), channel_id=1, source_target_pairs={{0,4},{4,8},{8,12},{12,0},{16,20},{20,24},{24,28},{28,16},{32,36},... | collective-permute-start | bytes 4423688 | tf_op jit(solution)/shard_map/ppermute | solution.py:697
  243.9 33.5 %collective-permute-start.42 = (bf16[384,1920]{1,0:T(8,128)(2,1)}, bf16[384,1920]{1,0:T(8,128)(2,1)}, u32[]{:S(2)}, u32[]{:S(2)}) collective-permute-start(bf16[384,1920]{1,0:T(8,128)(2,1)} %get-tuple-element.270), channel_id=1, source_target_pairs={{0,12},{4,0},{8,4},{12,8},{16,28},{20,16},{24,20},{28,24},{32,44},... | collective-permute-start | bytes 4423688 | tf_op jit(solution)/shard_map/ppermute | solution.py:697
  293.3 22.6 %collective-permute-start.43 = (bf16[192,1920]{1,0:T(8,128)(2,1)S(1)}, bf16[192,1920]{1,0:T(8,128)(2,1)S(1)}, u32[]{:S(2)}, u32[]{:S(2)}) collective-permute-start(bf16[192,1920]{1,0:T(8,128)(2,1)S(1)} %get-tuple-element.293), channel_id=1, source_target_pairs={{0,32},{4,36},{8,40},{12,44},{16,48},{20,52},{24,56},{28,60},{32,6... | collective-permute-start | bytes 2211848 | tf_op jit(solution)/shard_map/ppermute | solution.py:697
  293.6 22.2 %collective-permute-start.44 = (bf16[192,1920]{1,0:T(8,128)(2,1)S(1)}, bf16[192,1920]{1,0:T(8,128)(2,1)S(1)}, u32[]{:S(2)}, u32[]{:S(2)}) collective-permute-start(bf16[192,1920]{1,0:T(8,128)(2,1)S(1)} %get-tuple-element.294), channel_id=1, source_target_pairs={{0,96},{4,100},{8,104},{12,108},{16,112},{20,116},{24,120},{28,124... | collective-permute-start | bytes 2211848 | tf_op jit(solution)/shard_map/ppermute | solution.py:697
  332.8 22.1 %collective-permute-start.52 = (bf16[96,1920]{1,0:T(8,128)(2,1)S(1)}, bf16[96,1920]{1,0:T(8,128)(2,1)S(1)}, u32[]{:S(2)}, u32[]{:S(2)}) collective-permute-start(bf16[96,1920]{1,0:T(8,128)(2,1)S(1)} %get-tuple-element.335), channel_id=1, source_target_pairs={{0,4},{4,8},{8,12},{12,0},{16,20},{20,24},{24,28},{28,16},{32,36},... | collective-permute-start | bytes 1105928 | tf_op jit(solution)/shard_map/ppermute | solution.py:697
  369.0 22.9 %collective-permute-start.56 = (bf16[384,1280]{1,0:T(8,128)(2,1)S(1)}, bf16[384,1280]{1,0:T(8,128)(2,1)S(1)}, u32[]{:S(2)}, u32[]{:S(2)}) collective-permute-start(bf16[384,1280]{1,0:T(8,128)(2,1)S(1)} %get-tuple-element.350), channel_id=1, source_target_pairs={{0,32},{4,36},{8,40},{12,44},{16,48},{20,52},{24,56},{28,60},{32,6... | collective-permute-start | bytes 2949128 | tf_op jit(solution)/shard_map/ppermute | solution.py:697
  370.7 39.5 %collective-permute-start.58 = (bf16[384,1408]{1,0:T(8,128)(2,1)}, bf16[384,1408]{1,0:T(8,128)(2,1)S(1)}, u32[]{:S(2)}, u32[]{:S(2)}) collective-permute-start(bf16[384,1408]{1,0:T(8,128)(2,1)} %get-tuple-element.356), channel_id=1, source_target_pairs={{0,4},{4,8},{8,12},{12,0},{16,20},{20,24},{24,28},{28,16},{32,36},... | collective-permute-start | bytes 3244040 | tf_op jit(solution)/shard_map/ppermute | solution.py:697
  370.7 40.9 %collective-permute-start.59 = (bf16[384,1408]{1,0:T(8,128)(2,1)}, bf16[384,1408]{1,0:T(8,128)(2,1)S(1)}, u32[]{:S(2)}, u32[]{:S(2)}) collective-permute-start(bf16[384,1408]{1,0:T(8,128)(2,1)} %get-tuple-element.357), channel_id=1, source_target_pairs={{0,12},{4,0},{8,4},{12,8},{16,28},{20,16},{24,20},{28,24},{32,44},... | collective-permute-start | bytes 3244040 | tf_op jit(solution)/shard_map/ppermute | solution.py:697
  373.4 35.6 %collective-permute-start.57 = (bf16[384,1280]{1,0:T(8,128)(2,1)}, bf16[384,1280]{1,0:T(8,128)(2,1)}, u32[]{:S(2)}, u32[]{:S(2)}) collective-permute-start(bf16[384,1280]{1,0:T(8,128)(2,1)} %get-tuple-element.352), channel_id=1, source_target_pairs={{0,96},{4,100},{8,104},{12,108},{16,112},{20,116},{24,120},{28,124... | collective-permute-start | bytes 2949128 | tf_op jit(solution)/shard_map/ppermute | solution.py:697
  374.3 45.5 %collective-permute-start.34 = (bf16[128,1536]{1,0:T(8,128)(2,1)}, bf16[128,1536]{1,0:T(8,128)(2,1)}, u32[]{:S(2)}, u32[]{:S(2)}) collective-permute-start(bf16[128,1536]{1,0:T(8,128)(2,1)} %get-tuple-element.254), channel_id=1, source_target_pairs={{0,1},{1,0},{2,3},{3,2},{4,5},{5,4},{6,7},{7,6},{8,9},{9,8},{10,11... | collective-permute-start | bytes 1179656 | tf_op jit(solution)/shard_map/ppermute | solution.py:674
  391.9 29.4 %collective-permute-start.48 = (bf16[128,1536]{1,0:T(8,128)(2,1)}, bf16[128,1536]{1,0:T(8,128)(2,1)}, u32[]{:S(2)}, u32[]{:S(2)}) collective-permute-start(bf16[128,1536]{1,0:T(8,128)(2,1)} %get-tuple-element.325), channel_id=1, source_target_pairs={{0,1},{1,0},{2,3},{3,2},{4,5},{5,4},{6,7},{7,6},{8,9},{9,8},{10,11... | collective-permute-start | bytes 1179656 | tf_op jit(solution)/shard_map/ppermute | solution.py:674
  418.6 29.3 %collective-permute-start.60 = (bf16[192,1280]{1,0:T(8,128)(2,1)}, bf16[192,1280]{1,0:T(8,128)(2,1)}, u32[]{:S(2)}, u32[]{:S(2)}) collective-permute-start(bf16[192,1280]{1,0:T(8,128)(2,1)} %get-tuple-element.378), channel_id=1, source_target_pairs={{0,32},{4,36},{8,40},{12,44},{16,48},{20,52},{24,56},{28,60},{32,6... | collective-permute-start | bytes 1474568 | tf_op jit(solution)/shard_map/ppermute | solution.py:697
  419.9 33.1 %collective-permute-start.61 = (bf16[192,1280]{1,0:T(8,128)(2,1)}, bf16[192,1280]{1,0:T(8,128)(2,1)}, u32[]{:S(2)}, u32[]{:S(2)}) collective-permute-start(bf16[192,1280]{1,0:T(8,128)(2,1)} %get-tuple-element.379), channel_id=1, source_target_pairs={{0,96},{4,100},{8,104},{12,108},{16,112},{20,116},{24,120},{28,124... | collective-permute-start | bytes 1474568 | tf_op jit(solution)/shard_map/ppermute | solution.py:697
  421.3 32.3 %collective-permute-start.62 = (bf16[192,1408]{1,0:T(8,128)(2,1)}, bf16[192,1408]{1,0:T(8,128)(2,1)}, u32[]{:S(2)}, u32[]{:S(2)}) collective-permute-start(bf16[192,1408]{1,0:T(8,128)(2,1)} %get-tuple-element.380), channel_id=1, source_target_pairs={{0,4},{4,8},{8,12},{12,0},{16,20},{20,24},{24,28},{28,16},{32,36},... | collective-permute-start | bytes 1622024 | tf_op jit(solution)/shard_map/ppermute | solution.py:697
  421.5 32.1 %collective-permute-start.63 = (bf16[192,1408]{1,0:T(8,128)(2,1)}, bf16[192,1408]{1,0:T(8,128)(2,1)}, u32[]{:S(2)}, u32[]{:S(2)}) collective-permute-start(bf16[192,1408]{1,0:T(8,128)(2,1)} %get-tuple-element.381), channel_id=1, source_target_pairs={{0,12},{4,0},{8,4},{12,8},{16,28},{20,16},{24,20},{28,24},{32,44},... | collective-permute-start | bytes 1622024 | tf_op jit(solution)/shard_map/ppermute | solution.py:697
  425.1 28.5 %all-to-all-start.5 = ((f32[128,8,128]{2,1,0:T(8,128)}), f32[128,8,128]{2,1,0:T(8,128)}, u32[]{:S(2)}, u32[]{:S(2)}) async-start(f32[128,8,128]{2,1,0:T(8,128)} %copy-done.12), calls=%async_computation.5 | async-start | bytes 1048576 | tf_op jit(solution)/shard_map/all_to_all | solution.py:1340
  (201 other events, 2471.5 us)

commit v2 on v1

--- a/solution.py
+++ b/solution.py
@@ -16,7 +16,9 @@
 EDGE = 16
 SUB = 8
 RAW_LIMIT = 48 * 1024 * 1024
-VMEM_SPARE = 12 * 1024 * 1024
+WHOLE_LIMIT = 62 * 1024 * 1024
+RING_SPARE = 4 * 1024 * 1024
+VMEM_SPARE = 8 * 1024 * 1024
 
 NN = (((1,), (0,)), ((), ()))
 NT = (((1,), (1,)), ((), ()))
@@ -53,23 +55,32 @@
     return lax.ppermute(value, axis, [(source, source + steps) for source in range(leading, last)])
 
 
-def kernel_call(kernel, out_shapes, *args, flops=0, scratch=(), small=(), raw=()):
+def kernel_call(kernel, out_shapes, *args, flops=0, scratch=(), small=(), raw=(), whole=False, alone=False, wait=()):
     moved = sum(a.size * a.dtype.itemsize for a in args)
     moved += sum(s.size * s.dtype.itemsize for s in out_shapes)
     kept = [a for i, a in enumerate(args) if i not in raw and i not in small] + list(out_shapes)
     kept += [s for s in scratch if s.dtype in (f32, bf16)]
     held = sum(math.prod(a.shape) * (4 if a.dtype == f32 else 2) for a in kept)
+    limit = held + (RING_SPARE if whole else VMEM_SPARE)
+    limit = WHOLE_LIMIT if alone else max(limit, RAW_LIMIT if len(raw) > 1 else 0)
     spaces = [
         pltpu.SMEM if i in small else pl.ANY if i in raw else pltpu.VMEM for i in range(len(args))
     ]
+    wait = jax.tree.leaves(wait)
+    count = len(args)
+
+    def body_of(*refs):
+        kernel(*refs[:count], *refs[count + len(wait) :])
+
     return pl.pallas_call(
-        kernel,
+        body_of,
+        name=kernel.__qualname__.split(".")[0],
         out_shape=out_shapes,
-        in_specs=[pl.BlockSpec(memory_space=space) for space in spaces],
+        in_specs=[pl.BlockSpec(memory_space=space) for space in spaces + [pl.ANY] * len(wait)],
         scratch_shapes=scratch,
-        compiler_params=pltpu.CompilerParams(vmem_limit_bytes=max(held + VMEM_SPARE, RAW_LIMIT if len(raw) > 1 else 0)),
+        compiler_params=pltpu.CompilerParams(vmem_limit_bytes=limit),
         cost_estimate=pl.CostEstimate(flops=flops, bytes_accessed=moved, transcendentals=0),
-    )(*args)
+    )(*args, *wait)
 
 
 def shape_of(shape, dtype=f32):
@@ -94,17 +105,17 @@
     return turned, run_col, run_col[rows - 1 : rows, :], keep
 
 
-PIECES = 10
-
-
-def load_blocks(pieces, target, done, here, ranges, shard):
+HALVED = ((0, 0, 8), (-1, 0, 8), (1, 0, 8), (2, 0, 4), (2, 4, 4))
+
+
+def load_blocks(pieces, target, done, here, ranges, shard, form):
     x_size, z_size, y_size = DP_SHAPE
     x, z, y = here[0], here[1], here[2]
     copies = []
     for half, start, at, width in ranges:
-        for index, far in enumerate((0, -1, 1, 2, 2)):
-            for block in range(4 if far == 2 else 8):
-                place_in = block + 4 * (index == 4)
+        for index, (far, begin, blocks) in enumerate(form):
+            for block in range(blocks):
+                place_in = begin + block
                 near = RING[place_in // 2]
                 to_x, to_y = (far, near) if half == 0 else (near, far)
                 to_x = lax.rem(x + (to_x + x_size), x_size)
@@ -112,7 +123,7 @@
                 to_z = lax.rem(z + place_in % 2, z_size)
                 row = pl.multiple_of(((to_x * z_size + to_z) * y_size + to_y) * shard, 16)
                 copy = pltpu.make_async_copy(
-                    pieces[half * 5 + index].at[block, :, pl.ds(start, width)],
+                    pieces[half * len(form) + index].at[block, :, pl.ds(start, width)],
                     target.at[pl.ds(row, shard), pl.ds(at, width)],
                     done.at[len(copies)],
                 )
@@ -144,19 +155,52 @@
     return sigma * (1.0 + value * (1.0 - sigma))
 
 
-def input_rows(quarter, width):
-    def kernel(here, own, across, core_own, core_across, gain, rows_out, normed_out, own_out):
-        core, pair = here[3], here[4]
-        places = (pair * 2 + core, (1 - pair) * 2 + core, pair * 2 + 1 - core, (1 - pair) * 2 + 1 - core)
-        for ref, place_at in zip((own, across, core_own, core_across), places, strict=True):
-            rows = ref[0:quarter, :]
-            value = rows.astype(f32)
-            scale = lax.rsqrt(jnp.mean(value * value, -1, keepdims=True) + eps)
-            rows_out[rows_at(place_at, quarter), :] = rows
-            normed = (value * scale * gain[...]).astype(bf16)
-            normed_out[rows_at(place_at, quarter), :] = normed
-            if ref is own:
-                own_out[...] = normed
+def pack_blocks(plan, width):
+    def kernel(*refs):
+        ins, out = refs[:-1], refs[-1]
+        for arg, lead, first, columns, at in plan:
+            if columns % LANES:
+                out[:, at : at + LANES] = jnp.zeros((out.shape[0], LANES), bf16)
+            ref = ins[arg]
+            value = ref[:, first : first + columns] if lead is None else ref[lead, :, first : first + columns]
+            out[:, at : at + columns] = value
+
+    return kernel
+
+
+def pack_plan(args, in_count, in_split, rest_split):
+    plan, sizes, at, group = [], [0, 0], 0, 0
+    entries = []
+    for arg, value in enumerate(args):
+        if arg == in_count:
+            group, at = 1, 0
+        for lead in range(value.shape[0]) if len(value.shape) == 3 else (None,):
+            for first in range(0, value.shape[-1], LANES):
+                columns = min(LANES, value.shape[-1] - first)
+                entries.append((group, at, arg, lead, first, columns))
+                at += LANES
+        sizes[group] = at
+    splits = (in_split, rest_split)
+    for group, at, arg, lead, first, columns in entries:
+        if at < splits[group]:
+            to = at + (in_split if group else 0)
+        else:
+            to = in_split + rest_split + at - splits[group] + (sizes[0] - in_split if group else 0)
+        plan.append((arg, lead, first, columns, to))
+    return plan, sum(sizes)
+
+
+def input_rows(quarter):
+    def kernel(here, rows_in, ids_in, gain, normed_out, own_out, tail_out):
+        rank = here[4] * 2 + here[3]
+        rows, width = rows_in.shape
+        value = rows_in[...].astype(f32)
+        scale = lax.rsqrt(jnp.mean(value * value, -1, keepdims=True) + eps)
+        normed = (value * scale * gain[...]).astype(bf16)
+        normed_out[...] = normed
+        own_out[...] = normed_out[rows_at(rank, quarter), :]
+        tail_out[:, :width] = normed[rows - EDGE :, :]
+        tail_out[:, width:] = ids_in[rows - EDGE :, :].astype(bf16)
 
     return kernel
 
@@ -165,18 +209,32 @@
     pairs = heads // 2
     tiles = (inner + 2 * state) // LANES
 
-    def kernel(here, normed, tail, taps, lags, bias, alog, skip, *refs):
-        pieces, refs = refs[:PIECES], refs[PIECES:]
-        weights_in, proj, y_out, conv_out, cum_out, steps_out, state_out, act, sums, done = refs
-        copies = load_blocks(pieces, weights_in, done, here, ranges, shard)
-        wait_all(copies)
+    def kernel(here, normed, tail, taps, ids_in, bias, alog, skip, *refs):
+        pieces, refs = refs[: 2 * len(HALVED)], refs[2 * len(HALVED) :]
+        proj, lags, y_out, conv_out, cum_out, steps_out, state_out, act, sums, weights_in, ids_ext, done = refs
+        copies = load_blocks(pieces, weights_in, done, here, ranges, shard, HALVED)
         columns = weights_in.shape[1]
         wide = 3 * LANES
+        rows, depth = normed.shape
+        ids_ext[0:EDGE, :] = tail[:, depth:].astype(f32)
+        ids_ext[EDGE:, :] = ids_in[...]
+        lane = ids((rows, LANES), 1)
+        row = ids((rows, LANES), 0)
+        no_row_before = here[0] + here[1] + here[2] == 0
+        lags[...] = jnp.zeros_like(lags)
+        for back in range(taps.shape[0] // 2):
+            same = ids_ext[EDGE - back : EDGE - back + rows, :] == ids_in[...]
+            same = same & ((row >= back) | jnp.logical_not(no_row_before))
+            lags[...] = jnp.where((lane == back) & same, 1.0, lags[...])
+        first = len(copies) // 2
+        wait_all(copies[:first])
         for at in range(0, columns, wide):
+            if at + wide > ranges[0][3] and first:
+                wait_all(copies[first:])
+                first = 0
             part = weights_in[:, at : at + wide]
-            proj[0:EDGE, at : at + wide] = dot(tail[...], part)
+            proj[0:EDGE, at : at + wide] = dot(tail[:, :depth], part)
             proj[EDGE:, at : at + wide] = dot(normed[...], part)
-        rows = y_out.shape[0]
         count = taps.shape[0] // 2
         for tile in range(tiles):
             at = tile * LANES
@@ -191,7 +249,6 @@
         c_rows = act[:, inner + state : inner + 2 * state]
         raw = proj[EDGE : EDGE + rows, 2 * inner + 2 * state :] + bias[...]
         steps = jnp.maximum(raw, 0.0) + jnp.log1p(jnp.exp(-jnp.abs(raw)))
-        lane = ids((rows, LANES), 1)
         reset = 1.0 - lags[:, 1:2]
         logs = jnp.where(lane < heads, -steps * jnp.exp(alog[...]), jnp.where(lane == heads, reset, 0.0))
         lower = (ids((rows, rows), 0) >= ids((rows, rows), 1)).astype(f32)
@@ -237,9 +294,9 @@
     pairs = heads // 2
 
     def kernel(here, y_in, proj, conv, cum_in, entering, gain, *refs):
-        pieces, refs = refs[:PIECES], refs[PIECES:]
+        pieces, refs = refs[: 2 * len(HALVED)], refs[2 * len(HALVED) :]
         w_back, y_out, mixed_out, mine_out, theirs_out, mixed_low, partial, done = refs
-        copies = load_blocks(pieces, w_back, done, here, ranges, shard)
+        copies = load_blocks(pieces, w_back, done, here, ranges, shard, HALVED)
         rows = y_in.shape[0]
         quarter = rows // 4
         width = partial.shape[1] - LANES
@@ -290,13 +347,14 @@
 
 
 def middle_rows(quarter, width, inner_total):
-    def kernel(here, sent, got, own, across, gain, middle_out, post_out, scales_out):
-        pair = here[4]
+    def kernel(here, sent, got, rows_in, gain, middle_out, post_out, scales_out):
+        core = here[3]
         total = sent[...].astype(f32) + got[...].astype(f32)
         squares = total[:, width : width + 1] + total[:, width + 1 : width + 2]
         scale_mix = lax.rsqrt(squares / inner_total + eps)
-        middle_out[rows_at(pair, quarter), :] = own[0:quarter, :].astype(f32)
-        middle_out[rows_at(1 - pair, quarter), :] = across[0:quarter, :].astype(f32)
+        for half in range(2):
+            to = slice(half * quarter, (half + 1) * quarter)
+            middle_out[to, :] = rows_in[rows_at(2 * half + core, quarter), :].astype(f32)
         middle = middle_out[...] + scale_mix * total[:, :width]
         middle_out[...] = middle
         scale = lax.rsqrt(jnp.mean(middle * middle, -1, keepdims=True) + eps)
@@ -308,23 +366,23 @@
 
 
 def experts_both(quarter, hidden, ffe, experts, shard, ranges):
-    def kernel(here, post_mine, post_theirs, own, across, core_own, core_across, share, *refs):
-        pieces, refs = refs[:PIECES], refs[PIECES:]
+    def kernel(here, post_mine, post_theirs, cot_in, share, *refs):
+        pieces, refs = refs[: 2 * len(HALVED)], refs[2 * len(HALVED) :]
         (
             post, cot, act_out, dpre_out, out_mine, out_theirs, dpost_mine, dpost_theirs,
             weights, shares, done,
         ) = refs
-        copies = load_blocks(pieces, weights, done, here, ranges, shard)
-        core, pair = here[3], here[4]
+        copies = load_blocks(pieces, weights, done, here, ranges, shard, HALVED)
+        core = here[3]
         half = 2 * quarter
         width = post.shape[1]
         post[0:half, :] = post_mine[...]
         post[half:, :] = post_theirs[...]
-        cot[rows_at(pair, quarter), :] = own[quarter:, :]
-        cot[rows_at(1 - pair, quarter), :] = across[quarter:, :]
-        cot[rows_at(2 + pair, quarter), :] = core_own[quarter:, :]
-        cot[rows_at(3 - pair, quarter), :] = core_across[quarter:, :]
         for index in range(2):
+            to = slice(index * quarter, (index + 1) * quarter)
+            cot[to, :] = cot_in[rows_at(2 * index + core, quarter), :]
+            to = slice(half + index * quarter, half + (index + 1) * quarter)
+            cot[to, :] = cot_in[rows_at(2 * index + 1 - core, quarter), :]
             shares[index * quarter : (index + 1) * quarter, :] = share[rows_at(2 * index + core, quarter), :]
             shares[half + index * quarter : half + (index + 1) * quarter, :] = share[
                 rows_at(2 * index + 1 - core, quarter), :
@@ -379,17 +437,18 @@
 
 def middle_back(quarter, width, inner_total):
     def kernel(
-        here, sent, got, own, across, middle_in, scales, core_total, pair_sent, gain,
+        here, sent, got, cot_in, middle_in, scales, core_total, pair_sent, gain,
         dmiddle_out, back_out, gain_out,
     ):
-        pair = here[4]
+        core = here[3]
         d_post = sent[...].astype(f32) + got[...].astype(f32)
         middle = middle_in[...]
         scale_mix, scale = scales[:, 0:1], scales[:, 1:2]
         gain_out[...] = 0.5 * jnp.sum(d_post * middle * scale, 0, keepdims=True)
         scaled = d_post * gain[...]
-        dmiddle_out[rows_at(pair, quarter), :] = own[quarter:, :].astype(f32)
-        dmiddle_out[rows_at(1 - pair, quarter), :] = across[quarter:, :].astype(f32)
+        for half in range(2):
+            to = slice(half * quarter, (half + 1) * quarter)
+            dmiddle_out[to, :] = cot_in[rows_at(2 * half + core, quarter), :].astype(f32)
         d_middle = (
             dmiddle_out[...]
             + scale * scaled
@@ -451,48 +510,60 @@
     return kernel
 
 
-def bc_split(quarter, inner):
+def bc_split(state, inner):
     def kernel(here, d_bc, tail, mine_out, theirs_out, whole):
         core = here[3]
         last = d_bc.shape[0] - EDGE
         whole[0:last, :] = d_bc[0:last, :]
         whole[last:, :] = d_bc[last:, :] + tail[:, inner:]
-        for index in range(2):
-            part = slice(index * quarter, (index + 1) * quarter)
-            mine_out[part, :] = whole[rows_at(2 * index + core, quarter), :]
-            theirs_out[part, :] = whole[rows_at(2 * index + 1 - core, quarter), :]
-
-    return kernel
-
-
-def bc_back(first, state):
-    def kernel(own_sum, got, tokens, win, own_out, rows_out, gain_out, weights, done):
-        copy = pltpu.make_async_copy(win.at[:, pl.ds(first, 2 * state)], weights, done)
-        copy.start()
-        total = (own_sum[...] + got[...]).astype(bf16)
-        own_out[...] = total
-        value = tokens[...].astype(f32)
-        scale = lax.rsqrt(jnp.mean(value * value, -1, keepdims=True) + eps)
-        copy.wait()
-        rows = dot(total, weights[...], NT)
-        rows_out[...] = rows
-        gain_out[...] = jnp.sum(rows * value * scale, 0, keepdims=True)
-
-    return kernel
-
-
-def input_back(quarter, inner, state):
-    def kernel(here, d_z, d_x, tail, d_dt, win, rows_in, dall_out, mine_out, theirs_out, gain_out, d_in):
+        first, second = whole[:, :state], whole[:, state:]
+        mine_out[...] = jnp.where(core == 0, first, second)
+        theirs_out[...] = jnp.where(core == 0, second, first)
+
+    return kernel
+
+
+def add_exact():
+    def kernel(mine, theirs, out):
+        out[...] = mine[...] + theirs[...]
+
+    return kernel
+
+
+def join_grads(inner):
+    def prepare(arrays, out):
+        d_z, d_x, tail, d_dt, bc_mine, bc_theirs = arrays
+        rows = out.shape[0]
+        out[:, :inner] = d_z[...]
+        out[:, inner : 2 * inner] = d_x[...].astype(bf16)
+        out[rows - EDGE :, inner : 2 * inner] = (d_x[rows - EDGE :, :] + tail[:, :inner]).astype(bf16)
+        out[:, 2 * inner : 2 * inner + LANES] = d_dt[...]
+        out[:, 2 * inner + LANES :] = (bc_mine[...] + bc_theirs[...]).astype(bf16)
+
+    return prepare
+
+
+def input_back(quarter, inner, state, shard, ranges):
+    def kernel(here, d_all, rows_in, *refs):
+        pieces, refs = refs[: 2 * len(HALVED)], refs[2 * len(HALVED) :]
+        mine_out, theirs_out, gain_out, d_in, win, done = refs
+        wait_all(load_blocks(pieces, win, done, here, ranges, shard, HALVED))
         core = here[3]
         rows, width = rows_in.shape
-        dall_out[:, :inner] = d_z[...]
-        dall_out[:, inner : 2 * inner] = d_x[...].astype(bf16)
-        dall_out[rows - EDGE :, inner : 2 * inner] = (d_x[rows - EDGE :, :] + tail[:, :inner]).astype(bf16)
-        dall_out[:, 2 * inner :] = d_dt[...]
         wide = 2 * LANES
+        bc_at = 2 * inner + 2 * state
+        d_bc = 0.5 * d_all[:, 2 * inner + LANES :].astype(f32)
         for at in range(0, width, wide):
-            d_in[:, at : at + wide] = dot(dall_out[:, : 2 * inner], win[at : at + wide, : 2 * inner], NT) + dot(
-                d_dt[...], win[at : at + wide, 2 * inner + 2 * state :], NT
+            part = win[at : at + wide, :]
+            w_bc = jnp.where(
+                core == 0,
+                part[:, 2 * inner : 2 * inner + state].astype(f32),
+                part[:, 2 * inner + state : bc_at].astype(f32),
+            )
+            d_in[:, at : at + wide] = (
+                dot(d_all[:, : 2 * inner], part[:, : 2 * inner], NT)
+                + dot(d_all[:, 2 * inner : 2 * inner + LANES], part[:, bc_at:], NT)
+                + dot(d_bc, w_bc, NT)
             )
         value = rows_in[...].astype(f32)
         scale = lax.rsqrt(jnp.mean(value * value, -1, keepdims=True) + eps)
@@ -506,11 +577,11 @@
 
 
 def input_grad(quarter):
-    def kernel(here, own_sum, got, bc_part, tokens, d_middle, gain, grad_out):
+    def kernel(here, own_sum, got, tokens, d_middle, gain, grad_out):
         pair = here[4]
         value = tokens[...].astype(f32)
         scale = lax.rsqrt(jnp.mean(value * value, -1, keepdims=True) + eps)
-        scaled = (own_sum[...] + got[...].astype(f32) + bc_part[...]) * gain[...]
+        scaled = (own_sum[...] + got[...].astype(f32)) * gain[...]
         grad_out[...] = (
             d_middle[rows_at(pair, quarter), :]
             + scale * scaled
@@ -661,21 +732,17 @@
 
 def exchange_states(sent, size, axis, reverse, wait=()):
     blocks = lax.axis_size(axis)
-    parts = after(wait, lax.all_to_all(sent, axis, 0, 0, tiled=True))
+    parts = lax.all_to_all(sent, axis, 0, 0, tiled=True)
     carried = kernel_call(
-        chain_states(reverse, blocks, size), [shape_of((blocks, size, LANES))], parts
+        chain_states(reverse, blocks, size), [shape_of((blocks, size, LANES))], parts, wait=wait
     )[0]
     back = lax.all_to_all(carried, axis, 0, 0, tiled=True)
-    return back.reshape(blocks * size, LANES), carried
+    return back.reshape(blocks * size, LANES)
 
 
 def other(value, bit):
     count = lax.axis_size("tensor")
     return lax.ppermute(value, "tensor", [(rank, rank ^ bit) for rank in range(count)])
-
-
-def after(first, value):
-    return lax.optimization_barrier((first, value))[1]
 
 
 def place():
@@ -714,10 +781,54 @@
     return [(mid, shift(mid, axis, 1), shift(mid, axis, -1)) for mid, axis in zip(mids, "xy", strict=True)]
 
 
-def finish_far(rings):
+def join_mids(cuts):
+    def kernel(*refs):
+        done = refs[-1]
+        copies = []
+        for half, cut in enumerate(cuts):
+            at = 0
+            out = refs[10 + half]
+            for ref in refs[5 * half : 5 * half + 5]:
+                copy = pltpu.make_async_copy(
+                    ref.at[:, :, pl.ds(cut, out.shape[2])], out.at[pl.ds(at, ref.shape[0])], done.at[len(copies)]
+                )
+                copy.start()
+                copies.append(copy)
+                at += ref.shape[0]
+        wait_all(copies)
+
+    return kernel
+
+
+def cut_far():
+    def kernel(*refs):
+        done = refs[-1]
+        copies = []
+        for index in range(4):
+            out = refs[4 + index]
+            half = out.shape[0]
+            copy = pltpu.make_async_copy(refs[index].at[pl.ds((index % 2) * half, half)], out, done.at[index])
+            copy.start()
+            copies.append(copy)
+        wait_all(copies)
+
+    return kernel
+
+
+def finish_cut(rings, wait):
+    arrived = [part for ring in rings for part in ring[1:]]
+    return kernel_call(
+        cut_far(), [shape_of((part.shape[0] // 2, *part.shape[1:]), bf16) for part in arrived], *arrived,
+        raw=range(4),
+        scratch=[pltpu.SemaphoreType.DMA((4,))],
+        wait=wait,
+    )
+
+
+def finish_far(rings, cut):
     pieces = []
-    for (mid, back, ahead), axis in zip(rings, "xy", strict=True):
-        pieces += [mid, back, ahead, shift(back[:4], axis, 1), shift(ahead[4:], axis, -1)]
+    for half, axis in enumerate("xy"):
+        pieces += [*rings[half], shift(cut[2 * half], axis, 1), shift(cut[2 * half + 1], axis, -1)]
     return pieces
 
 
@@ -747,13 +858,16 @@
     return lax.rem(index + (step + 4), 4)
 
 
-def term_products(plan, shard):
+def term_products(plan, shard, prepare=None, joined=0):
     x_size, z_size, y_size = DP_SHAPE
     part = 4 * shard
 
     def kernel(here, *refs):
-        count = 1 + max(max(lhs, rhs) for terms in plan for lhs, rhs, _, _ in terms)
-        arrays, outs, scratch = refs[:count], refs[count : count + 2 * SENT], refs[count + 2 * SENT :]
+        count = len(refs) - 2 * SENT - 2 - (prepare is not None)
+        arrays, outs, scratch = list(refs[:count]), refs[count : count + 2 * SENT], refs[-2:]
+        if prepare is not None:
+            prepare(arrays[count - joined :], refs[-3])
+            arrays = [*arrays[: count - joined], refs[-3]]
         x, y = here[0], here[2]
         for half, terms in enumerate(plan):
             product = scratch[half]
@@ -798,15 +912,30 @@
     return first, second
 
 
+def ring_total():
+    def kernel(*refs):
+        for half in range(2):
+            out = refs[2 * SENT + half]
+            part = out.shape[0] // 2
+            first, second = ring_totals(refs[half * SENT : (half + 1) * SENT], part)
+            out[0:part, :] = first.astype(bf16)
+            out[part:, :] = second.astype(bf16)
+
+    return kernel
+
+
 def ring_fold(shard):
     part = 4 * shard
 
     def kernel(here, *refs):
         x, y = here[0], here[2]
+        ended, refs = refs[:2], refs[2:]
         outs, scratch = refs[2 * SENT : 4 * SENT], refs[4 * SENT :]
         for half in range(2):
             total = scratch[half]
-            total[0:part, :], total[part:, :] = ring_totals(refs[half * SENT : (half + 1) * SENT], part)
+            wide = ended[half].shape[1]
+            total[:, :wide] = ended[half][...].astype(f32)
+            total[0:part, wide:], total[part:, wide:] = ring_totals(refs[half * SENT : (half + 1) * SENT], part)
 
             def along_y(step, side, total=total):
                 row = side * part + wrapped(y, step) * shard
@@ -845,14 +974,15 @@
     return arrived, stays
 
 
-def ring_pass(arrived, stays, plan, axes, part, wait=None):
+def ring_added(arrived, stays, widths, part, wait=()):
     terms = []
     for half in range(2):
         terms += [*arrived[2 * half : 2 * half + 2], *stays[half][1:]]
-    if wait is not None:
-        terms = after(wait, terms)
-    shapes = [shape_of((part, width), bf16) for width in widths_of(plan) for _ in range(2)]
-    sent = kernel_call(ring_add(part), shapes, *terms)
+    shapes = [shape_of((part, width), bf16) for width in widths for _ in range(2)]
+    return kernel_call(ring_add(part), shapes, *terms, whole=True, wait=wait)
+
+
+def ring_passed(arrived, stays, sent, axes):
     results = []
     for half, axis in enumerate(axes):
         last = [shift(sent[2 * half], axis, 1), shift(sent[2 * half + 1], axis, -1)]
@@ -860,38 +990,41 @@
     return results
 
 
+def ring_pass(arrived, stays, widths, axes, part, wait=()):
+    return ring_passed(arrived, stays, ring_added(arrived, stays, widths, part, wait), axes)
+
+
 def widths_of(plan):
     return [sum(last - first for _, _, first, last in terms) for terms in plan]
 
 
-def scatter_begin(here, plan, arrays, shard):
+def scatter_begin(here, plan, arrays, shard, prepare=None, joined=0, columns=0, wait=()):
     part = 4 * shard
     widths = widths_of(plan)
+    shapes = chunk_shapes(part, widths)
+    if prepare is not None:
+        shapes.append(shape_of((arrays[0].shape[0], columns), bf16))
     return kernel_call(
-        term_products(plan, shard), chunk_shapes(part, widths), here, *arrays,
+        term_products(plan, shard, prepare, joined), shapes, here, *arrays,
         flops=sum(2 * arrays[0].shape[0] * 8 * part * width for width in widths),
         small=(0,),
         scratch=[pltpu.VMEM((8 * part, width), bf16) for width in widths],
-    )
-
-
-def scatter_fold(here, results, plan, shard):
-    widths = widths_of(plan)
-    return kernel_call(
-        ring_fold(shard), chunk_shapes(shard, widths), here, *results,
-        small=(0,),
-        scratch=[pltpu.VMEM((8 * shard, width), f32) for width in widths],
-    )
-
-
-def scatter_last(here, results, plan, shard):
-    widths = widths_of(plan)
-    shape = (shard, sum(widths))
-    mine, sent = kernel_call(
-        ring_end(shard, widths), [shape_of(shape), shape_of(shape, bf16)], here, *results,
-        small=(0,),
-    )
-    return mine + shift(sent, "z", 1).astype(f32)
+        whole=True,
+        wait=wait,
+    )
+
+
+def grad_blocks(plan, shard):
+    def kernel(mine, got, *outs):
+        for out, entries in zip(outs, plan, strict=True):
+            for lead, first, at, columns in entries:
+                value = mine[:, at : at + columns] + got[:, at : at + columns].astype(f32)
+                if lead is None:
+                    out[:, first : first + columns] = value
+                else:
+                    out[lead, :, first : first + columns] = value
+
+    return kernel
 
 
 EACH = 6
@@ -918,7 +1051,7 @@
 def small_table(layout, inner, state, taps, heads):
     share = inner // LANES
 
-    def kernel(here, norm, norm_bc, post, conv, gain, head, skip, out, table):
+    def kernel(here, norm, post, conv, gain, head, skip, out, table):
         rank = here[4] * 2 + here[3]
         ranks = (layout["skip"] - layout["gain"]) // share
 
@@ -927,7 +1060,7 @@
 
         table[...] = jnp.zeros_like(table)
         for i in range(layout["post"] - layout["norm"]):
-            table[layout["norm"] + i : layout["norm"] + i + 1, :] = norm[:, lanes(i)] + norm_bc[:, lanes(i)]
+            table[layout["norm"] + i : layout["norm"] + i + 1, :] = norm[:, lanes(i)]
             table[layout["post"] + i : layout["post"] + i + 1, :] = post[:, lanes(i)]
         for i in range(share):
             for tap in range(taps):
@@ -1025,60 +1158,43 @@
     hidden = experts * ffe + ffs
     wide_in = 2 * inner + 2 * state + LANES
 
-    own_rows = jnp.concatenate([tokens, cotangent], 0)
-    pack_in = jnp.concatenate(
-        [
-            w_zx.reshape(shard, 2 * inner),
-            w_bc.reshape(shard, 2 * state),
-            jnp.pad(w_dt, ((0, 0), (0, LANES - heads))),
-            w_out.T,
-        ],
-        1,
-    )
-    pack_rest = jnp.concatenate(
-        [
-            exp_gate.transpose(1, 0, 2).reshape(shard, experts * ffe),
-            sh_gate,
-            exp_up.transpose(1, 0, 2).reshape(shard, experts * ffe),
-            sh_up,
-            exp_down.transpose(2, 0, 1).reshape(shard, experts * ffe),
-            sh_down.T,
-        ],
-        1,
-    )
-    in_columns, rest_columns = wide_in, pack_rest.shape[1]
-    in_split, rest_split = pack_in.shape[1] // 256 * LANES, rest_columns // 256 * LANES
-    in_near, rest_near = shift(pack_in, "z", 1), shift(pack_rest, "z", 1)
-    both_splits = zip((pack_in, pack_rest), (in_split, rest_split), strict=True)
-    pack = [[part[:, :split], part[:, split:]] for part, split in both_splits]
-    both_splits = zip((in_near, rest_near), (in_split, rest_split), strict=True)
-    near = [[part[:, :split], part[:, split:]] for part, split in both_splits]
-    mids = spread(
-        jnp.concatenate([pack[0][0], pack[1][0], pack[0][1], pack[1][1]], 1),
-        jnp.concatenate([near[0][0], near[1][0], near[0][1], near[1][1]], 1),
-        in_split + rest_split,
-    )
-    cuts = (in_split, pack_in.shape[1] - in_split)
+    shards = [
+        w_zx.reshape(shard, 2 * inner),
+        w_bc.reshape(shard, 2 * state),
+        w_dt,
+        w_out.T,
+        exp_gate,
+        sh_gate,
+        exp_up,
+        sh_up,
+        exp_down.transpose(0, 2, 1),
+        sh_down.T,
+    ]
+    in_columns, mix_columns, rest_columns = wide_in, wide_in + inner, 3 * hidden
+    in_split, rest_split = mix_columns // 256 * LANES, rest_columns // 256 * LANES
+    plan, pack_columns = pack_plan(shards, 4, in_split, rest_split)
+    pack = kernel_call(pack_blocks(plan, pack_columns), [shape_of((shard, pack_columns), bf16)], *shards, alone=True)[0]
+    near = shift(pack, "z", 1)
+    mids = spread(pack, near, in_split + rest_split)
+    cuts = (in_split, mix_columns - in_split)
     in_mids = [
         jnp.concatenate([part[:, :, :cut] for part in parts], 0) for parts, cut in zip(mids, cuts, strict=True)
     ]
-    rest_mids = [
-        jnp.concatenate([part[:, :, cut:] for part in parts], 0) for parts, cut in zip(mids, cuts, strict=True)
-    ]
     in_rings = finish(in_mids)
-    core_rows = other(own_rows, 1)
-    pair_rows = other(own_rows, 2)
-    far_rows = other(pair_rows, 1)
-    rows_all, normed_in, normed_own = kernel_call(
-        input_rows(quarter, model_dim),
-        [shape_of((block_rows, model_dim), bf16)] * 2 + [shape_of((quarter, model_dim), bf16)],
-        here, own_rows, pair_rows, core_rows, far_rows, norm_gain[None, :],
-        small=(0,),
-    )
-    tail_rows = from_behind(normed_in[block_rows - EDGE :], "dp", 1)
-    in_pieces = finish_far(after(tail_rows, in_rings))
-    rest_rings = finish(after(in_pieces, rest_mids))
-
+    rows_all = lax.all_gather(tokens, "tensor", axis=0, tiled=True)
+    cot_all = lax.all_gather(cotangent, "tensor", axis=0, tiled=True)
+    seg_lanes = jnp.broadcast_to(segments.astype(f32)[:, None], (block_rows, LANES))
+    normed_in, normed_own, tail_sent = kernel_call(
+        input_rows(quarter),
+        [
+            shape_of((block_rows, model_dim), bf16),
+            shape_of((quarter, model_dim), bf16),
+            shape_of((EDGE, model_dim + LANES), bf16),
+        ],
+        here, rows_all, seg_lanes, norm_gain[None, :],
+        small=(0,),
+    )
+    tail_rows = from_behind(tail_sent, "dp", 1)
     head_start = tensor_rank * heads
     chan_start = tensor_rank * inner
     bias_local = lax.dynamic_slice_in_dim(dt_bias, head_start, heads)
@@ -1092,45 +1208,50 @@
     alog_row = jnp.pad(alog_local, (0, LANES - heads))[None, :]
     skip_row = jnp.repeat(skip_local, head_dim)[None, :]
 
-    seg_float = segments.astype(f32)
-    tail_ids = from_behind(seg_float[block_rows - EDGE :], "dp", 1)
-    ids_ext = jnp.concatenate([tail_ids, seg_float])
-    global_rows = lax.axis_index("dp") * block_rows + jnp.arange(block_rows, dtype=jnp.int32)
-    lags = [
-        (
-            (ids_ext[EDGE - back : EDGE - back + block_rows] == seg_float) & (global_rows >= back)
-        ).astype(f32)
-        for back in range(conv_taps)
-    ]
-    lags = jnp.pad(jnp.stack(lags, 1), ((0, 0), (0, LANES - conv_taps)))
+    hot = routes[:, :, None] == jnp.arange(LANES, dtype=jnp.int32)[None, None, :]
+    share = jnp.sum(jnp.where(hot, gate_weights[:, :, None], 0.0), 1)
+    early = (tail_rows, taps, bias_row, alog_row, skip_row, gain_row, share)
+    in_pieces = finish_far(in_rings, finish_cut(in_rings, early))
+    rest_mids = kernel_call(
+        join_mids(cuts),
+        [shape_of((8, shard, parts[0].shape[2] - cut), bf16) for parts, cut in zip(mids, cuts, strict=True)],
+        *[part for parts in mids for part in parts],
+        raw=range(10),
+        alone=True,
+        scratch=[pltpu.SemaphoreType.DMA((10,))],
+        wait=in_pieces,
+    )
+    rest_rings = finish(rest_mids)
+    rest_cut = finish_cut(rest_rings, ())
+    rest_pieces = finish_far(rest_rings, rest_cut)
 
     scan_flops = 2 * block_rows * block_rows * inner * 2
     size = inner // dp_count
     state_shape = shape_of((dp_count, size + SUB, state))
-    win, proj, y_first, conv, cum, steps, state_sum = kernel_call(
+    proj, lags, y_first, conv, cum, steps, state_sum = kernel_call(
         scan_front(heads, inner, state, shard, column_ranges(in_split, 0, in_columns)),
         [
-            shape_of((model_dim, in_columns), bf16),
             shape_of((block_rows + EDGE, in_columns)),
+            shape_of((block_rows, LANES)),
             shape_of((block_rows, inner)),
             shape_of((block_rows, inner + 2 * state)),
             shape_of((block_rows, LANES)),
             shape_of((block_rows, LANES)),
             state_shape,
         ],
-        here, normed_in, tail_rows, taps, lags, bias_row, alog_row, skip_row, *in_pieces,
+        here, normed_in, tail_rows, taps, seg_lanes, bias_row, alog_row, skip_row, *in_pieces,
         flops=scan_flops + 2 * block_rows * model_dim * in_columns,
         small=(0,),
-        raw=range(8, 8 + PIECES),
+        raw=range(8, 8 + len(in_pieces)),
         scratch=[
             pltpu.VMEM((block_rows, inner + 2 * state), f32),
             pltpu.VMEM((inner, state), f32),
+            pltpu.VMEM((model_dim, in_columns), bf16),
+            pltpu.VMEM((block_rows + EDGE, LANES), f32),
             pltpu.SemaphoreType.DMA((64,)),
         ],
     )
-    entering, carried = exchange_states(state_sum, size, "dp", False, [ring[1:] for ring in rest_rings])
-    rest_pieces = finish_far(after(carried, rest_rings))
-    entering = after(rest_pieces, entering)
+    entering = exchange_states(state_sum, size, "dp", False, rest_mids)
     w_back, y_all, mixer_in, mine, theirs = kernel_call(
         gate_front(heads, inner, state, shard, column_ranges(in_split, in_columns, in_columns + inner)),
         [
@@ -1143,7 +1264,7 @@
         here, y_first, proj, conv, cum, entering, gain_row, *in_pieces,
         flops=scan_flops,
         small=(0,),
-        raw=range(7, 7 + PIECES),
+        raw=range(7, 7 + len(in_pieces)),
         scratch=[
             pltpu.VMEM((block_rows, inner), bf16),
             pltpu.VMEM((block_rows, model_dim + LANES), f32),
@@ -1154,6 +1275,7 @@
         core_sum(model_dim),
         [shape_of((2 * quarter, model_dim)), shape_of((2 * quarter, model_dim + LANES), bf16)],
         mine, other(theirs, 1),
+        wait=[ring[1:] for ring in rest_rings],
     )
     from_pair = other(sent, 2)
     middle, post_mine, scales = kernel_call(
@@ -1163,12 +1285,10 @@
             shape_of((2 * quarter, model_dim), bf16),
             shape_of((2 * quarter, LANES)),
         ],
-        here, sent, from_pair, own_rows, pair_rows, post_gain[None, :],
+        here, sent, from_pair, rows_all, post_gain[None, :],
         small=(0,),
     )
     post_theirs = other(post_mine, 1)
-    hot = routes[:, :, None] == jnp.arange(LANES, dtype=jnp.int32)[None, None, :]
-    share = jnp.sum(jnp.where(hot, gate_weights[:, :, None], 0.0), 1)
     half_shape = (2 * quarter, model_dim)
     post, cot, act, d_pre, ffn_mine, ffn_theirs, dpost_mine, dpost_theirs = kernel_call(
         experts_both(quarter, hidden, ffe, experts, shard, column_ranges(rest_split, 0, 3 * hidden)),
@@ -1182,10 +1302,10 @@
             shape_of(half_shape),
             shape_of(half_shape, bf16),
         ],
-        here, post_mine, post_theirs, own_rows, pair_rows, core_rows, far_rows, share, *rest_pieces,
+        here, post_mine, post_theirs, cot_all, share, *rest_pieces,
         flops=12 * block_rows * model_dim * hidden,
         small=(0,),
-        raw=range(8, 8 + PIECES),
+        raw=range(5, 5 + len(rest_pieces)),
         scratch=[
             pltpu.VMEM((model_dim, 3 * hidden), bf16),
             pltpu.VMEM((block_rows, LANES), f32),
@@ -1194,10 +1314,9 @@
     )
     ffn_split = (3 * hidden) // 256 * LANES
     ffn_plan = (((0, 2, 0, ffn_split),), ((0, 2, ffn_split, 2 * hidden), (1, 3, 0, hidden)))
+    sent_post = kernel_call(add_round(), [shape_of(half_shape, bf16)], dpost_mine, other(dpost_theirs, 1))[0]
     ffn_chunks = scatter_begin(here, ffn_plan, (post, cot, d_pre, act), shard)
     ffn_sent, ffn_terms = ring_send(ffn_chunks, "xy")
-    dpost_theirs = after(ffn_chunks, dpost_theirs)
-    sent_post = kernel_call(add_round(), [shape_of(half_shape, bf16)], dpost_mine, other(dpost_theirs, 1))[0]
     d_middle, back_mine, grad_post_gain = kernel_call(
         middle_back(quarter, model_dim, inner_total),
         [
@@ -1205,7 +1324,7 @@
             shape_of((2 * quarter, model_dim + LANES), bf16),
             shape_of((1, model_dim)),
         ],
-        here, sent_post, other(sent_post, 2), own_rows, pair_rows, middle, scales, core_total, from_pair,
+        here, sent_post, other(sent_post, 2), cot_all, middle, scales, core_total, from_pair,
         post_gain[None, :],
         small=(0,),
     )
@@ -1242,9 +1361,9 @@
         small=(0,),
     )[0]
 
-    leaving, carried = exchange_states(d_enter, size, "dp", True, ffn_sent)
-    ffn_rings = ring_pass(ffn_sent, ffn_terms, ffn_plan, "xy", 4 * shard, carried)
-    leaving = after(ffn_rings, leaving)
+    leaving = exchange_states(d_enter, size, "dp", True, block_out)
+    ffn_widths = widths_of(ffn_plan)
+    ffn_added = ring_added(ffn_sent, ffn_terms, ffn_widths, 4 * shard)
     d_x, d_bc, tail, d_dt, grad_taps, grad_heads, grad_skip = kernel_call(
         scan_back(heads, inner, state),
         [
@@ -1258,46 +1377,51 @@
         ],
         proj, taps, lags, bias_row, alog_row, skip_row, conv, cum, steps, d_y, entering, leaving,
         flops=3 * scan_flops,
+        wait=ffn_added,
         scratch=[
             pltpu.VMEM((block_rows, inner + 2 * state), f32),
             pltpu.VMEM((LANES, block_rows), f32),
             pltpu.VMEM((block_rows + EDGE, inner + 2 * state), f32),
         ],
     )
-    ffn_chunks = scatter_fold(here, after(d_dt, ffn_rings), ffn_plan, shard)
-    tail = after(ffn_chunks, from_behind(tail, "dp", -1))
-    ffn_sent, ffn_terms = ring_send(after(tail, ffn_chunks), "yx")
-    bc_half = (2 * quarter, 2 * state)
+    tail = from_behind(tail, "dp", -1)
+    ffn_rings = ring_passed(ffn_sent, ffn_terms, ffn_added, "xy")
+    ffn_totals = kernel_call(
+        ring_total(), [shape_of((8 * shard, width), bf16) for width in ffn_widths], *ffn_rings, whole=True
+    )
+    bc_half = shape_of((block_rows, state))
     bc_mine, bc_theirs = kernel_call(
-        bc_split(quarter, inner),
-        [shape_of(bc_half)] * 2,
+        bc_split(state, inner),
+        [bc_half] * 2,
         here, d_bc, tail,
         small=(0,),
         scratch=[pltpu.VMEM((block_rows, 2 * state), f32)],
     )
-    bc_shape = (quarter, 2 * state)
-    bc_sum, bc_sent = kernel_call(
-        add_split(quarter), [shape_of(bc_shape)] * 2, here, bc_mine, other(bc_theirs, 1), small=(0,)
-    )
-    d_all, din_mine, din_theirs, grad_norm = kernel_call(
-        input_back(quarter, inner, state),
-        [
-            shape_of((block_rows, 2 * inner + LANES), bf16),
-            shape_of(half_shape),
-            shape_of(half_shape, bf16),
-            shape_of((1, model_dim)),
+    bc_sum = kernel_call(add_exact(), [bc_half], bc_mine, other(bc_theirs, 1))[0]
+    dt_at = 2 * inner
+    bc_at = dt_at + LANES
+    out_at = bc_at + state
+    mix_split = (out_at + inner) // 256 * LANES
+    mix_plan = (((0, 3, 0, mix_split),), ((0, 3, mix_split, out_at), (1, 2, 0, inner)))
+    mix_widths = widths_of(mix_plan)
+    *mix_chunks, d_all = scatter_begin(
+        here, mix_plan,
+        (normed_in, d_proj, mixer_in, d_z, d_x, tail, d_dt, bc_sum, other(bc_sum, 2)),
+        shard, join_grads(inner), 6, out_at, ffn_totals,
+    )
+    mix_sent, mix_terms = ring_send(mix_chunks, "xy")
+    din_mine, din_theirs, grad_norm = kernel_call(
+        input_back(quarter, inner, state, shard, column_ranges(in_split, 0, in_columns)),
+        [shape_of(half_shape), shape_of(half_shape, bf16), shape_of((1, model_dim))],
+        here, d_all, rows_all, *in_pieces,
+        flops=2 * block_rows * model_dim * in_columns,
+        small=(0,),
+        raw=range(3, 3 + len(in_pieces)),
+        scratch=[
+            pltpu.VMEM((block_rows, model_dim), f32),
+            pltpu.VMEM((model_dim, in_columns), bf16),
+            pltpu.SemaphoreType.DMA((64,)),
         ],
-        here, d_z, d_x, tail, d_dt, win, rows_all,
-        flops=2 * block_rows * model_dim * in_columns,
-        small=(0,),
-        scratch=[pltpu.VMEM((block_rows, model_dim), f32)],
-    )
-    bc_own, din_bc, norm_bc = kernel_call(
-        bc_back(2 * inner, state),
-        [shape_of(bc_shape, bf16), shape_of((quarter, model_dim)), shape_of((1, model_dim))],
-        bc_sum, other(bc_sent, 2), tokens, win,
-        raw=(3,),
-        scratch=[pltpu.VMEM((model_dim, 2 * state), bf16), pltpu.SemaphoreType.DMA],
     )
     din_own, din_sent = kernel_call(
         add_split(quarter),
@@ -1308,37 +1432,23 @@
     grad_tokens = kernel_call(
         input_grad(quarter),
         [shape_of((quarter, model_dim))],
-        here, din_own, other(din_sent, 2), din_bc, tokens, d_middle, norm_gain[None, :],
+        here, din_own, other(din_sent, 2), tokens, d_middle, norm_gain[None, :],
         small=(0,),
     )[0]
-
-    dt_at = 2 * inner
-    bc_at = dt_at + LANES
-    out_at = bc_at + 2 * state
-    mix_split = (out_at + inner) // 256 * LANES
-    mix_plan = (
-        ((0, 2, 0, mix_split),),
-        ((0, 2, mix_split, bc_at), (4, 5, 0, 2 * state), (1, 3, 0, inner)),
-    )
-    mix_arrays = (normed_in, d_proj, d_all, mixer_in, normed_own, bc_own)
-    mix_arrays = after(ffn_sent, (normed_in, d_proj, d_all, mixer_in, normed_own, bc_own))
-    mix_chunks = scatter_begin(here, mix_plan, mix_arrays, shard)
-    mix_sent, mix_terms = ring_send(mix_chunks, "xy")
     layout = small_rows(model_dim, inner, state, conv_taps, tensor_count)
     table_shape = shape_of((dp_count, SUB, LANES))
     table = kernel_call(
         small_table(layout, inner, state, conv_taps, heads),
         [table_shape],
-        here, after(mix_chunks, grad_norm), norm_bc, grad_post_gain, grad_taps, grad_gain, grad_heads, grad_skip,
+        here, grad_norm, grad_post_gain, grad_taps, grad_gain, grad_heads, grad_skip,
         small=(0,),
         scratch=[pltpu.VMEM((dp_count * EACH, LANES), f32)],
     )[0]
     table = lax.all_to_all(table, "dp", 0, 0, tiled=True)
-    mix_rings = ring_pass(mix_sent, mix_terms, mix_plan, "xy", 4 * shard, table)
+    mix_rings = ring_pass(mix_sent, mix_terms, mix_widths, "xy", 4 * shard, grad_tokens)
     devices = dp_count * tensor_count
-    table = kernel_call(small_sum(), [shape_of((devices, SUB, LANES))], after(mix_rings[1], table))[0]
-    table = lax.all_to_all(table, ("dp", "tensor"), 0, 0, tiled=True)
-    mix_rings = after(table, mix_rings)
+    table = kernel_call(small_sum(), [shape_of((devices, SUB, LANES))], table)[0]
+    table_end = lax.all_to_all(table, ("dp", "tensor"), 0, 0, tiled=True)
     small = kernel_call(
         small_out(layout, tensor_count, inner, state, conv_taps),
         [
@@ -1350,50 +1460,91 @@
             shape_of((1, inner_total)),
             shape_of((2 * tensor_count, LANES)),
         ],
-        table,
+        table_end,
         scratch=[pltpu.VMEM((dp_count * EACH, LANES), f32)],
     )
     norm_sum, post_sum, taps_x, taps_bc, gain_sum, skip_sum, head_sums = small
     head_sums = head_sums.reshape(2, tensor_count, LANES)[:, :, :heads].reshape(2, -1)
-    ffn_rings = ring_pass(ffn_sent, ffn_terms, ffn_plan, "yx", shard, mix_chunks)
-    grad_ffn = scatter_last(here, ffn_rings, ffn_plan, shard)
-    mix_chunks_last = scatter_fold(here, mix_rings, mix_plan, shard)
-    mix_sent, mix_terms = ring_send(mix_chunks_last, "yx")
-    mix_rings_last = ring_pass(mix_sent, mix_terms, mix_plan, "yx", shard)
-    grad_mix = scatter_last(here, mix_rings_last, mix_plan, shard)
-    grad_bc = grad_mix[:, bc_at:out_at]
-    grad_bc = grad_bc + other(grad_bc, 1)
-    grad_bc = grad_bc + other(grad_bc, 2)
-    def experts_of(columns):
-        return columns.reshape(shard, experts, ffe)
+    widths = [one + two for one, two in zip(ffn_widths, mix_widths, strict=True)]
+    chunks = kernel_call(
+        ring_fold(shard), chunk_shapes(shard, widths), here, *ffn_totals, *mix_rings,
+        small=(0,),
+        scratch=[pltpu.VMEM((8 * shard, width), f32) for width in widths],
+        whole=True,
+        wait=table,
+    )
+    sent, terms = ring_send(chunks, "yx")
+    results = ring_pass(sent, terms, widths, "yx", shard, table_end)
+    sum_shape = (shard, sum(widths))
+    mine, sent = kernel_call(
+        ring_end(shard, widths), [shape_of(sum_shape), shape_of(sum_shape, bf16)], here, *results,
+        small=(0,),
+        whole=True,
+    )
+    def found(group, first, columns):
+        ffn_wide, mix_wide = ffn_widths[0], mix_widths[0]
+        entries = []
+        for at in range(first, first + columns, LANES):
+            half, shift_by = (0, 0) if at < (ffn_wide, mix_wide)[group] else (1, (ffn_wide, mix_wide)[group])
+            begin = half * widths[0] + (ffn_widths[half] if group else 0)
+            entries.append((at - first, begin + at - shift_by, LANES))
+        return entries
+
+    def plain(group, first, columns):
+        return [(None, *entry) for entry in found(group, first, columns)]
+
+    def by_expert(first):
+        entries = found(0, first, experts * ffe)
+        return [(at // ffe, at % ffe, begin, columns) for at, begin, columns in entries]
 
     wide_e = experts * ffe
-    g_gate, g_up, g_down = (
-        grad_ffn[:, :hidden],
-        grad_ffn[:, hidden : 2 * hidden],
-        grad_ffn[:, 2 * hidden :],
-    )
+    out_plan = [
+        plain(1, 0, 2 * inner),
+        plain(1, dt_at, LANES),
+        plain(1, bc_at, state),
+        plain(1, out_at, inner),
+        by_expert(0),
+        by_expert(hidden),
+        by_expert(2 * hidden),
+        plain(0, wide_e, ffs),
+        plain(0, hidden + wide_e, ffs),
+        plain(0, 2 * hidden + wide_e, ffs),
+    ]
+    grad_zx, grad_dt, bc_half, grad_out, grad_eg, grad_eu, grad_ed, grad_sg, grad_su, grad_sd = kernel_call(
+        grad_blocks(out_plan, shard),
+        [
+            shape_of((shard, 2 * inner)),
+            shape_of((shard, LANES)),
+            shape_of((shard, state)),
+            shape_of((shard, inner)),
+            *[shape_of((experts, shard, ffe))] * 3,
+            *[shape_of((shard, ffs))] * 3,
+        ],
+        mine, shift(sent, "z", 1),
+    )
+    bc_far = other(bc_half, 1)
+    grad_bc = jnp.stack([jnp.where(core == 0, bc_half, bc_far), jnp.where(core == 0, bc_far, bc_half)], 1)
     return (
         block_out,
         grad_tokens,
         norm_sum[0],
-        grad_mix[:, : 2 * inner].reshape(shard, 2, inner),
-        grad_bc.reshape(shard, 2, state),
-        grad_mix[:, dt_at : dt_at + heads],
+        grad_zx.reshape(shard, 2, inner),
+        grad_bc,
+        grad_dt[:, :heads],
         taps_x,
         taps_bc.reshape(conv_taps, 2, state),
         head_sums[0],
         head_sums[1],
         jnp.sum(skip_sum.reshape(head_total, head_dim), 1),
         gain_sum[0],
-        grad_mix[:, out_at:].T,
+        grad_out.T,
         post_sum[0],
-        experts_of(g_gate[:, :wide_e]).transpose(1, 0, 2),
-        experts_of(g_up[:, :wide_e]).transpose(1, 0, 2),
-        experts_of(g_down[:, :wide_e]).transpose(1, 2, 0),
-        g_gate[:, wide_e:],
-        g_up[:, wide_e:],
-        g_down[:, wide_e:].T,
+        grad_eg,
+        grad_eu,
+        grad_ed.transpose(0, 2, 1),
+        grad_sg,
+        grad_su,
+        grad_sd.T,
     )
 
 

time: 508 us -> 469 us (0.923)
  blocking collectives: 31.4 us -> 93.5 us
  starting transfers between devices: 164 us -> 116 us
  local copies, waits for them, and re-layouts: 87.8 us -> 48.5 us
  waiting for transfers between devices: 110 us -> 92.6 us
    ppermute x17 -> x13, starting transfers between devices: 56 us -> 26.6 us  [other(): lax.ppermute(value, 'tensor', [(rank, rank ^ bit) for rank in range(count)])]
    unnamed x322 -> x216, local copies, waits for them, and re-layouts: 66.2 us -> 40.3 us
    all_gather x0 -> x2, blocking collectives: none -> 25.6 us  [the longest x1 15 us: body(): rows_all = lax.all_gather(tokens, 'tensor', axis=0, tiled=True)]
    all_to_all x1 -> x2, blocking collectives: 14.3 us -> 33.9 us  [the longest x1 22.3 us: body(): table_end = lax.all_to_all(table, ('dp', 'tensor'), 0, 0, tiled=True)]
    all_to_all x1, blocking collectives: 17.1 us -> 33.9 us  [exchange_states(): back = lax.all_to_all(carried, axis, 0, 0, tiled=True)]
    ppermute x60 -> x50, waiting for transfers between devices: 66 us -> 52.8 us  [shift(): return lax.ppermute(value, 'dp', pairs)]
    ppermute x60 -> x50, starting transfers between devices: 82.3 us -> 72.4 us  [shift(): return lax.ppermute(value, 'dp', pairs)]
    slice x18 -> x0, local copies, waits for them, and re-layouts: 9.01 us -> none  [the longest x4 4.18 us: finish_far(): ahead[4:]]
  transfers between devices with their start and end apart: 84 -> 68, of which waited for: 28 -> 18; matrix products, arithmetic and copies ran while one was open for 7% -> 4% of each run, Pallas kernels for 9% -> 13%
where the time goes in v2:
time: 469 us; the launch traced here: 460 us
  starting transfers between devices  116 us (25%)
  Pallas kernels  102 us (22%)
  blocking collectives  93.5 us (20%)
  waiting for transfers between devices  92.6 us (20%)
  local copies, waits for them, and re-layouts  48.5 us (10%)
  other arithmetic  4.7 us (1%)
    pallas_call x35, Pallas kernels, kernel_call(): pl.pallas_call(body_of, name=kernel.__qualname__.split('.')[0], out_shape...  102 us
    ppermute x50, starting transfers between devices, shift(): return lax.ppermute(value, 'dp', pairs)  72.4 us
    ppermute x50, waiting for transfers between devices, shift(): return lax.ppermute(value, 'dp', pairs)  52.8 us
    unnamed x216, local copies, waits for them, and re-layouts  40.3 us
    ppermute x13, waiting for transfers between devices, other(): lax.ppermute(value, 'tensor', [(rank, rank ^ bit) for rank in range(count)])  35.9 us
    all_to_all x1, blocking collectives, exchange_states(): back = lax.all_to_all(carried, axis, 0, 0, tiled=True)  33.9 us
    ppermute x13, starting transfers between devices, other(): lax.ppermute(value, 'tensor', [(rank, rank ^ bit) for rank in range(count)])  26.6 us
    all_to_all x1, blocking collectives, body(): table_end = lax.all_to_all(table, ('dp', 'tensor'), 0, 0, tiled=True)  22.3 us
  transfers between devices with their start and end apart: 68, of which 18 were waited for; matrix products, arithmetic and copies ran while one was open for 4% of the time, Pallas kernels for 13%

profile of v2, /device:TPU:1, one launch (start us, length us, event | category | flops | bytes accessed | tf_op | source)
XLA Modules:
  0.0 460.5 jit_solution(7572202191749298981)
XLA Ops:
  11.6 12.0 %collective-permute-done.1 = bf16[48,6528]{1,0:T(8,128)(2,1)S(1)} collective-permute-done((bf16[48,6528]{1,0:T(8,128)(2,1)}, bf16[48,6528]{1,0:T(8,128)(2,1)S(1)}, u32[]{:S(2)}, u32[]{:S(2)}) %collective-permute-start.1) | collective-permute-done | bytes 626720 | tf_op jit(solution)/shard_map/ppermute | solution.py:764
  30.8 8.3 %collective-permute-done.2.refs_1_ = bf16[2,48,3200]{2,1,0:T(8,128)(2,1)S(1)} collective-permute-done((bf16[2,48,3200]{2,1,0:T(8,128)(2,1)S(1)}, bf16[2,48,3200]{2,1,0:T(8,128)(2,1)S(1)}, u32[]{:S(2)}, u32[]{:S(2)}) %collective-permute-start.2) | collective-permute-done | bytes 614432 | tf_op jit(solution)/shard_map/ppermute | solution.py:764
  58.6 15.0 %all_gather.6.refs_1_.refs_3_.refs_2_ = bf16[256,1536]{1,0:T(8,128)(2,1)S(1)} all-gather(bf16[64,1536]{1,0:T(8,128)(2,1)S(1)} %copy-done.44), channel_id=1, replica_groups=mesh['dp'=32,'tensor'=4] {'tensor'}, dimensions={0}, use_global_device_ids=true | all-gather | bytes 983040 | tf_op jit(solution)/shard_map/all_gather | solution.py:1184
  85.4 3.3 collective-permute-start.14
  90.3 9.5 %collective-permute-done.14.refs_11_.refs_13_.refs_10_.refs_6_ = bf16[4,48,1280]{2,1,0:T(8,128)(2,1)S(1)} collective-permute-done((bf16[4,48,1280]{2,1,0:T(8,128)(2,1)S(1)}, bf16[4,48,1280]{2,1,0:T(8,128)(2,1)S(1)}, u32[]{:S(2)}, u32[]{:S(2)}) %collective-permute-start.14) | collective-permute-done | bytes 491552 | tf_op jit(solution)/shard_map/ppermute | solution.py:764
  99.9 11.8 %scan_front.1 = (f32[272,1920]{1,0:T(8,128)}, f32[256,128]{1,0:T(8,128)S(1)}, f32[256,768]{1,0:T(8,128)S(1)}, f32[256,1024]{1,0:T(8,128)}, f32[256,128]{1,0:T(8,...) custom-call(s32[5]{0:T(128)S(1)} %stack.50.refs_0_, bf16[256,1536]{1,0:T(8,128)(2,1)S(1)} %copy-done.47, ...), custom_call_target="tpu_custom_call" | custom-call | flops 1711276032 | bytes 14106644 | tf_op jit(solution)/shard_map/scan_front/pallas_call | solution.py:75
  114.7 5.0 %all-to-all-start = ((f32[32,32,128]{2,1,0:T(8,128)}), f32[32,32,128]{2,1,0:T(8,128)S(1)}, u32[]{:S(2)}, u32[]{:S(2)}) async-start(f32[32,32,128]{2,1,0:T(8,128)} %get-tuple-element.155), calls=%async_computation | async-start | bytes 1048576 | tf_op jit(solution)/shard_map/all_to_all | solution.py:735
  119.7 3.4 join_mids.1
  131.9 33.9 %all_to_all.30 = f32[32,24,128]{2,1,0:T(8,128)S(1)} all-to-all(f32[32,24,128]{2,1,0:T(8,128)S(1)} %chain_states.2), channel_id=1, replica_groups=mesh['dp'=32,'tensor'=4] {'dp'}, dimensions={0} | all-to-all | bytes 786432 | tf_op jit(solution)/shard_map/all_to_all | solution.py:739
  165.9 7.0 %gate_front.1 = (bf16[1536,768]{1,0:T(8,128)(2,1)}, f32[256,768]{1,0:T(8,128)S(1)}, bf16[256,768]{1,0:T(8,128)(2,1)S(1)}, f32[128,1664]{1,0:T(8,128)S(1)}, f32[128,1664]{1,0:T(8,128)}) custom-call(s32[5]{0:T(128)S(1)} %stack.50.refs_0_, f32[256,768]{1,0:T(8,128)S(1)} %copy-done.41, f32[272,1920]{1,0:T(8,128)} %get-tuple-element.152.refs_2_.refs_5_.refs_0_, ...), custom_call_target="tpu_custom_call" | custom-call | flops 201326592 | bytes 17951764 | tf_op jit(solution)/shard_map/gate_front/pallas_call | solution.py:75
  173.0 3.5 collective-permute-start.18
  188.2 3.3 collective-permute-done.23.refs_2_.refs_7_
  193.7 10.7 %all_gather.7.refs_3_ = bf16[256,1536]{1,0:T(8,128)(2,1)} all-gather(bf16[64,1536]{1,0:T(8,128)(2,1)S(1)} %copy-done.92), channel_id=1, replica_groups=mesh['dp'=32,'tensor'=4] {'tensor'}, dimensions={0}, use_global_device_ids=true | all-gather | bytes 983040 | tf_op jit(solution)/shard_map/all_gather | solution.py:1185
  204.4 14.3 %experts_both.1 = (bf16[256,1536]{1,0:T(8,128)(2,1)S(1)}, bf16[256,1536]{1,0:T(8,128)(2,1)}, bf16[256,1280]{1,0:T(8,128)(2,1)S(1)}, bf16[256,2560]{1,0:T(8,128)(...) custom-call(s32[5]{0:T(128)S(1)} %stack.50.refs_0_, ...), custom_call_target="tpu_custom_call" | custom-call | flops 6039797760 | bytes 19398676 | tf_op jit(solution)/shard_map/experts_both/pallas_call | solution.py:75
  222.9 7.9 %term_products.2 = (bf16[384,1920]{1,0:T(8,128)(2,1)S(1)}, bf16[384,1920]{1,0:T(8,128)(2,1)}, bf16[384,1920]{1,0:T(8,128)(2,1)}, bf16[192,1920]{1,0:T(8,128)(2,1...) custom-call(s32[5]{0:T(128)S(1)} %stack.50.refs_0_, ...), custom_call_target="tpu_custom_call" | custom-call | flops 3019898880 | bytes 15335444 | tf_op jit(solution)/shard_map/term_products/pallas_call | solution.py:75
  238.3 10.0 %collective-permute-done.32.refs_2_ = bf16[128,1536]{1,0:T(8,128)(2,1)S(1)} collective-permute-done((bf16[128,1536]{1,0:T(8,128)(2,1)S(1)}, bf16[128,1536]{1,0:T(8,128)(2,1)S(1)}, u32[]{:S(2)}, u32[]{:S(2)}) %collective-permute-start.32) | collective-permute-done | bytes 393248 | tf_op jit(solution)/shard_map/ppermute | solution.py:745
  260.2 4.6 %all-to-all-start.2 = ((f32[32,32,128]{2,1,0:T(8,128)}), f32[32,32,128]{2,1,0:T(8,128)}, u32[]{:S(2)}, u32[]{:S(2)}) async-start(f32[32,32,128]{2,1,0:T(8,128)} %copy-done.59), calls=%async_computation.2 | async-start | bytes 1048576 | tf_op jit(solution)/shard_map/all_to_all | solution.py:735
  268.2 11.0 %collective-permute-done.30.refs_2_ = bf16[64,1536]{1,0:T(8,128)(2,1)S(1)} collective-permute-done((bf16[64,1536]{1,0:T(8,128)(2,1)S(1)}, bf16[64,1536]{1,0:T(8,128)(2,1)S(1)}, u32[]{:S(2)}, u32[]{:S(2)}) %collective-permute-start.30) | collective-permute-done | bytes 196640 | tf_op jit(solution)/shard_map/ppermute | solution.py:745
  283.6 5.2 %all-to-all-start.3 = ((f32[32,24,128]{2,1,0:T(8,128)}), f32[32,24,128]{2,1,0:T(8,128)}, u32[]{:S(2)}, u32[]{:S(2)}) async-start(f32[32,24,128]{2,1,0:T(8,128)} %copy-done.25), calls=%async_computation.3 | async-start | bytes 786432 | tf_op jit(solution)/shard_map/all_to_all | solution.py:739
  293.3 4.6 ring_add.3
  309.4 11.5 %scan_back.1 = (f32[256,768]{1,0:T(8,128)S(1)}, f32[256,256]{1,0:T(8,128)S(1)}, f32[16,1024]{1,0:T(8,128)S(1)}, bf16[256,128]{1,0:T(8,128)(2,1)S(1)}, f32[8,1024...) custom-call(f32[272,1920]{1,0:T(8,128)S(1)} %copy-done.4, ...), custom_call_target="tpu_custom_call" | custom-call | flops 603979776 | bytes 6360064 | tf_op jit(solution)/shard_map/scan_back/pallas_call | solution.py:75
  322.2 3.7 collective-permute-done.38.refs_2_.refs_6_
  333.9 4.7 %ring_total.1 = (bf16[384,1920]{1,0:T(8,128)(2,1)S(1)}, bf16[384,1920]{1,0:T(8,128)(2,1)S(1)}) custom-call(bf16[384,1920]{1,0:T(8,128)(2,1)S(1)} %copy-done.28, bf16[384,1920]{1,0:T(8,128)(2,1)} %collective-permute-done.34.refs_0_.refs_1_, bf16[384,1920]{1,0:T(8,128)(2,1)} %collective-permute-done.35.refs_1_.refs_2_, ...), custom_call_target="tpu_custom_call" | custom-call | bytes 14745600 | tf_op jit(solution)/shard_map/ring_total/pallas_call | solution.py:75
  338.7 5.7 %term_products.3 = (bf16[384,1280]{1,0:T(8,128)(2,1)S(1)}, bf16[384,1280]{1,0:T(8,128)(2,1)}, bf16[384,1280]{1,0:T(8,128)(2,1)}, bf16[192,1280]{1,0:T(8,128)(2,1...) custom-call(s32[5]{0:T(128)S(1)} %stack.50.refs_0_, ...), custom_call_target="tpu_custom_call" | custom-call | flops 2013265920 | bytes 12320788 | tf_op jit(solution)/shard_map/term_products/pallas_call | solution.py:75
  349.1 3.3 collective-permute-start.50
  352.5 5.4 %input_back.1 = (f32[128,1536]{1,0:T(8,128)S(1)}, bf16[128,1536]{1,0:T(8,128)(2,1)S(1)}, f32[1,1536]{1,0:T(1,128)S(1)}) custom-call(s32[5]{0:T(128)S(1)} %stack.50.refs_0_, bf16[256,1792]{1,0:T(8,128)(2,1)S(1)} %get-tuple-element.211.refs_1_, bf16[256,1536]{1,0:T(8,128)(2,1)S(1)} %all_gather.6.refs_1_.refs_3_.refs_2_, ...), custom_call_target="tpu_custom_call" | custom-call | flops 1509949440 | bytes 11147284 | tf_op jit(solution)/shard_map/input_back/pallas_call | solution.py:75
  363.5 5.7 %collective-permute-done.46.refs_2_ = bf16[64,1536]{1,0:T(8,128)(2,1)S(1)} collective-permute-done((bf16[64,1536]{1,0:T(8,128)(2,1)S(1)}, bf16[64,1536]{1,0:T(8,128)(2,1)S(1)}, u32[]{:S(2)}, u32[]{:S(2)}) %collective-permute-start.46) | collective-permute-done | bytes 196640 | tf_op jit(solution)/shard_map/ppermute | solution.py:745
  381.0 11.7 %all_to_all.31.refs_0_ = f32[32,8,128]{2,1,0:T(8,128)S(1)} all-to-all(f32[32,8,128]{2,1,0:T(8,128)S(1)} %small_table.1), channel_id=1, replica_groups=mesh['dp'=32,'tensor'=4] {'dp'}, dimensions={0} | all-to-all | bytes 262144 | tf_op jit(solution)/shard_map/all_to_all | solution.py:1447
  400.8 22.3 %all_to_all.32.refs_0_.refs_8_ = f32[128,8,128]{2,1,0:T(8,128)S(1)} all-to-all(f32[128,8,128]{2,1,0:T(8,128)S(1)} %small_sum.1.refs_13_), channel_id=1, replica_groups=mesh['dp'=32,'tensor'=4] {'dp','tensor'}, dimensions={0} | all-to-all | bytes 1048576 | tf_op jit(solution)/shard_map/all_to_all | solution.py:1451
  428.8 3.5 collective-permute-done.59.refs_4_
  436.5 11.8 %collective-permute-done.63.refs_1_ = bf16[48,6400]{1,0:T(8,128)(2,1)S(1)} collective-permute-done((bf16[48,6400]{1,0:T(8,128)(2,1)S(1)}, bf16[48,6400]{1,0:T(8,128)(2,1)S(1)}, u32[]{:S(2)}, u32[]{:S(2)}) %collective-permute-start.63) | collective-permute-done | bytes 614432 | tf_op jit(solution)/shard_map/ppermute | solution.py:764
  449.3 3.6 collective-permute-start.64
  (403 shorter events, 181.0 us)
Async XLA Ops:
  52.4 26.9 %collective-permute-start.12 = (bf16[8,48,1408]{2,1,0:T(8,128)(2,1)}, bf16[8,48,1408]{2,1,0:T(8,128)(2,1)S(1)}, u32[]{:S(2)}, u32[]{:S(2)}) collective-permute-start(bf16[8,48,1408]{2,1,0:T(8,128)(2,1)} %slice_dynamic-update-slice_fusion.4.refs_13_.refs_15_.refs_12_.refs_8_), channel_id=1, source_target_pairs={{0,4},{4,8},{8,12},{12,0},{16,20},{20,24},{24,28},{28,16},{32,36},... | collective-permute-start | bytes 3244040 | tf_op jit(solution)/shard_map/ppermute | solution.py:764
  52.4 26.9 %collective-permute-start.13 = (bf16[8,48,1408]{2,1,0:T(8,128)(2,1)}, bf16[8,48,1408]{2,1,0:T(8,128)(2,1)}, u32[]{:S(2)}, u32[]{:S(2)}) collective-permute-start(bf16[8,48,1408]{2,1,0:T(8,128)(2,1)} %slice_dynamic-update-slice_fusion.4.refs_13_.refs_15_.refs_12_.refs_8_), channel_id=1, source_target_pairs={{0,12},{4,0},{8,4},{12,8},{16,28},{20,16},{24,20},{28,24},{32,44},... | collective-permute-start | bytes 3244040 | tf_op jit(solution)/shard_map/ppermute | solution.py:764
  55.8 23.5 %collective-permute-start.6 = (bf16[8,48,1280]{2,1,0:T(8,128)(2,1)}, bf16[8,48,1280]{2,1,0:T(8,128)(2,1)S(1)}, u32[]{:S(2)}, u32[]{:S(2)}) collective-permute-start(bf16[8,48,1280]{2,1,0:T(8,128)(2,1)} %slice_dynamic-update-slice_fusion.6.refs_8_.refs_10_.refs_7_.refs_3_), channel_id=1, source_target_pairs={{0,32},{4,36},{8,40},{12,44},{16,48},{20,52},{24,56},{28,60},{32,6... | collective-permute-start | bytes 2949128 | tf_op jit(solution)/shard_map/ppermute | solution.py:764
  56.2 23.1 %collective-permute-start.7 = (bf16[8,48,1280]{2,1,0:T(8,128)(2,1)}, bf16[8,48,1280]{2,1,0:T(8,128)(2,1)}, u32[]{:S(2)}, u32[]{:S(2)}) collective-permute-start(bf16[8,48,1280]{2,1,0:T(8,128)(2,1)} %slice_dynamic-update-slice_fusion.6.refs_8_.refs_10_.refs_7_.refs_3_), channel_id=1, source_target_pairs={{0,96},{4,100},{8,104},{12,108},{16,112},{20,116},{24,120},{28,124... | collective-permute-start | bytes 2949128 | tf_op jit(solution)/shard_map/ppermute | solution.py:764
  81.5 18.3 %collective-permute-start.16 = (bf16[4,48,1408]{2,1,0:T(8,128)(2,1)S(1)}, bf16[4,48,1408]{2,1,0:T(8,128)(2,1)S(1)}, u32[]{:S(2)}, u32[]{:S(2)}) collective-permute-start(bf16[4,48,1408]{2,1,0:T(8,128)(2,1)S(1)} %get-tuple-element.149), channel_id=1, source_target_pairs={{0,4},{4,8},{8,12},{12,0},{16,20},{20,24},{24,28},{28,16},{32,36},... | collective-permute-start | bytes 1622024 | tf_op jit(solution)/shard_map/ppermute | solution.py:764
  123.1 53.3 %collective-permute-start.19 = (bf16[8,48,1920]{2,1,0:T(8,128)(2,1)}, bf16[8,48,1920]{2,1,0:T(8,128)(2,1)}, u32[]{:S(2)}, u32[]{:S(2)}) collective-permute-start(bf16[8,48,1920]{2,1,0:T(8,128)(2,1)} %get-tuple-element.156.refs_1_.refs_5_), channel_id=1, source_target_pairs={{0,32},{4,36},{8,40},{12,44},{16,48},{20,52},{24,56},{28,60},{32,6... | collective-permute-start | bytes 4423688 | tf_op jit(solution)/shard_map/ppermute | solution.py:764
  124.4 52.0 %collective-permute-start.20 = (bf16[8,48,1920]{2,1,0:T(8,128)(2,1)}, bf16[8,48,1920]{2,1,0:T(8,128)(2,1)}, u32[]{:S(2)}, u32[]{:S(2)}) collective-permute-start(bf16[8,48,1920]{2,1,0:T(8,128)(2,1)} %get-tuple-element.156.refs_1_.refs_5_), channel_id=1, source_target_pairs={{0,96},{4,100},{8,104},{12,108},{16,112},{20,116},{24,120},{28,124... | collective-permute-start | bytes 4423688 | tf_op jit(solution)/shard_map/ppermute | solution.py:764
  125.9 50.6 %collective-permute-start.21 = (bf16[8,48,1920]{2,1,0:T(8,128)(2,1)}, bf16[8,48,1920]{2,1,0:T(8,128)(2,1)}, u32[]{:S(2)}, u32[]{:S(2)}) collective-permute-start(bf16[8,48,1920]{2,1,0:T(8,128)(2,1)} %get-tuple-element.157.refs_2_.refs_10_), channel_id=1, source_target_pairs={{0,4},{4,8},{8,12},{12,0},{16,20},{20,24},{24,28},{28,16},{32,36},... | collective-permute-start | bytes 4423688 | tf_op jit(solution)/shard_map/ppermute | solution.py:764
  127.2 49.3 %collective-permute-start.22 = (bf16[8,48,1920]{2,1,0:T(8,128)(2,1)}, bf16[8,48,1920]{2,1,0:T(8,128)(2,1)}, u32[]{:S(2)}, u32[]{:S(2)}) collective-permute-start(bf16[8,48,1920]{2,1,0:T(8,128)(2,1)} %get-tuple-element.157.refs_2_.refs_10_), channel_id=1, source_target_pairs={{0,12},{4,0},{8,4},{12,8},{16,28},{20,16},{24,20},{28,24},{32,44},... | collective-permute-start | bytes 4423688 | tf_op jit(solution)/shard_map/ppermute | solution.py:764
  182.7 21.6 %collective-permute-start.25 = (bf16[4,48,1920]{2,1,0:T(8,128)(2,1)S(1)}, bf16[4,48,1920]{2,1,0:T(8,128)(2,1)S(1)}, u32[]{:S(2)}, u32[]{:S(2)}) collective-permute-start(bf16[4,48,1920]{2,1,0:T(8,128)(2,1)S(1)} %get-tuple-element.162), channel_id=1, source_target_pairs={{0,32},{4,36},{8,40},{12,44},{16,48},{20,52},{24,56},{28,60},{32,6... | collective-permute-start | bytes 2211848 | tf_op jit(solution)/shard_map/ppermute | solution.py:764
  183.0 21.3 %collective-permute-start.26 = (bf16[4,48,1920]{2,1,0:T(8,128)(2,1)S(1)}, bf16[4,48,1920]{2,1,0:T(8,128)(2,1)S(1)}, u32[]{:S(2)}, u32[]{:S(2)}) collective-permute-start(bf16[4,48,1920]{2,1,0:T(8,128)(2,1)S(1)} %get-tuple-element.163), channel_id=1, source_target_pairs={{0,96},{4,100},{8,104},{12,108},{16,112},{20,116},{24,120},{28,124... | collective-permute-start | bytes 2211848 | tf_op jit(solution)/shard_map/ppermute | solution.py:764
  185.5 18.9 %collective-permute-start.27 = (bf16[4,48,1920]{2,1,0:T(8,128)(2,1)S(1)}, bf16[4,48,1920]{2,1,0:T(8,128)(2,1)S(1)}, u32[]{:S(2)}, u32[]{:S(2)}) collective-permute-start(bf16[4,48,1920]{2,1,0:T(8,128)(2,1)S(1)} %get-tuple-element.164), channel_id=1, source_target_pairs={{0,4},{4,8},{8,12},{12,0},{16,20},{20,24},{24,28},{28,16},{32,36},... | collective-permute-start | bytes 2211848 | tf_op jit(solution)/shard_map/ppermute | solution.py:764
  185.9 18.4 %collective-permute-start.28 = (bf16[4,48,1920]{2,1,0:T(8,128)(2,1)S(1)}, bf16[4,48,1920]{2,1,0:T(8,128)(2,1)S(1)}, u32[]{:S(2)}, u32[]{:S(2)}) collective-permute-start(bf16[4,48,1920]{2,1,0:T(8,128)(2,1)S(1)} %get-tuple-element.165), channel_id=1, source_target_pairs={{0,12},{4,0},{8,4},{12,8},{16,28},{20,16},{24,20},{28,24},{32,44},... | collective-permute-start | bytes 2211848 | tf_op jit(solution)/shard_map/ppermute | solution.py:764
  218.7 18.4 %collective-permute-start.31 = (bf16[128,1536]{1,0:T(8,128)(2,1)S(1)}, bf16[128,1536]{1,0:T(8,128)(2,1)S(1)}, u32[]{:S(2)}, u32[]{:S(2)}) collective-permute-start(bf16[128,1536]{1,0:T(8,128)(2,1)S(1)} %get-tuple-element.172), channel_id=1, source_target_pairs={{0,1},{1,0},{2,3},{3,2},{4,5},{5,4},{6,7},{7,6},{8,9},{9,8},{10,11... | collective-permute-start | bytes 1179656 | tf_op jit(solution)/shard_map/ppermute | solution.py:745
  231.7 57.1 %collective-permute-start.34 = (bf16[384,1920]{1,0:T(8,128)(2,1)}, bf16[384,1920]{1,0:T(8,128)(2,1)}, u32[]{:S(2)}, u32[]{:S(2)}) collective-permute-start(bf16[384,1920]{1,0:T(8,128)(2,1)} %get-tuple-element.189), channel_id=1, source_target_pairs={{0,32},{4,36},{8,40},{12,44},{16,48},{20,52},{24,56},{28,60},{32,6... | collective-permute-start | bytes 4423688 | tf_op jit(solution)/shard_map/ppermute | solution.py:764
  231.8 57.0 %collective-permute-start.35 = (bf16[384,1920]{1,0:T(8,128)(2,1)}, bf16[384,1920]{1,0:T(8,128)(2,1)}, u32[]{:S(2)}, u32[]{:S(2)}) collective-permute-start(bf16[384,1920]{1,0:T(8,128)(2,1)} %get-tuple-element.190), channel_id=1, source_target_pairs={{0,96},{4,100},{8,104},{12,108},{16,112},{20,116},{24,120},{28,124... | collective-permute-start | bytes 4423688 | tf_op jit(solution)/shard_map/ppermute | solution.py:764
  234.5 54.4 %collective-permute-start.36 = (bf16[384,1920]{1,0:T(8,128)(2,1)}, bf16[384,1920]{1,0:T(8,128)(2,1)}, u32[]{:S(2)}, u32[]{:S(2)}) collective-permute-start(bf16[384,1920]{1,0:T(8,128)(2,1)} %get-tuple-element.193), channel_id=1, source_target_pairs={{0,4},{4,8},{8,12},{12,0},{16,20},{20,24},{24,28},{28,16},{32,36},... | collective-permute-start | bytes 4423688 | tf_op jit(solution)/shard_map/ppermute | solution.py:764
  234.5 54.4 %collective-permute-start.37 = (bf16[384,1920]{1,0:T(8,128)(2,1)}, bf16[384,1920]{1,0:T(8,128)(2,1)}, u32[]{:S(2)}, u32[]{:S(2)}) collective-permute-start(bf16[384,1920]{1,0:T(8,128)(2,1)} %get-tuple-element.194), channel_id=1, source_target_pairs={{0,12},{4,0},{8,4},{12,8},{16,28},{20,16},{24,20},{28,24},{32,44},... | collective-permute-start | bytes 4423688 | tf_op jit(solution)/shard_map/ppermute | solution.py:764
  260.2 20.4 %all-to-all-start.2 = ((f32[32,32,128]{2,1,0:T(8,128)}), f32[32,32,128]{2,1,0:T(8,128)}, u32[]{:S(2)}, u32[]{:S(2)}) async-start(f32[32,32,128]{2,1,0:T(8,128)} %copy-done.59), calls=%async_computation.2 | async-start | bytes 1048576 | tf_op jit(solution)/shard_map/all_to_all | solution.py:735
  283.6 19.7 %all-to-all-start.3 = ((f32[32,24,128]{2,1,0:T(8,128)}), f32[32,24,128]{2,1,0:T(8,128)}, u32[]{:S(2)}, u32[]{:S(2)}) async-start(f32[32,24,128]{2,1,0:T(8,128)} %copy-done.25), calls=%async_computation.3 | async-start | bytes 786432 | tf_op jit(solution)/shard_map/all_to_all | solution.py:739
  297.9 35.9 %collective-permute-start.41 = (bf16[192,1920]{1,0:T(8,128)(2,1)}, bf16[192,1920]{1,0:T(8,128)(2,1)}, u32[]{:S(2)}, u32[]{:S(2)}) collective-permute-start(bf16[192,1920]{1,0:T(8,128)(2,1)} %get-tuple-element.197.refs_12_), channel_id=1, source_target_pairs={{0,32},{4,36},{8,40},{12,44},{16,48},{20,52},{24,56},{28,60},{32,6... | collective-permute-start | bytes 2211848 | tf_op jit(solution)/shard_map/ppermute | solution.py:764
  299.3 34.6 %collective-permute-start.42 = (bf16[192,1920]{1,0:T(8,128)(2,1)}, bf16[192,1920]{1,0:T(8,128)(2,1)}, u32[]{:S(2)}, u32[]{:S(2)}) collective-permute-start(bf16[192,1920]{1,0:T(8,128)(2,1)} %get-tuple-element.198.refs_13_), channel_id=1, source_target_pairs={{0,96},{4,100},{8,104},{12,108},{16,112},{20,116},{24,120},{28,124... | collective-permute-start | bytes 2211848 | tf_op jit(solution)/shard_map/ppermute | solution.py:764
  300.6 33.2 %collective-permute-start.43 = (bf16[192,1920]{1,0:T(8,128)(2,1)}, bf16[192,1920]{1,0:T(8,128)(2,1)}, u32[]{:S(2)}, u32[]{:S(2)}) collective-permute-start(bf16[192,1920]{1,0:T(8,128)(2,1)} %get-tuple-element.199.refs_14_), channel_id=1, source_target_pairs={{0,4},{4,8},{8,12},{12,0},{16,20},{20,24},{24,28},{28,16},{32,36},... | collective-permute-start | bytes 2211848 | tf_op jit(solution)/shard_map/ppermute | solution.py:764
  302.0 31.9 %collective-permute-start.44 = (bf16[192,1920]{1,0:T(8,128)(2,1)}, bf16[192,1920]{1,0:T(8,128)(2,1)}, u32[]{:S(2)}, u32[]{:S(2)}) collective-permute-start(bf16[192,1920]{1,0:T(8,128)(2,1)} %get-tuple-element.200.refs_15_), channel_id=1, source_target_pairs={{0,12},{4,0},{8,4},{12,8},{16,28},{20,16},{24,20},{28,24},{32,44},... | collective-permute-start | bytes 2211848 | tf_op jit(solution)/shard_map/ppermute | solution.py:764
  346.0 24.6 %collective-permute-start.47 = (bf16[384,1280]{1,0:T(8,128)(2,1)}, bf16[384,1280]{1,0:T(8,128)(2,1)S(1)}, u32[]{:S(2)}, u32[]{:S(2)}) collective-permute-start(bf16[384,1280]{1,0:T(8,128)(2,1)} %get-tuple-element.225), channel_id=1, source_target_pairs={{0,32},{4,36},{8,40},{12,44},{16,48},{20,52},{24,56},{28,60},{32,6... | collective-permute-start | bytes 2949128 | tf_op jit(solution)/shard_map/ppermute | solution.py:764
  347.7 23.0 %collective-permute-start.48 = (bf16[384,1280]{1,0:T(8,128)(2,1)}, bf16[384,1280]{1,0:T(8,128)(2,1)S(1)}, u32[]{:S(2)}, u32[]{:S(2)}) collective-permute-start(bf16[384,1280]{1,0:T(8,128)(2,1)} %get-tuple-element.226), channel_id=1, source_target_pairs={{0,96},{4,100},{8,104},{12,108},{16,112},{20,116},{24,120},{28,124... | collective-permute-start | bytes 2949128 | tf_op jit(solution)/shard_map/ppermute | solution.py:764
  348.7 24.8 %collective-permute-start.49 = (bf16[384,1280]{1,0:T(8,128)(2,1)}, bf16[384,1280]{1,0:T(8,128)(2,1)S(1)}, u32[]{:S(2)}, u32[]{:S(2)}) collective-permute-start(bf16[384,1280]{1,0:T(8,128)(2,1)} %get-tuple-element.229), channel_id=1, source_target_pairs={{0,4},{4,8},{8,12},{12,0},{16,20},{20,24},{24,28},{28,16},{32,36},... | collective-permute-start | bytes 2949128 | tf_op jit(solution)/shard_map/ppermute | solution.py:764
  349.1 24.4 %collective-permute-start.50 = (bf16[384,1280]{1,0:T(8,128)(2,1)}, bf16[384,1280]{1,0:T(8,128)(2,1)S(1)}, u32[]{:S(2)}, u32[]{:S(2)}) collective-permute-start(bf16[384,1280]{1,0:T(8,128)(2,1)} %get-tuple-element.230), channel_id=1, source_target_pairs={{0,12},{4,0},{8,4},{12,8},{16,28},{20,16},{24,20},{28,24},{32,44},... | collective-permute-start | bytes 2949128 | tf_op jit(solution)/shard_map/ppermute | solution.py:764
  395.4 27.7 %collective-permute-start.55 = (bf16[96,3200]{1,0:T(8,128)(2,1)S(1)}, bf16[96,3200]{1,0:T(8,128)(2,1)S(1)}, u32[]{:S(2)}, u32[]{:S(2)}) collective-permute-start(bf16[96,3200]{1,0:T(8,128)(2,1)S(1)} %get-tuple-element.239), channel_id=1, source_target_pairs={{0,4},{4,8},{8,12},{12,0},{16,20},{20,24},{24,28},{28,16},{32,36},... | collective-permute-start | bytes 1843208 | tf_op jit(solution)/shard_map/ppermute | solution.py:764
  395.9 27.2 %collective-permute-start.56 = (bf16[96,3200]{1,0:T(8,128)(2,1)S(1)}, bf16[96,3200]{1,0:T(8,128)(2,1)S(1)}, u32[]{:S(2)}, u32[]{:S(2)}) collective-permute-start(bf16[96,3200]{1,0:T(8,128)(2,1)S(1)} %get-tuple-element.240), channel_id=1, source_target_pairs={{0,12},{4,0},{8,4},{12,8},{16,28},{20,16},{24,20},{28,24},{32,44},... | collective-permute-start | bytes 1843208 | tf_op jit(solution)/shard_map/ppermute | solution.py:764
  398.2 24.9 %collective-permute-start.57 = (bf16[96,3200]{1,0:T(8,128)(2,1)S(1)}, bf16[96,3200]{1,0:T(8,128)(2,1)S(1)}, u32[]{:S(2)}, u32[]{:S(2)}) collective-permute-start(bf16[96,3200]{1,0:T(8,128)(2,1)S(1)} %get-tuple-element.243), channel_id=1, source_target_pairs={{0,32},{4,36},{8,40},{12,44},{16,48},{20,52},{24,56},{28,60},{32,6... | collective-permute-start | bytes 1843208 | tf_op jit(solution)/shard_map/ppermute | solution.py:764
  398.7 24.4 %collective-permute-start.58 = (bf16[96,3200]{1,0:T(8,128)(2,1)S(1)}, bf16[96,3200]{1,0:T(8,128)(2,1)S(1)}, u32[]{:S(2)}, u32[]{:S(2)}) collective-permute-start(bf16[96,3200]{1,0:T(8,128)(2,1)S(1)} %get-tuple-element.244), channel_id=1, source_target_pairs={{0,96},{4,100},{8,104},{12,108},{16,112},{20,116},{24,120},{28,124... | collective-permute-start | bytes 1843208 | tf_op jit(solution)/shard_map/ppermute | solution.py:764
  (138 other events, 1669.6 us)

commit v3 on v2

--- a/solution.py
+++ b/solution.py
@@ -162,7 +162,12 @@
             if columns % LANES:
                 out[:, at : at + LANES] = jnp.zeros((out.shape[0], LANES), bf16)
             ref = ins[arg]
-            value = ref[:, first : first + columns] if lead is None else ref[lead, :, first : first + columns]
+            if lead is None:
+                value = ref[:, first : first + columns]
+            elif ref.shape[0] == out.shape[0]:
+                value = ref[:, lead, first : first + columns]
+            else:
+                value = ref[lead, :, first : first + columns]
             out[:, at : at + columns] = value
 
     return kernel
@@ -174,7 +179,7 @@
     for arg, value in enumerate(args):
         if arg == in_count:
             group, at = 1, 0
-        for lead in range(value.shape[0]) if len(value.shape) == 3 else (None,):
+        for lead in range(min(value.shape[:2])) if len(value.shape) == 3 else (None,):
             for first in range(0, value.shape[-1], LANES):
                 columns = min(LANES, value.shape[-1] - first)
                 entries.append((group, at, arg, lead, first, columns))
@@ -267,7 +272,7 @@
             for head in (2 * pair, 2 * pair + 1):
                 gaps = cum[:, head : head + 1] - turned[head : head + 1, :]
                 weights = jnp.exp(jnp.where(keep, gaps, -jnp.inf)) * inner_cb
-                parts.append(dot_both(weights, scaled))
+                parts.append(dot_left(weights, scaled))
             y_out[:, at : at + LANES] = (
                 jnp.where(left, parts[0], parts[1]) + skip[:, at : at + LANES] * x_pair
             )
@@ -370,7 +375,7 @@
         pieces, refs = refs[: 2 * len(HALVED)], refs[2 * len(HALVED) :]
         (
             post, cot, act_out, dpre_out, out_mine, out_theirs, dpost_mine, dpost_theirs,
-            weights, shares, done,
+            weights, shares, gates, ups, done,
         ) = refs
         copies = load_blocks(pieces, weights, done, here, ranges, shard, HALVED)
         core = here[3]
@@ -387,12 +392,22 @@
             shares[half + index * quarter : half + (index + 1) * quarter, :] = share[
                 rows_at(2 * index + 1 - core, quarter), :
             ]
-        wait_all(copies)
         wide = 2 * LANES
         left = ids((2 * half, wide), 1) < ffe
+        first = ranges[0][3]
+        wait_all(copies[: len(copies) // 2])
         for at in range(0, hidden, wide):
-            gate = dot(post[...], weights[:, at : at + wide])
-            up = dot(post[...], weights[:, hidden + at : hidden + at + wide])
+            gates[:, at : at + wide] = dot(post[...], weights[:, at : at + wide])
+        for at in range(0, hidden, wide):
+            if hidden + at + wide <= first:
+                ups[:, at : at + wide] = dot(post[...], weights[:, hidden + at : hidden + at + wide])
+        wait_all(copies[len(copies) // 2 :])
+        for at in range(0, hidden, wide):
+            gate = gates[:, at : at + wide]
+            if hidden + at + wide <= first:
+                up = ups[:, at : at + wide]
+            else:
+                up = dot(post[...], weights[:, hidden + at : hidden + at + wide])
             d_act = dot(cot[...], weights[:, 2 * hidden + at : 2 * hidden + at + wide])
             sigma = jax.nn.sigmoid(gate)
             silu = gate * sigma
@@ -655,7 +670,7 @@
                 gaps = cum[:, head : head + 1] - turned[head : head + 1, :]
                 decay = jnp.exp(jnp.where(keep, gaps, -jnp.inf))
                 weights = decay * inner_cb
-                d_weights = dot_both(jnp.where(mine, d_y, 0.0), scaled, NT)
+                d_weights = dot_left(jnp.where(mine, d_y, 0.0), scaled, NT)
                 d_cb = d_cb + d_weights * decay
                 flow = d_weights * weights
                 d_cum = d_cum + jnp.where(lane == head, jnp.sum(flow, 1, keepdims=True), 0.0)
@@ -1019,7 +1034,10 @@
         for out, entries in zip(outs, plan, strict=True):
             for lead, first, at, columns in entries:
                 value = mine[:, at : at + columns] + got[:, at : at + columns].astype(f32)
-                if lead is None:
+                if lead is None and len(out.shape) == 3:
+                    side, begin = first // out.shape[2], first % out.shape[2]
+                    out[:, side, begin : begin + columns] = value
+                elif lead is None:
                     out[:, first : first + columns] = value
                 else:
                     out[lead, :, first : first + columns] = value
@@ -1159,8 +1177,8 @@
     wide_in = 2 * inner + 2 * state + LANES
 
     shards = [
-        w_zx.reshape(shard, 2 * inner),
-        w_bc.reshape(shard, 2 * state),
+        w_zx,
+        w_bc,
         w_dt,
         w_out.T,
         exp_gate,
@@ -1309,7 +1327,9 @@
         scratch=[
             pltpu.VMEM((model_dim, 3 * hidden), bf16),
             pltpu.VMEM((block_rows, LANES), f32),
-            pltpu.SemaphoreType.DMA((128,)),
+            pltpu.VMEM((block_rows, hidden), f32),
+            pltpu.VMEM((block_rows, hidden), f32),
+            pltpu.SemaphoreType.DMA((64,)),
         ],
     )
     ffn_split = (3 * hidden) // 256 * LANES
@@ -1361,7 +1381,7 @@
         small=(0,),
     )[0]
 
-    leaving = exchange_states(d_enter, size, "dp", True, block_out)
+    leaving = exchange_states(d_enter, size, "dp", True)
     ffn_widths = widths_of(ffn_plan)
     ffn_added = ring_added(ffn_sent, ffn_terms, ffn_widths, 4 * shard)
     d_x, d_bc, tail, d_dt, grad_taps, grad_heads, grad_skip = kernel_call(
@@ -1445,7 +1465,7 @@
         scratch=[pltpu.VMEM((dp_count * EACH, LANES), f32)],
     )[0]
     table = lax.all_to_all(table, "dp", 0, 0, tiled=True)
-    mix_rings = ring_pass(mix_sent, mix_terms, mix_widths, "xy", 4 * shard, grad_tokens)
+    mix_rings = ring_pass(mix_sent, mix_terms, mix_widths, "xy", 4 * shard, (grad_tokens, block_out))
     devices = dp_count * tensor_count
     table = kernel_call(small_sum(), [shape_of((devices, SUB, LANES))], table)[0]
     table_end = lax.all_to_all(table, ("dp", "tensor"), 0, 0, tiled=True)
@@ -1464,7 +1484,15 @@
         scratch=[pltpu.VMEM((dp_count * EACH, LANES), f32)],
     )
     norm_sum, post_sum, taps_x, taps_bc, gain_sum, skip_sum, head_sums = small
-    head_sums = head_sums.reshape(2, tensor_count, LANES)[:, :, :heads].reshape(2, -1)
+    head_grads = head_sums.reshape(2, tensor_count, LANES)[:, :, :heads].reshape(2, -1)
+    small_outs = (
+        norm_sum[0],
+        post_sum[0],
+        head_grads[0],
+        head_grads[1],
+        jnp.sum(skip_sum.reshape(head_total, head_dim), 1),
+        gain_sum[0],
+    )
     widths = [one + two for one, two in zip(ffn_widths, mix_widths, strict=True)]
     chunks = kernel_call(
         ring_fold(shard), chunk_shapes(shard, widths), here, *ffn_totals, *mix_rings,
@@ -1513,7 +1541,7 @@
     grad_zx, grad_dt, bc_half, grad_out, grad_eg, grad_eu, grad_ed, grad_sg, grad_su, grad_sd = kernel_call(
         grad_blocks(out_plan, shard),
         [
-            shape_of((shard, 2 * inner)),
+            shape_of((shard, 2, inner)),
             shape_of((shard, LANES)),
             shape_of((shard, state)),
             shape_of((shard, inner)),
@@ -1521,24 +1549,25 @@
             *[shape_of((shard, ffs))] * 3,
         ],
         mine, shift(sent, "z", 1),
+        wait=small_outs,
     )
     bc_far = other(bc_half, 1)
     grad_bc = jnp.stack([jnp.where(core == 0, bc_half, bc_far), jnp.where(core == 0, bc_far, bc_half)], 1)
     return (
         block_out,
         grad_tokens,
-        norm_sum[0],
-        grad_zx.reshape(shard, 2, inner),
+        small_outs[0],
+        grad_zx,
         grad_bc,
         grad_dt[:, :heads],
         taps_x,
         taps_bc.reshape(conv_taps, 2, state),
-        head_sums[0],
-        head_sums[1],
-        jnp.sum(skip_sum.reshape(head_total, head_dim), 1),
-        gain_sum[0],
+        small_outs[2],
+        small_outs[3],
+        small_outs[4],
+        small_outs[5],
         grad_out.T,
-        post_sum[0],
+        small_outs[1],
         grad_eg,
         grad_eu,
         grad_ed.transpose(0, 2, 1),

time: 469 us -> 457 us (0.974)
  blocking collectives: 93.5 us -> 110 us
  waiting for transfers between devices: 92.6 us -> 79.7 us
  local copies, waits for them, and re-layouts: 48.5 us -> 42.2 us
  starting transfers between devices: 116 us -> 111 us
    all_to_all x0 -> x1, blocking collectives: none -> 17.3 us  [exchange_states(): parts = lax.all_to_all(sent, axis, 0, 0, tiled=True)]
    ppermute x13, waiting for transfers between devices: 35.9 us -> 27.6 us  [other(): lax.ppermute(value, 'tensor', [(rank, rank ^ bit) for rank in range(count)])]
    all_to_all x2 -> x1, starting transfers between devices: 9.62 us -> 5.01 us  [exchange_states(): parts = lax.all_to_all(sent, axis, 0, 0, tiled=True)]
    unnamed x216 -> x232, local copies, waits for them, and re-layouts: 40.3 us -> 36 us
  transfers between devices with their start and end apart: 68 -> 67, of which waited for: 18 -> 17; matrix products, arithmetic and copies ran while one was open for 4% -> 3% of each run, Pallas kernels for 13% -> 14%
where the time goes in v3:
time: 457 us; the launch traced here: 448 us
  starting transfers between devices  111 us (24%)
  blocking collectives  110 us (24%)
  Pallas kernels  99.5 us (22%)
  waiting for transfers between devices  79.7 us (17%)
  local copies, waits for them, and re-layouts  42.2 us (9%)
    pallas_call x35, Pallas kernels, kernel_call(): pl.pallas_call(body_of, name=kernel.__qualname__.split('.')[0], out_shape...  99.5 us
    ppermute x50, starting transfers between devices, shift(): return lax.ppermute(value, 'dp', pairs)  72.2 us
    ppermute x50, waiting for transfers between devices, shift(): return lax.ppermute(value, 'dp', pairs)  48.2 us
    unnamed x232, local copies, waits for them, and re-layouts  36 us
    all_to_all x1, blocking collectives, exchange_states(): back = lax.all_to_all(carried, axis, 0, 0, tiled=True)  33.9 us
    ppermute x13, waiting for transfers between devices, other(): lax.ppermute(value, 'tensor', [(rank, rank ^ bit) for rank in range(count)])  27.6 us
    ppermute x13, starting transfers between devices, other(): lax.ppermute(value, 'tensor', [(rank, rank ^ bit) for rank in range(count)])  26.8 us
    all_to_all x1, blocking collectives, body(): table_end = lax.all_to_all(table, ('dp', 'tensor'), 0, 0, tiled=True)  22.2 us
  transfers between devices with their start and end apart: 67, of which 17 were waited for; matrix products, arithmetic and copies ran while one was open for 3% of the time, Pallas kernels for 14%

profile of v3, /device:TPU:1, one launch (start us, length us, event | category | flops | bytes accessed | tf_op | source)
XLA Modules:
  0.0 448.5 jit_solution(3868500696729649848)
XLA Ops:
  9.0 12.0 %collective-permute-done.1 = bf16[48,6528]{1,0:T(8,128)(2,1)S(1)} collective-permute-done((bf16[48,6528]{1,0:T(8,128)(2,1)}, bf16[48,6528]{1,0:T(8,128)(2,1)S(1)}, u32[]{:S(2)}, u32[]{:S(2)}) %collective-permute-start.1) | collective-permute-done | bytes 626720 | tf_op jit(solution)/shard_map/ppermute | solution.py:779
  28.3 8.3 %collective-permute-done.2.refs_1_ = bf16[2,48,3200]{2,1,0:T(8,128)(2,1)S(1)} collective-permute-done((bf16[2,48,3200]{2,1,0:T(8,128)(2,1)S(1)}, bf16[2,48,3200]{2,1,0:T(8,128)(2,1)S(1)}, u32[]{:S(2)}, u32[]{:S(2)}) %collective-permute-start.2) | collective-permute-done | bytes 614432 | tf_op jit(solution)/shard_map/ppermute | solution.py:779
  56.1 15.0 %all_gather.6.refs_1_.refs_3_.refs_2_ = bf16[256,1536]{1,0:T(8,128)(2,1)S(1)} all-gather(bf16[64,1536]{1,0:T(8,128)(2,1)S(1)} %copy-done.44), channel_id=1, replica_groups=mesh['dp'=32,'tensor'=4] {'tensor'}, dimensions={0}, use_global_device_ids=true | all-gather | bytes 983040 | tf_op jit(solution)/shard_map/all_gather | solution.py:1202
  87.9 9.5 %collective-permute-done.14.refs_11_.refs_13_.refs_10_.refs_6_ = bf16[4,48,1280]{2,1,0:T(8,128)(2,1)S(1)} collective-permute-done((bf16[4,48,1280]{2,1,0:T(8,128)(2,1)S(1)}, bf16[4,48,1280]{2,1,0:T(8,128)(2,1)S(1)}, u32[]{:S(2)}, u32[]{:S(2)}) %collective-permute-start.14) | collective-permute-done | bytes 491552 | tf_op jit(solution)/shard_map/ppermute | solution.py:779
  97.5 11.3 %scan_front.1 = (f32[272,1920]{1,0:T(8,128)}, f32[256,128]{1,0:T(8,128)S(1)}, f32[256,768]{1,0:T(8,128)S(1)}, f32[256,1024]{1,0:T(8,128)}, f32[256,128]{1,0:T(8,...) custom-call(s32[5]{0:T(128)S(1)} %stack.50.refs_0_, bf16[256,1536]{1,0:T(8,128)(2,1)S(1)} %copy-done.47, ...), custom_call_target="tpu_custom_call" | custom-call | flops 1711276032 | bytes 14106644 | tf_op jit(solution)/shard_map/scan_front/pallas_call | solution.py:75
  111.7 5.0 %all-to-all-start = ((f32[32,32,128]{2,1,0:T(8,128)}), f32[32,32,128]{2,1,0:T(8,128)S(1)}, u32[]{:S(2)}, u32[]{:S(2)}) async-start(f32[32,32,128]{2,1,0:T(8,128)} %get-tuple-element.155), calls=%async_computation | async-start | bytes 1048576 | tf_op jit(solution)/shard_map/all_to_all | solution.py:750
  116.7 3.5 join_mids.1
  129.0 33.9 %all_to_all.30 = f32[32,24,128]{2,1,0:T(8,128)S(1)} all-to-all(f32[32,24,128]{2,1,0:T(8,128)S(1)} %chain_states.2), channel_id=1, replica_groups=mesh['dp'=32,'tensor'=4] {'dp'}, dimensions={0} | all-to-all | bytes 786432 | tf_op jit(solution)/shard_map/all_to_all | solution.py:754
  162.9 7.0 %gate_front.1 = (bf16[1536,768]{1,0:T(8,128)(2,1)}, f32[256,768]{1,0:T(8,128)S(1)}, bf16[256,768]{1,0:T(8,128)(2,1)S(1)}, f32[128,1664]{1,0:T(8,128)S(1)}, f32[128,1664]{1,0:T(8,128)}) custom-call(s32[5]{0:T(128)S(1)} %stack.50.refs_0_, f32[256,768]{1,0:T(8,128)S(1)} %copy-done.41, f32[272,1920]{1,0:T(8,128)} %get-tuple-element.152.refs_2_.refs_5_.refs_0_, ...), custom_call_target="tpu_custom_call" | custom-call | flops 201326592 | bytes 17951764 | tf_op jit(solution)/shard_map/gate_front/pallas_call | solution.py:75
  170.0 3.8 collective-permute-start.18
  185.4 3.3 collective-permute-done.23.refs_2_.refs_7_
  191.0 10.7 %all_gather.7.refs_3_ = bf16[256,1536]{1,0:T(8,128)(2,1)} all-gather(bf16[64,1536]{1,0:T(8,128)(2,1)S(1)} %copy-done.101), channel_id=1, replica_groups=mesh['dp'=32,'tensor'=4] {'tensor'}, dimensions={0}, use_global_device_ids=true | all-gather | bytes 983040 | tf_op jit(solution)/shard_map/all_gather | solution.py:1203
  201.7 12.8 %experts_both.1 = (bf16[256,1536]{1,0:T(8,128)(2,1)S(1)}, bf16[256,1536]{1,0:T(8,128)(2,1)}, bf16[256,1280]{1,0:T(8,128)(2,1)S(1)}, bf16[256,2560]{1,0:T(8,128)(...) custom-call(s32[5]{0:T(128)S(1)} %stack.50.refs_0_, ...), custom_call_target="tpu_custom_call" | custom-call | flops 6039797760 | bytes 19398676 | tf_op jit(solution)/shard_map/experts_both/pallas_call | solution.py:75
  218.7 8.0 %term_products.2 = (bf16[384,1920]{1,0:T(8,128)(2,1)S(1)}, bf16[384,1920]{1,0:T(8,128)(2,1)}, bf16[384,1920]{1,0:T(8,128)(2,1)}, bf16[192,1920]{1,0:T(8,128)(2,1...) custom-call(s32[5]{0:T(128)S(1)} %stack.50.refs_0_, ...), custom_call_target="tpu_custom_call" | custom-call | flops 3019898880 | bytes 15335444 | tf_op jit(solution)/shard_map/term_products/pallas_call | solution.py:75
  234.1 10.0 %collective-permute-done.32.refs_2_ = bf16[128,1536]{1,0:T(8,128)(2,1)S(1)} collective-permute-done((bf16[128,1536]{1,0:T(8,128)(2,1)S(1)}, bf16[128,1536]{1,0:T(8,128)(2,1)S(1)}, u32[]{:S(2)}, u32[]{:S(2)}) %collective-permute-start.32) | collective-permute-done | bytes 393248 | tf_op jit(solution)/shard_map/ppermute | solution.py:760
  253.9 17.3 %all_to_all.31.refs_0_ = f32[32,32,128]{2,1,0:T(8,128)S(1)} all-to-all(f32[32,32,128]{2,1,0:T(8,128)S(1)} %get-tuple-element.184), channel_id=1, replica_groups=mesh['dp'=32,'tensor'=4] {'dp'}, dimensions={0} | all-to-all | bytes 1048576 | tf_op jit(solution)/shard_map/all_to_all | solution.py:750
  272.2 4.6 %all-to-all-start.3 = ((f32[32,24,128]{2,1,0:T(8,128)}), f32[32,24,128]{2,1,0:T(8,128)}, u32[]{:S(2)}, u32[]{:S(2)}) async-start(f32[32,24,128]{2,1,0:T(8,128)} %copy-done.25), calls=%async_computation.3 | async-start | bytes 786432 | tf_op jit(solution)/shard_map/all_to_all | solution.py:754
  281.3 4.5 %ring_add.3 = (bf16[192,1920]{1,0:T(8,128)(2,1)}, bf16[192,1920]{1,0:T(8,128)(2,1)}, bf16[192,1920]{1,0:T(8,128)(2,1)}, bf16[192,1920]{1,0:T(8,128)(2,1)}) custom-call(bf16[384,1920]{1,0:T(8,128)(2,1)} %collective-permute-done.34.refs_0_.refs_1_, bf16[384,1920]{1,0:T(8,128)(2,1)} %collective-permute-done.35.refs_1_.refs_2_, ...), custom_call_target="tpu_custom_call" | custom-call | bytes 11796480 | tf_op jit(solution)/shard_map/ring_add/pallas_call | solution.py:75
  297.4 11.2 %scan_back.1 = (f32[256,768]{1,0:T(8,128)S(1)}, f32[256,256]{1,0:T(8,128)S(1)}, f32[16,1024]{1,0:T(8,128)S(1)}, bf16[256,128]{1,0:T(8,128)(2,1)S(1)}, f32[8,1024...) custom-call(f32[272,1920]{1,0:T(8,128)S(1)} %copy-done.4, ...), custom_call_target="tpu_custom_call" | custom-call | flops 603979776 | bytes 6360064 | tf_op jit(solution)/shard_map/scan_back/pallas_call | solution.py:75
  309.9 3.7 collective-permute-done.38.refs_2_.refs_6_
  314.2 4.2 collective-permute-start.39
  322.4 4.8 %ring_total.1 = (bf16[384,1920]{1,0:T(8,128)(2,1)S(1)}, bf16[384,1920]{1,0:T(8,128)(2,1)S(1)}) custom-call(bf16[384,1920]{1,0:T(8,128)(2,1)S(1)} %copy-done.28, bf16[384,1920]{1,0:T(8,128)(2,1)} %collective-permute-done.34.refs_0_.refs_1_, bf16[384,1920]{1,0:T(8,128)(2,1)} %collective-permute-done.35.refs_1_.refs_2_, ...), custom_call_target="tpu_custom_call" | custom-call | bytes 14745600 | tf_op jit(solution)/shard_map/ring_total/pallas_call | solution.py:75
  327.3 5.9 %term_products.3 = (bf16[384,1280]{1,0:T(8,128)(2,1)S(1)}, bf16[384,1280]{1,0:T(8,128)(2,1)}, bf16[384,1280]{1,0:T(8,128)(2,1)}, bf16[192,1280]{1,0:T(8,128)(2,1...) custom-call(s32[5]{0:T(128)S(1)} %stack.50.refs_0_, ...), custom_call_target="tpu_custom_call" | custom-call | flops 2013265920 | bytes 12320788 | tf_op jit(solution)/shard_map/term_products/pallas_call | solution.py:75
  339.2 3.3 collective-permute-start.50
  342.6 5.4 %input_back.1 = (f32[128,1536]{1,0:T(8,128)S(1)}, bf16[128,1536]{1,0:T(8,128)(2,1)S(1)}, f32[1,1536]{1,0:T(1,128)S(1)}) custom-call(s32[5]{0:T(128)S(1)} %stack.50.refs_0_, bf16[256,1792]{1,0:T(8,128)(2,1)S(1)} %get-tuple-element.211.refs_1_, bf16[256,1536]{1,0:T(8,128)(2,1)S(1)} %all_gather.6.refs_1_.refs_3_.refs_2_, ...), custom_call_target="tpu_custom_call" | custom-call | flops 1509949440 | bytes 11147284 | tf_op jit(solution)/shard_map/input_back/pallas_call | solution.py:75
  352.6 5.4 %collective-permute-done.30.refs_2_ = bf16[64,1536]{1,0:T(8,128)(2,1)S(1)} collective-permute-done((bf16[64,1536]{1,0:T(8,128)(2,1)S(1)}, bf16[64,1536]{1,0:T(8,128)(2,1)S(1)}, u32[]{:S(2)}, u32[]{:S(2)}) %collective-permute-start.30) | collective-permute-done | bytes 196640 | tf_op jit(solution)/shard_map/ppermute | solution.py:760
  360.9 3.7 collective-permute-done.46.refs_2_
  373.7 11.5 %all_to_all.32.refs_0_ = f32[32,8,128]{2,1,0:T(8,128)S(1)} all-to-all(f32[32,8,128]{2,1,0:T(8,128)S(1)} %small_table.1), channel_id=1, replica_groups=mesh['dp'=32,'tensor'=4] {'dp'}, dimensions={0} | all-to-all | bytes 262144 | tf_op jit(solution)/shard_map/all_to_all | solution.py:1467
  393.3 22.2 %all_to_all.33.refs_0_.refs_8_ = f32[128,8,128]{2,1,0:T(8,128)S(1)} all-to-all(f32[128,8,128]{2,1,0:T(8,128)S(1)} %small_sum.1.refs_13_), channel_id=1, replica_groups=mesh['dp'=32,'tensor'=4] {'dp','tensor'}, dimensions={0} | all-to-all | bytes 1048576 | tf_op jit(solution)/shard_map/all_to_all | solution.py:1471
  421.2 3.5 collective-permute-done.59.refs_4_
  430.5 10.2 %collective-permute-done.63.refs_1_ = bf16[48,6400]{1,0:T(8,128)(2,1)S(1)} collective-permute-done((bf16[48,6400]{1,0:T(8,128)(2,1)S(1)}, bf16[48,6400]{1,0:T(8,128)(2,1)S(1)}, u32[]{:S(2)}, u32[]{:S(2)}) %collective-permute-start.63) | collective-permute-done | bytes 614432 | tf_op jit(solution)/shard_map/ppermute | solution.py:779
  442.5 3.6 collective-permute-start.64
  (417 shorter events, 167.2 us)
Async XLA Ops:
  49.9 27.0 %collective-permute-start.12 = (bf16[8,48,1408]{2,1,0:T(8,128)(2,1)}, bf16[8,48,1408]{2,1,0:T(8,128)(2,1)S(1)}, u32[]{:S(2)}, u32[]{:S(2)}) collective-permute-start(bf16[8,48,1408]{2,1,0:T(8,128)(2,1)} %slice_dynamic-update-slice_fusion.4.refs_13_.refs_15_.refs_12_.refs_8_), channel_id=1, source_target_pairs={{0,4},{4,8},{8,12},{12,0},{16,20},{20,24},{24,28},{28,16},{32,36},... | collective-permute-start | bytes 3244040 | tf_op jit(solution)/shard_map/ppermute | solution.py:779
  49.9 27.0 %collective-permute-start.13 = (bf16[8,48,1408]{2,1,0:T(8,128)(2,1)}, bf16[8,48,1408]{2,1,0:T(8,128)(2,1)}, u32[]{:S(2)}, u32[]{:S(2)}) collective-permute-start(bf16[8,48,1408]{2,1,0:T(8,128)(2,1)} %slice_dynamic-update-slice_fusion.4.refs_13_.refs_15_.refs_12_.refs_8_), channel_id=1, source_target_pairs={{0,12},{4,0},{8,4},{12,8},{16,28},{20,16},{24,20},{28,24},{32,44},... | collective-permute-start | bytes 3244040 | tf_op jit(solution)/shard_map/ppermute | solution.py:779
  53.3 23.6 %collective-permute-start.6 = (bf16[8,48,1280]{2,1,0:T(8,128)(2,1)}, bf16[8,48,1280]{2,1,0:T(8,128)(2,1)S(1)}, u32[]{:S(2)}, u32[]{:S(2)}) collective-permute-start(bf16[8,48,1280]{2,1,0:T(8,128)(2,1)} %slice_dynamic-update-slice_fusion.6.refs_8_.refs_10_.refs_7_.refs_3_), channel_id=1, source_target_pairs={{0,32},{4,36},{8,40},{12,44},{16,48},{20,52},{24,56},{28,60},{32,6... | collective-permute-start | bytes 2949128 | tf_op jit(solution)/shard_map/ppermute | solution.py:779
  53.7 23.2 %collective-permute-start.7 = (bf16[8,48,1280]{2,1,0:T(8,128)(2,1)}, bf16[8,48,1280]{2,1,0:T(8,128)(2,1)}, u32[]{:S(2)}, u32[]{:S(2)}) collective-permute-start(bf16[8,48,1280]{2,1,0:T(8,128)(2,1)} %slice_dynamic-update-slice_fusion.6.refs_8_.refs_10_.refs_7_.refs_3_), channel_id=1, source_target_pairs={{0,96},{4,100},{8,104},{12,108},{16,112},{20,116},{24,120},{28,124... | collective-permute-start | bytes 2949128 | tf_op jit(solution)/shard_map/ppermute | solution.py:779
  79.1 18.3 %collective-permute-start.16 = (bf16[4,48,1408]{2,1,0:T(8,128)(2,1)S(1)}, bf16[4,48,1408]{2,1,0:T(8,128)(2,1)S(1)}, u32[]{:S(2)}, u32[]{:S(2)}) collective-permute-start(bf16[4,48,1408]{2,1,0:T(8,128)(2,1)S(1)} %get-tuple-element.149), channel_id=1, source_target_pairs={{0,4},{4,8},{8,12},{12,0},{16,20},{20,24},{24,28},{28,16},{32,36},... | collective-permute-start | bytes 1622024 | tf_op jit(solution)/shard_map/ppermute | solution.py:779
  120.2 53.5 %collective-permute-start.19 = (bf16[8,48,1920]{2,1,0:T(8,128)(2,1)}, bf16[8,48,1920]{2,1,0:T(8,128)(2,1)}, u32[]{:S(2)}, u32[]{:S(2)}) collective-permute-start(bf16[8,48,1920]{2,1,0:T(8,128)(2,1)} %get-tuple-element.156.refs_1_.refs_5_), channel_id=1, source_target_pairs={{0,32},{4,36},{8,40},{12,44},{16,48},{20,52},{24,56},{28,60},{32,6... | collective-permute-start | bytes 4423688 | tf_op jit(solution)/shard_map/ppermute | solution.py:779
  121.5 52.2 %collective-permute-start.20 = (bf16[8,48,1920]{2,1,0:T(8,128)(2,1)}, bf16[8,48,1920]{2,1,0:T(8,128)(2,1)}, u32[]{:S(2)}, u32[]{:S(2)}) collective-permute-start(bf16[8,48,1920]{2,1,0:T(8,128)(2,1)} %get-tuple-element.156.refs_1_.refs_5_), channel_id=1, source_target_pairs={{0,96},{4,100},{8,104},{12,108},{16,112},{20,116},{24,120},{28,124... | collective-permute-start | bytes 4423688 | tf_op jit(solution)/shard_map/ppermute | solution.py:779
  123.0 50.8 %collective-permute-start.21 = (bf16[8,48,1920]{2,1,0:T(8,128)(2,1)}, bf16[8,48,1920]{2,1,0:T(8,128)(2,1)}, u32[]{:S(2)}, u32[]{:S(2)}) collective-permute-start(bf16[8,48,1920]{2,1,0:T(8,128)(2,1)} %get-tuple-element.157.refs_2_.refs_10_), channel_id=1, source_target_pairs={{0,4},{4,8},{8,12},{12,0},{16,20},{20,24},{24,28},{28,16},{32,36},... | collective-permute-start | bytes 4423688 | tf_op jit(solution)/shard_map/ppermute | solution.py:779
  124.3 49.5 %collective-permute-start.22 = (bf16[8,48,1920]{2,1,0:T(8,128)(2,1)}, bf16[8,48,1920]{2,1,0:T(8,128)(2,1)}, u32[]{:S(2)}, u32[]{:S(2)}) collective-permute-start(bf16[8,48,1920]{2,1,0:T(8,128)(2,1)} %get-tuple-element.157.refs_2_.refs_10_), channel_id=1, source_target_pairs={{0,12},{4,0},{8,4},{12,8},{16,28},{20,16},{24,20},{28,24},{32,44},... | collective-permute-start | bytes 4423688 | tf_op jit(solution)/shard_map/ppermute | solution.py:779
  180.0 21.6 %collective-permute-start.25 = (bf16[4,48,1920]{2,1,0:T(8,128)(2,1)S(1)}, bf16[4,48,1920]{2,1,0:T(8,128)(2,1)S(1)}, u32[]{:S(2)}, u32[]{:S(2)}) collective-permute-start(bf16[4,48,1920]{2,1,0:T(8,128)(2,1)S(1)} %get-tuple-element.162), channel_id=1, source_target_pairs={{0,32},{4,36},{8,40},{12,44},{16,48},{20,52},{24,56},{28,60},{32,6... | collective-permute-start | bytes 2211848 | tf_op jit(solution)/shard_map/ppermute | solution.py:779
  180.3 21.3 %collective-permute-start.26 = (bf16[4,48,1920]{2,1,0:T(8,128)(2,1)S(1)}, bf16[4,48,1920]{2,1,0:T(8,128)(2,1)S(1)}, u32[]{:S(2)}, u32[]{:S(2)}) collective-permute-start(bf16[4,48,1920]{2,1,0:T(8,128)(2,1)S(1)} %get-tuple-element.163), channel_id=1, source_target_pairs={{0,96},{4,100},{8,104},{12,108},{16,112},{20,116},{24,120},{28,124... | collective-permute-start | bytes 2211848 | tf_op jit(solution)/shard_map/ppermute | solution.py:779
  182.8 18.9 %collective-permute-start.27 = (bf16[4,48,1920]{2,1,0:T(8,128)(2,1)S(1)}, bf16[4,48,1920]{2,1,0:T(8,128)(2,1)S(1)}, u32[]{:S(2)}, u32[]{:S(2)}) collective-permute-start(bf16[4,48,1920]{2,1,0:T(8,128)(2,1)S(1)} %get-tuple-element.164), channel_id=1, source_target_pairs={{0,4},{4,8},{8,12},{12,0},{16,20},{20,24},{24,28},{28,16},{32,36},... | collective-permute-start | bytes 2211848 | tf_op jit(solution)/shard_map/ppermute | solution.py:779
  183.2 18.5 %collective-permute-start.28 = (bf16[4,48,1920]{2,1,0:T(8,128)(2,1)S(1)}, bf16[4,48,1920]{2,1,0:T(8,128)(2,1)S(1)}, u32[]{:S(2)}, u32[]{:S(2)}) collective-permute-start(bf16[4,48,1920]{2,1,0:T(8,128)(2,1)S(1)} %get-tuple-element.165), channel_id=1, source_target_pairs={{0,12},{4,0},{8,4},{12,8},{16,28},{20,16},{24,20},{28,24},{32,44},... | collective-permute-start | bytes 2211848 | tf_op jit(solution)/shard_map/ppermute | solution.py:779
  214.5 18.4 %collective-permute-start.31 = (bf16[128,1536]{1,0:T(8,128)(2,1)S(1)}, bf16[128,1536]{1,0:T(8,128)(2,1)S(1)}, u32[]{:S(2)}, u32[]{:S(2)}) collective-permute-start(bf16[128,1536]{1,0:T(8,128)(2,1)S(1)} %get-tuple-element.172), channel_id=1, source_target_pairs={{0,1},{1,0},{2,3},{3,2},{4,5},{5,4},{6,7},{7,6},{8,9},{9,8},{10,11... | collective-permute-start | bytes 1179656 | tf_op jit(solution)/shard_map/ppermute | solution.py:760
  227.5 49.3 %collective-permute-start.34 = (bf16[384,1920]{1,0:T(8,128)(2,1)}, bf16[384,1920]{1,0:T(8,128)(2,1)}, u32[]{:S(2)}, u32[]{:S(2)}) collective-permute-start(bf16[384,1920]{1,0:T(8,128)(2,1)} %get-tuple-element.189), channel_id=1, source_target_pairs={{0,32},{4,36},{8,40},{12,44},{16,48},{20,52},{24,56},{28,60},{32,6... | collective-permute-start | bytes 4423688 | tf_op jit(solution)/shard_map/ppermute | solution.py:779
  227.6 49.2 %collective-permute-start.35 = (bf16[384,1920]{1,0:T(8,128)(2,1)}, bf16[384,1920]{1,0:T(8,128)(2,1)}, u32[]{:S(2)}, u32[]{:S(2)}) collective-permute-start(bf16[384,1920]{1,0:T(8,128)(2,1)} %get-tuple-element.190), channel_id=1, source_target_pairs={{0,96},{4,100},{8,104},{12,108},{16,112},{20,116},{24,120},{28,124... | collective-permute-start | bytes 4423688 | tf_op jit(solution)/shard_map/ppermute | solution.py:779
  230.3 46.6 %collective-permute-start.36 = (bf16[384,1920]{1,0:T(8,128)(2,1)}, bf16[384,1920]{1,0:T(8,128)(2,1)}, u32[]{:S(2)}, u32[]{:S(2)}) collective-permute-start(bf16[384,1920]{1,0:T(8,128)(2,1)} %get-tuple-element.193), channel_id=1, source_target_pairs={{0,4},{4,8},{8,12},{12,0},{16,20},{20,24},{24,28},{28,16},{32,36},... | collective-permute-start | bytes 4423688 | tf_op jit(solution)/shard_map/ppermute | solution.py:779
  230.3 46.6 %collective-permute-start.37 = (bf16[384,1920]{1,0:T(8,128)(2,1)}, bf16[384,1920]{1,0:T(8,128)(2,1)}, u32[]{:S(2)}, u32[]{:S(2)}) collective-permute-start(bf16[384,1920]{1,0:T(8,128)(2,1)} %get-tuple-element.194), channel_id=1, source_target_pairs={{0,12},{4,0},{8,4},{12,8},{16,28},{20,16},{24,20},{28,24},{32,44},... | collective-permute-start | bytes 4423688 | tf_op jit(solution)/shard_map/ppermute | solution.py:779
  272.2 19.1 %all-to-all-start.3 = ((f32[32,24,128]{2,1,0:T(8,128)}), f32[32,24,128]{2,1,0:T(8,128)}, u32[]{:S(2)}, u32[]{:S(2)}) async-start(f32[32,24,128]{2,1,0:T(8,128)} %copy-done.25), calls=%async_computation.3 | async-start | bytes 786432 | tf_op jit(solution)/shard_map/all_to_all | solution.py:754
  285.8 35.6 %collective-permute-start.41 = (bf16[192,1920]{1,0:T(8,128)(2,1)}, bf16[192,1920]{1,0:T(8,128)(2,1)}, u32[]{:S(2)}, u32[]{:S(2)}) collective-permute-start(bf16[192,1920]{1,0:T(8,128)(2,1)} %get-tuple-element.197.refs_12_), channel_id=1, source_target_pairs={{0,32},{4,36},{8,40},{12,44},{16,48},{20,52},{24,56},{28,60},{32,6... | collective-permute-start | bytes 2211848 | tf_op jit(solution)/shard_map/ppermute | solution.py:779
  286.9 35.4 %collective-permute-start.42 = (bf16[192,1920]{1,0:T(8,128)(2,1)}, bf16[192,1920]{1,0:T(8,128)(2,1)}, u32[]{:S(2)}, u32[]{:S(2)}) collective-permute-start(bf16[192,1920]{1,0:T(8,128)(2,1)} %get-tuple-element.198.refs_13_), channel_id=1, source_target_pairs={{0,96},{4,100},{8,104},{12,108},{16,112},{20,116},{24,120},{28,124... | collective-permute-start | bytes 2211848 | tf_op jit(solution)/shard_map/ppermute | solution.py:779
  288.7 33.7 %collective-permute-start.43 = (bf16[192,1920]{1,0:T(8,128)(2,1)}, bf16[192,1920]{1,0:T(8,128)(2,1)}, u32[]{:S(2)}, u32[]{:S(2)}) collective-permute-start(bf16[192,1920]{1,0:T(8,128)(2,1)} %get-tuple-element.199.refs_14_), channel_id=1, source_target_pairs={{0,4},{4,8},{8,12},{12,0},{16,20},{20,24},{24,28},{28,16},{32,36},... | collective-permute-start | bytes 2211848 | tf_op jit(solution)/shard_map/ppermute | solution.py:779
  289.7 32.6 %collective-permute-start.44 = (bf16[192,1920]{1,0:T(8,128)(2,1)}, bf16[192,1920]{1,0:T(8,128)(2,1)}, u32[]{:S(2)}, u32[]{:S(2)}) collective-permute-start(bf16[192,1920]{1,0:T(8,128)(2,1)} %get-tuple-element.200.refs_15_), channel_id=1, source_target_pairs={{0,12},{4,0},{8,4},{12,8},{16,28},{20,16},{24,20},{28,24},{32,44},... | collective-permute-start | bytes 2211848 | tf_op jit(solution)/shard_map/ppermute | solution.py:779
  321.5 26.5 %collective-permute-start.29 = (bf16[128,1536]{1,0:T(8,128)(2,1)}, bf16[128,1536]{1,0:T(8,128)(2,1)S(1)}, u32[]{:S(2)}, u32[]{:S(2)}) collective-permute-start(bf16[128,1536]{1,0:T(8,128)(2,1)} %get-tuple-element.167), channel_id=1, source_target_pairs={{0,1},{1,0},{2,3},{3,2},{4,5},{5,4},{6,7},{7,6},{8,9},{9,8},{10,11... | collective-permute-start | bytes 1179656 | tf_op jit(solution)/shard_map/ppermute | solution.py:760
  336.4 29.7 %collective-permute-start.47 = (bf16[384,1280]{1,0:T(8,128)(2,1)}, bf16[384,1280]{1,0:T(8,128)(2,1)S(1)}, u32[]{:S(2)}, u32[]{:S(2)}) collective-permute-start(bf16[384,1280]{1,0:T(8,128)(2,1)} %get-tuple-element.225), channel_id=1, source_target_pairs={{0,32},{4,36},{8,40},{12,44},{16,48},{20,52},{24,56},{28,60},{32,6... | collective-permute-start | bytes 2949128 | tf_op jit(solution)/shard_map/ppermute | solution.py:779
  337.8 28.3 %collective-permute-start.48 = (bf16[384,1280]{1,0:T(8,128)(2,1)}, bf16[384,1280]{1,0:T(8,128)(2,1)S(1)}, u32[]{:S(2)}, u32[]{:S(2)}) collective-permute-start(bf16[384,1280]{1,0:T(8,128)(2,1)} %get-tuple-element.226), channel_id=1, source_target_pairs={{0,96},{4,100},{8,104},{12,108},{16,112},{20,116},{24,120},{28,124... | collective-permute-start | bytes 2949128 | tf_op jit(solution)/shard_map/ppermute | solution.py:779
  339.1 27.0 %collective-permute-start.49 = (bf16[384,1280]{1,0:T(8,128)(2,1)}, bf16[384,1280]{1,0:T(8,128)(2,1)S(1)}, u32[]{:S(2)}, u32[]{:S(2)}) collective-permute-start(bf16[384,1280]{1,0:T(8,128)(2,1)} %get-tuple-element.229), channel_id=1, source_target_pairs={{0,4},{4,8},{8,12},{12,0},{16,20},{20,24},{24,28},{28,16},{32,36},... | collective-permute-start | bytes 2949128 | tf_op jit(solution)/shard_map/ppermute | solution.py:779
  339.2 26.9 %collective-permute-start.50 = (bf16[384,1280]{1,0:T(8,128)(2,1)}, bf16[384,1280]{1,0:T(8,128)(2,1)S(1)}, u32[]{:S(2)}, u32[]{:S(2)}) collective-permute-start(bf16[384,1280]{1,0:T(8,128)(2,1)} %get-tuple-element.230), channel_id=1, source_target_pairs={{0,12},{4,0},{8,4},{12,8},{16,28},{20,16},{24,20},{28,24},{32,44},... | collective-permute-start | bytes 2949128 | tf_op jit(solution)/shard_map/ppermute | solution.py:779
  387.8 27.6 %collective-permute-start.55 = (bf16[96,3200]{1,0:T(8,128)(2,1)S(1)}, bf16[96,3200]{1,0:T(8,128)(2,1)S(1)}, u32[]{:S(2)}, u32[]{:S(2)}) collective-permute-start(bf16[96,3200]{1,0:T(8,128)(2,1)S(1)} %get-tuple-element.239), channel_id=1, source_target_pairs={{0,4},{4,8},{8,12},{12,0},{16,20},{20,24},{24,28},{28,16},{32,36},... | collective-permute-start | bytes 1843208 | tf_op jit(solution)/shard_map/ppermute | solution.py:779
  388.3 27.2 %collective-permute-start.56 = (bf16[96,3200]{1,0:T(8,128)(2,1)S(1)}, bf16[96,3200]{1,0:T(8,128)(2,1)S(1)}, u32[]{:S(2)}, u32[]{:S(2)}) collective-permute-start(bf16[96,3200]{1,0:T(8,128)(2,1)S(1)} %get-tuple-element.240), channel_id=1, source_target_pairs={{0,12},{4,0},{8,4},{12,8},{16,28},{20,16},{24,20},{28,24},{32,44},... | collective-permute-start | bytes 1843208 | tf_op jit(solution)/shard_map/ppermute | solution.py:779
  390.6 24.9 %collective-permute-start.57 = (bf16[96,3200]{1,0:T(8,128)(2,1)S(1)}, bf16[96,3200]{1,0:T(8,128)(2,1)S(1)}, u32[]{:S(2)}, u32[]{:S(2)}) collective-permute-start(bf16[96,3200]{1,0:T(8,128)(2,1)S(1)} %get-tuple-element.243), channel_id=1, source_target_pairs={{0,32},{4,36},{8,40},{12,44},{16,48},{20,52},{24,56},{28,60},{32,6... | collective-permute-start | bytes 1843208 | tf_op jit(solution)/shard_map/ppermute | solution.py:779
  390.9 24.5 %collective-permute-start.58 = (bf16[96,3200]{1,0:T(8,128)(2,1)S(1)}, bf16[96,3200]{1,0:T(8,128)(2,1)S(1)}, u32[]{:S(2)}, u32[]{:S(2)}) collective-permute-start(bf16[96,3200]{1,0:T(8,128)(2,1)S(1)} %get-tuple-element.244), channel_id=1, source_target_pairs={{0,96},{4,100},{8,104},{12,108},{16,112},{20,116},{24,120},{28,124... | collective-permute-start | bytes 1843208 | tf_op jit(solution)/shard_map/ppermute | solution.py:779
  (146 other events, 1773.4 us)

commit v4 on v3

--- a/solution.py
+++ b/solution.py
@@ -739,7 +739,7 @@
         carried = jnp.zeros((size, LANES), f32)
         for turn in range(blocks):
             k = blocks - 1 - turn if reverse else turn
-            carried_out[k] = carried
+            carried_out[k] = carried.astype(carried_out.dtype)
             carried = factors[0:size, k : k + 1] * carried + parts[k, 0:size, :]
 
     return kernel
@@ -749,10 +749,10 @@
     blocks = lax.axis_size(axis)
     parts = lax.all_to_all(sent, axis, 0, 0, tiled=True)
     carried = kernel_call(
-        chain_states(reverse, blocks, size), [shape_of((blocks, size, LANES))], parts, wait=wait
+        chain_states(reverse, blocks, size), [shape_of((blocks, size, LANES), bf16)], parts, wait=wait
     )[0]
     back = lax.all_to_all(carried, axis, 0, 0, tiled=True)
-    return back.reshape(blocks * size, LANES)
+    return back.astype(f32).reshape(blocks * size, LANES)
 
 
 def other(value, bit):

time: 457 us -> 454 us (level)
  no operation moved by 1% of the time
where the time goes in v4:
time: 454 us; the launch traced here: 446 us
  starting transfers between devices  111 us (24%)
  blocking collectives  109 us (24%)
  Pallas kernels  98.3 us (22%)
  waiting for transfers between devices  79.7 us (18%)
  local copies, waits for them, and re-layouts  42.2 us (9%)
    pallas_call x35, Pallas kernels, kernel_call(): pl.pallas_call(body_of, name=kernel.__qualname__.split('.')[0], out_shape...  98.3 us
    ppermute x50, starting transfers between devices, shift(): return lax.ppermute(value, 'dp', pairs)  72.2 us
    ppermute x50, waiting for transfers between devices, shift(): return lax.ppermute(value, 'dp', pairs)  48.2 us
    unnamed x232, local copies, waits for them, and re-layouts  35.9 us
    all_to_all x1, blocking collectives, exchange_states(): back = lax.all_to_all(carried, axis, 0, 0, tiled=True)  32.3 us
    ppermute x13, waiting for transfers between devices, other(): lax.ppermute(value, 'tensor', [(rank, rank ^ bit) for rank in range(count)])  27.6 us
    ppermute x13, starting transfers between devices, other(): lax.ppermute(value, 'tensor', [(rank, rank ^ bit) for rank in range(count)])  26.2 us
    all_to_all x1, blocking collectives, body(): table_end = lax.all_to_all(table, ('dp', 'tensor'), 0, 0, tiled=True)  22.2 us
  transfers between devices with their start and end apart: 67, of which 17 were waited for; matrix products, arithmetic and copies ran while one was open for 3% of the time, Pallas kernels for 14%

profile of v4, /device:TPU:1, one launch (start us, length us, event | category | flops | bytes accessed | tf_op | source)
XLA Modules:
  0.0 446.2 jit_solution(18086801221020611136)
XLA Ops:
  9.0 12.0 %collective-permute-done.1 = bf16[48,6528]{1,0:T(8,128)(2,1)S(1)} collective-permute-done((bf16[48,6528]{1,0:T(8,128)(2,1)}, bf16[48,6528]{1,0:T(8,128)(2,1)S(1)}, u32[]{:S(2)}, u32[]{:S(2)}) %collective-permute-start.1) | collective-permute-done | bytes 626720 | tf_op jit(solution)/shard_map/ppermute | solution.py:779
  28.3 8.3 %collective-permute-done.2.refs_1_ = bf16[2,48,3200]{2,1,0:T(8,128)(2,1)S(1)} collective-permute-done((bf16[2,48,3200]{2,1,0:T(8,128)(2,1)S(1)}, bf16[2,48,3200]{2,1,0:T(8,128)(2,1)S(1)}, u32[]{:S(2)}, u32[]{:S(2)}) %collective-permute-start.2) | collective-permute-done | bytes 614432 | tf_op jit(solution)/shard_map/ppermute | solution.py:779
  56.1 15.0 %all_gather.6.refs_1_.refs_3_.refs_2_ = bf16[256,1536]{1,0:T(8,128)(2,1)S(1)} all-gather(bf16[64,1536]{1,0:T(8,128)(2,1)S(1)} %copy-done.44), channel_id=1, replica_groups=mesh['dp'=32,'tensor'=4] {'tensor'}, dimensions={0}, use_global_device_ids=true | all-gather | bytes 983040 | tf_op jit(solution)/shard_map/all_gather | solution.py:1202
  87.9 9.5 %collective-permute-done.14.refs_11_.refs_13_.refs_10_.refs_6_ = bf16[4,48,1280]{2,1,0:T(8,128)(2,1)S(1)} collective-permute-done((bf16[4,48,1280]{2,1,0:T(8,128)(2,1)S(1)}, bf16[4,48,1280]{2,1,0:T(8,128)(2,1)S(1)}, u32[]{:S(2)}, u32[]{:S(2)}) %collective-permute-start.14) | collective-permute-done | bytes 491552 | tf_op jit(solution)/shard_map/ppermute | solution.py:779
  97.5 11.3 %scan_front.1 = (f32[272,1920]{1,0:T(8,128)}, f32[256,128]{1,0:T(8,128)S(1)}, f32[256,768]{1,0:T(8,128)S(1)}, f32[256,1024]{1,0:T(8,128)}, f32[256,128]{1,0:T(8,...) custom-call(s32[5]{0:T(128)S(1)} %stack.50.refs_0_, bf16[256,1536]{1,0:T(8,128)(2,1)S(1)} %copy-done.47, ...), custom_call_target="tpu_custom_call" | custom-call | flops 1711276032 | bytes 14106644 | tf_op jit(solution)/shard_map/scan_front/pallas_call | solution.py:75
  111.7 5.0 %all-to-all-start = ((f32[32,32,128]{2,1,0:T(8,128)}), f32[32,32,128]{2,1,0:T(8,128)S(1)}, u32[]{:S(2)}, u32[]{:S(2)}) async-start(f32[32,32,128]{2,1,0:T(8,128)} %get-tuple-element.155), calls=%async_computation | async-start | bytes 1048576 | tf_op jit(solution)/shard_map/all_to_all | solution.py:750
  116.7 3.5 join_mids.1
  129.0 32.3 %all_to_all.30 = bf16[32,24,128]{2,1,0:T(8,128)(2,1)S(1)} all-to-all(bf16[32,24,128]{2,1,0:T(8,128)(2,1)S(1)} %chain_states.2), channel_id=1, replica_groups=mesh['dp'=32,'tensor'=4] {'dp'}, dimensions={0} | all-to-all | bytes 393216 | tf_op jit(solution)/shard_map/all_to_all | solution.py:754
  161.4 7.0 %gate_front.1 = (bf16[1536,768]{1,0:T(8,128)(2,1)}, f32[256,768]{1,0:T(8,128)S(1)}, bf16[256,768]{1,0:T(8,128)(2,1)S(1)}, f32[128,1664]{1,0:T(8,128)S(1)}, f32[128,1664]{1,0:T(8,128)}) custom-call(s32[5]{0:T(128)S(1)} %stack.50.refs_0_, f32[256,768]{1,0:T(8,128)S(1)} %copy-done.40, f32[272,1920]{1,0:T(8,128)} %get-tuple-element.152.refs_2_.refs_5_.refs_0_, ...), custom_call_target="tpu_custom_call" | custom-call | flops 201326592 | bytes 17951764 | tf_op jit(solution)/shard_map/gate_front/pallas_call | solution.py:75
  168.4 3.3 collective-permute-start.18
  183.4 3.3 collective-permute-done.23.refs_2_.refs_7_
  188.9 10.7 %all_gather.7.refs_3_ = bf16[256,1536]{1,0:T(8,128)(2,1)} all-gather(bf16[64,1536]{1,0:T(8,128)(2,1)S(1)} %copy-done.101), channel_id=1, replica_groups=mesh['dp'=32,'tensor'=4] {'tensor'}, dimensions={0}, use_global_device_ids=true | all-gather | bytes 983040 | tf_op jit(solution)/shard_map/all_gather | solution.py:1203
  199.6 12.8 %experts_both.1 = (bf16[256,1536]{1,0:T(8,128)(2,1)S(1)}, bf16[256,1536]{1,0:T(8,128)(2,1)}, bf16[256,1280]{1,0:T(8,128)(2,1)S(1)}, bf16[256,2560]{1,0:T(8,128)(...) custom-call(s32[5]{0:T(128)S(1)} %stack.50.refs_0_, ...), custom_call_target="tpu_custom_call" | custom-call | flops 6039797760 | bytes 19398676 | tf_op jit(solution)/shard_map/experts_both/pallas_call | solution.py:75
  216.6 8.0 %term_products.2 = (bf16[384,1920]{1,0:T(8,128)(2,1)S(1)}, bf16[384,1920]{1,0:T(8,128)(2,1)}, bf16[384,1920]{1,0:T(8,128)(2,1)}, bf16[192,1920]{1,0:T(8,128)(2,1...) custom-call(s32[5]{0:T(128)S(1)} %stack.50.refs_0_, ...), custom_call_target="tpu_custom_call" | custom-call | flops 3019898880 | bytes 15335444 | tf_op jit(solution)/shard_map/term_products/pallas_call | solution.py:75
  232.1 10.0 %collective-permute-done.32.refs_2_ = bf16[128,1536]{1,0:T(8,128)(2,1)S(1)} collective-permute-done((bf16[128,1536]{1,0:T(8,128)(2,1)S(1)}, bf16[128,1536]{1,0:T(8,128)(2,1)S(1)}, u32[]{:S(2)}, u32[]{:S(2)}) %collective-permute-start.32) | collective-permute-done | bytes 393248 | tf_op jit(solution)/shard_map/ppermute | solution.py:760
  251.8 17.3 %all_to_all.31.refs_0_ = f32[32,32,128]{2,1,0:T(8,128)S(1)} all-to-all(f32[32,32,128]{2,1,0:T(8,128)S(1)} %get-tuple-element.184), channel_id=1, replica_groups=mesh['dp'=32,'tensor'=4] {'dp'}, dimensions={0} | all-to-all | bytes 1048576 | tf_op jit(solution)/shard_map/all_to_all | solution.py:750
  270.1 4.6 %all-to-all-start.3 = ((bf16[32,24,128]{2,1,0:T(8,128)(2,1)}), bf16[32,24,128]{2,1,0:T(8,128)(2,1)}, u32[]{:S(2)}, u32[]{:S(2)}) async-start(bf16[32,24,128]{2,1,0:T(8,128)(2,1)} %copy-done.43), calls=%async_computation.3 | async-start | bytes 393216 | tf_op jit(solution)/shard_map/all_to_all | solution.py:754
  279.2 4.5 %ring_add.3 = (bf16[192,1920]{1,0:T(8,128)(2,1)}, bf16[192,1920]{1,0:T(8,128)(2,1)}, bf16[192,1920]{1,0:T(8,128)(2,1)}, bf16[192,1920]{1,0:T(8,128)(2,1)}) custom-call(bf16[384,1920]{1,0:T(8,128)(2,1)} %collective-permute-done.34.refs_0_.refs_1_, bf16[384,1920]{1,0:T(8,128)(2,1)} %collective-permute-done.35.refs_1_.refs_2_, ...), custom_call_target="tpu_custom_call" | custom-call | bytes 11796480 | tf_op jit(solution)/shard_map/ring_add/pallas_call | solution.py:75
  296.3 10.1 %scan_back.1 = (f32[256,768]{1,0:T(8,128)S(1)}, f32[256,256]{1,0:T(8,128)S(1)}, f32[16,1024]{1,0:T(8,128)S(1)}, bf16[256,128]{1,0:T(8,128)(2,1)S(1)}, f32[8,1024...) custom-call(f32[272,1920]{1,0:T(8,128)S(1)} %copy-done.4, ...), custom_call_target="tpu_custom_call" | custom-call | flops 603979776 | bytes 6360064 | tf_op jit(solution)/shard_map/scan_back/pallas_call | solution.py:75
  307.6 3.7 collective-permute-done.38.refs_2_.refs_6_
  311.9 4.3 collective-permute-start.39
  320.0 4.8 %ring_total.1 = (bf16[384,1920]{1,0:T(8,128)(2,1)S(1)}, bf16[384,1920]{1,0:T(8,128)(2,1)S(1)}) custom-call(bf16[384,1920]{1,0:T(8,128)(2,1)S(1)} %copy-done.29, bf16[384,1920]{1,0:T(8,128)(2,1)} %collective-permute-done.34.refs_0_.refs_1_, bf16[384,1920]{1,0:T(8,128)(2,1)} %collective-permute-done.35.refs_1_.refs_2_, ...), custom_call_target="tpu_custom_call" | custom-call | bytes 14745600 | tf_op jit(solution)/shard_map/ring_total/pallas_call | solution.py:75
  324.9 5.9 %term_products.3 = (bf16[384,1280]{1,0:T(8,128)(2,1)S(1)}, bf16[384,1280]{1,0:T(8,128)(2,1)}, bf16[384,1280]{1,0:T(8,128)(2,1)}, bf16[192,1280]{1,0:T(8,128)(2,1...) custom-call(s32[5]{0:T(128)S(1)} %stack.50.refs_0_, ...), custom_call_target="tpu_custom_call" | custom-call | flops 2013265920 | bytes 12320788 | tf_op jit(solution)/shard_map/term_products/pallas_call | solution.py:75
  336.8 3.4 collective-permute-start.50
  340.2 5.4 %input_back.1 = (f32[128,1536]{1,0:T(8,128)S(1)}, bf16[128,1536]{1,0:T(8,128)(2,1)S(1)}, f32[1,1536]{1,0:T(1,128)S(1)}) custom-call(s32[5]{0:T(128)S(1)} %stack.50.refs_0_, bf16[256,1792]{1,0:T(8,128)(2,1)S(1)} %get-tuple-element.211.refs_1_, bf16[256,1536]{1,0:T(8,128)(2,1)S(1)} %all_gather.6.refs_1_.refs_3_.refs_2_, ...), custom_call_target="tpu_custom_call" | custom-call | flops 1509949440 | bytes 11147284 | tf_op jit(solution)/shard_map/input_back/pallas_call | solution.py:75
  350.2 5.4 %collective-permute-done.30.refs_2_ = bf16[64,1536]{1,0:T(8,128)(2,1)S(1)} collective-permute-done((bf16[64,1536]{1,0:T(8,128)(2,1)S(1)}, bf16[64,1536]{1,0:T(8,128)(2,1)S(1)}, u32[]{:S(2)}, u32[]{:S(2)}) %collective-permute-start.30) | collective-permute-done | bytes 196640 | tf_op jit(solution)/shard_map/ppermute | solution.py:760
  358.5 3.7 collective-permute-done.46.refs_2_
  371.3 11.5 %all_to_all.32.refs_0_ = f32[32,8,128]{2,1,0:T(8,128)S(1)} all-to-all(f32[32,8,128]{2,1,0:T(8,128)S(1)} %small_table.1), channel_id=1, replica_groups=mesh['dp'=32,'tensor'=4] {'dp'}, dimensions={0} | all-to-all | bytes 262144 | tf_op jit(solution)/shard_map/all_to_all | solution.py:1467
  391.0 22.2 %all_to_all.33.refs_0_.refs_8_ = f32[128,8,128]{2,1,0:T(8,128)S(1)} all-to-all(f32[128,8,128]{2,1,0:T(8,128)S(1)} %small_sum.1.refs_13_), channel_id=1, replica_groups=mesh['dp'=32,'tensor'=4] {'dp','tensor'}, dimensions={0} | all-to-all | bytes 1048576 | tf_op jit(solution)/shard_map/all_to_all | solution.py:1471
  418.9 3.5 collective-permute-done.59.refs_4_
  428.2 10.2 %collective-permute-done.63.refs_1_ = bf16[48,6400]{1,0:T(8,128)(2,1)S(1)} collective-permute-done((bf16[48,6400]{1,0:T(8,128)(2,1)S(1)}, bf16[48,6400]{1,0:T(8,128)(2,1)S(1)}, u32[]{:S(2)}, u32[]{:S(2)}) %collective-permute-start.63) | collective-permute-done | bytes 614432 | tf_op jit(solution)/shard_map/ppermute | solution.py:779
  440.2 3.6 collective-permute-start.64
  (419 shorter events, 168.0 us)
Async XLA Ops:
  49.9 27.0 %collective-permute-start.12 = (bf16[8,48,1408]{2,1,0:T(8,128)(2,1)}, bf16[8,48,1408]{2,1,0:T(8,128)(2,1)S(1)}, u32[]{:S(2)}, u32[]{:S(2)}) collective-permute-start(bf16[8,48,1408]{2,1,0:T(8,128)(2,1)} %slice_dynamic-update-slice_fusion.4.refs_13_.refs_15_.refs_12_.refs_8_), channel_id=1, source_target_pairs={{0,4},{4,8},{8,12},{12,0},{16,20},{20,24},{24,28},{28,16},{32,36},... | collective-permute-start | bytes 3244040 | tf_op jit(solution)/shard_map/ppermute | solution.py:779
  49.9 27.0 %collective-permute-start.13 = (bf16[8,48,1408]{2,1,0:T(8,128)(2,1)}, bf16[8,48,1408]{2,1,0:T(8,128)(2,1)}, u32[]{:S(2)}, u32[]{:S(2)}) collective-permute-start(bf16[8,48,1408]{2,1,0:T(8,128)(2,1)} %slice_dynamic-update-slice_fusion.4.refs_13_.refs_15_.refs_12_.refs_8_), channel_id=1, source_target_pairs={{0,12},{4,0},{8,4},{12,8},{16,28},{20,16},{24,20},{28,24},{32,44},... | collective-permute-start | bytes 3244040 | tf_op jit(solution)/shard_map/ppermute | solution.py:779
  53.3 23.6 %collective-permute-start.6 = (bf16[8,48,1280]{2,1,0:T(8,128)(2,1)}, bf16[8,48,1280]{2,1,0:T(8,128)(2,1)S(1)}, u32[]{:S(2)}, u32[]{:S(2)}) collective-permute-start(bf16[8,48,1280]{2,1,0:T(8,128)(2,1)} %slice_dynamic-update-slice_fusion.6.refs_8_.refs_10_.refs_7_.refs_3_), channel_id=1, source_target_pairs={{0,32},{4,36},{8,40},{12,44},{16,48},{20,52},{24,56},{28,60},{32,6... | collective-permute-start | bytes 2949128 | tf_op jit(solution)/shard_map/ppermute | solution.py:779
  53.7 23.2 %collective-permute-start.7 = (bf16[8,48,1280]{2,1,0:T(8,128)(2,1)}, bf16[8,48,1280]{2,1,0:T(8,128)(2,1)}, u32[]{:S(2)}, u32[]{:S(2)}) collective-permute-start(bf16[8,48,1280]{2,1,0:T(8,128)(2,1)} %slice_dynamic-update-slice_fusion.6.refs_8_.refs_10_.refs_7_.refs_3_), channel_id=1, source_target_pairs={{0,96},{4,100},{8,104},{12,108},{16,112},{20,116},{24,120},{28,124... | collective-permute-start | bytes 2949128 | tf_op jit(solution)/shard_map/ppermute | solution.py:779
  79.1 18.3 %collective-permute-start.16 = (bf16[4,48,1408]{2,1,0:T(8,128)(2,1)S(1)}, bf16[4,48,1408]{2,1,0:T(8,128)(2,1)S(1)}, u32[]{:S(2)}, u32[]{:S(2)}) collective-permute-start(bf16[4,48,1408]{2,1,0:T(8,128)(2,1)S(1)} %get-tuple-element.149), channel_id=1, source_target_pairs={{0,4},{4,8},{8,12},{12,0},{16,20},{20,24},{24,28},{28,16},{32,36},... | collective-permute-start | bytes 1622024 | tf_op jit(solution)/shard_map/ppermute | solution.py:779
  120.2 51.4 %collective-permute-start.19 = (bf16[8,48,1920]{2,1,0:T(8,128)(2,1)}, bf16[8,48,1920]{2,1,0:T(8,128)(2,1)}, u32[]{:S(2)}, u32[]{:S(2)}) collective-permute-start(bf16[8,48,1920]{2,1,0:T(8,128)(2,1)} %get-tuple-element.156.refs_1_.refs_5_), channel_id=1, source_target_pairs={{0,32},{4,36},{8,40},{12,44},{16,48},{20,52},{24,56},{28,60},{32,6... | collective-permute-start | bytes 4423688 | tf_op jit(solution)/shard_map/ppermute | solution.py:779
  121.5 50.1 %collective-permute-start.20 = (bf16[8,48,1920]{2,1,0:T(8,128)(2,1)}, bf16[8,48,1920]{2,1,0:T(8,128)(2,1)}, u32[]{:S(2)}, u32[]{:S(2)}) collective-permute-start(bf16[8,48,1920]{2,1,0:T(8,128)(2,1)} %get-tuple-element.156.refs_1_.refs_5_), channel_id=1, source_target_pairs={{0,96},{4,100},{8,104},{12,108},{16,112},{20,116},{24,120},{28,124... | collective-permute-start | bytes 4423688 | tf_op jit(solution)/shard_map/ppermute | solution.py:779
  123.0 48.7 %collective-permute-start.21 = (bf16[8,48,1920]{2,1,0:T(8,128)(2,1)}, bf16[8,48,1920]{2,1,0:T(8,128)(2,1)}, u32[]{:S(2)}, u32[]{:S(2)}) collective-permute-start(bf16[8,48,1920]{2,1,0:T(8,128)(2,1)} %get-tuple-element.157.refs_2_.refs_10_), channel_id=1, source_target_pairs={{0,4},{4,8},{8,12},{12,0},{16,20},{20,24},{24,28},{28,16},{32,36},... | collective-permute-start | bytes 4423688 | tf_op jit(solution)/shard_map/ppermute | solution.py:779
  124.3 47.4 %collective-permute-start.22 = (bf16[8,48,1920]{2,1,0:T(8,128)(2,1)}, bf16[8,48,1920]{2,1,0:T(8,128)(2,1)}, u32[]{:S(2)}, u32[]{:S(2)}) collective-permute-start(bf16[8,48,1920]{2,1,0:T(8,128)(2,1)} %get-tuple-element.157.refs_2_.refs_10_), channel_id=1, source_target_pairs={{0,12},{4,0},{8,4},{12,8},{16,28},{20,16},{24,20},{28,24},{32,44},... | collective-permute-start | bytes 4423688 | tf_op jit(solution)/shard_map/ppermute | solution.py:779
  177.9 21.6 %collective-permute-start.25 = (bf16[4,48,1920]{2,1,0:T(8,128)(2,1)S(1)}, bf16[4,48,1920]{2,1,0:T(8,128)(2,1)S(1)}, u32[]{:S(2)}, u32[]{:S(2)}) collective-permute-start(bf16[4,48,1920]{2,1,0:T(8,128)(2,1)S(1)} %get-tuple-element.162), channel_id=1, source_target_pairs={{0,32},{4,36},{8,40},{12,44},{16,48},{20,52},{24,56},{28,60},{32,6... | collective-permute-start | bytes 2211848 | tf_op jit(solution)/shard_map/ppermute | solution.py:779
  178.4 21.2 %collective-permute-start.26 = (bf16[4,48,1920]{2,1,0:T(8,128)(2,1)S(1)}, bf16[4,48,1920]{2,1,0:T(8,128)(2,1)S(1)}, u32[]{:S(2)}, u32[]{:S(2)}) collective-permute-start(bf16[4,48,1920]{2,1,0:T(8,128)(2,1)S(1)} %get-tuple-element.163), channel_id=1, source_target_pairs={{0,96},{4,100},{8,104},{12,108},{16,112},{20,116},{24,120},{28,124... | collective-permute-start | bytes 2211848 | tf_op jit(solution)/shard_map/ppermute | solution.py:779
  180.7 18.9 %collective-permute-start.27 = (bf16[4,48,1920]{2,1,0:T(8,128)(2,1)S(1)}, bf16[4,48,1920]{2,1,0:T(8,128)(2,1)S(1)}, u32[]{:S(2)}, u32[]{:S(2)}) collective-permute-start(bf16[4,48,1920]{2,1,0:T(8,128)(2,1)S(1)} %get-tuple-element.164), channel_id=1, source_target_pairs={{0,4},{4,8},{8,12},{12,0},{16,20},{20,24},{24,28},{28,16},{32,36},... | collective-permute-start | bytes 2211848 | tf_op jit(solution)/shard_map/ppermute | solution.py:779
  181.0 18.6 %collective-permute-start.28 = (bf16[4,48,1920]{2,1,0:T(8,128)(2,1)S(1)}, bf16[4,48,1920]{2,1,0:T(8,128)(2,1)S(1)}, u32[]{:S(2)}, u32[]{:S(2)}) collective-permute-start(bf16[4,48,1920]{2,1,0:T(8,128)(2,1)S(1)} %get-tuple-element.165), channel_id=1, source_target_pairs={{0,12},{4,0},{8,4},{12,8},{16,28},{20,16},{24,20},{28,24},{32,44},... | collective-permute-start | bytes 2211848 | tf_op jit(solution)/shard_map/ppermute | solution.py:779
  212.5 18.4 %collective-permute-start.31 = (bf16[128,1536]{1,0:T(8,128)(2,1)S(1)}, bf16[128,1536]{1,0:T(8,128)(2,1)S(1)}, u32[]{:S(2)}, u32[]{:S(2)}) collective-permute-start(bf16[128,1536]{1,0:T(8,128)(2,1)S(1)} %get-tuple-element.172), channel_id=1, source_target_pairs={{0,1},{1,0},{2,3},{3,2},{4,5},{5,4},{6,7},{7,6},{8,9},{9,8},{10,11... | collective-permute-start | bytes 1179656 | tf_op jit(solution)/shard_map/ppermute | solution.py:760
  225.5 49.2 %collective-permute-start.34 = (bf16[384,1920]{1,0:T(8,128)(2,1)}, bf16[384,1920]{1,0:T(8,128)(2,1)}, u32[]{:S(2)}, u32[]{:S(2)}) collective-permute-start(bf16[384,1920]{1,0:T(8,128)(2,1)} %get-tuple-element.189), channel_id=1, source_target_pairs={{0,32},{4,36},{8,40},{12,44},{16,48},{20,52},{24,56},{28,60},{32,6... | collective-permute-start | bytes 4423688 | tf_op jit(solution)/shard_map/ppermute | solution.py:779
  225.6 49.1 %collective-permute-start.35 = (bf16[384,1920]{1,0:T(8,128)(2,1)}, bf16[384,1920]{1,0:T(8,128)(2,1)}, u32[]{:S(2)}, u32[]{:S(2)}) collective-permute-start(bf16[384,1920]{1,0:T(8,128)(2,1)} %get-tuple-element.190), channel_id=1, source_target_pairs={{0,96},{4,100},{8,104},{12,108},{16,112},{20,116},{24,120},{28,124... | collective-permute-start | bytes 4423688 | tf_op jit(solution)/shard_map/ppermute | solution.py:779
  228.2 46.5 %collective-permute-start.36 = (bf16[384,1920]{1,0:T(8,128)(2,1)}, bf16[384,1920]{1,0:T(8,128)(2,1)}, u32[]{:S(2)}, u32[]{:S(2)}) collective-permute-start(bf16[384,1920]{1,0:T(8,128)(2,1)} %get-tuple-element.193), channel_id=1, source_target_pairs={{0,4},{4,8},{8,12},{12,0},{16,20},{20,24},{24,28},{28,16},{32,36},... | collective-permute-start | bytes 4423688 | tf_op jit(solution)/shard_map/ppermute | solution.py:779
  228.2 46.5 %collective-permute-start.37 = (bf16[384,1920]{1,0:T(8,128)(2,1)}, bf16[384,1920]{1,0:T(8,128)(2,1)}, u32[]{:S(2)}, u32[]{:S(2)}) collective-permute-start(bf16[384,1920]{1,0:T(8,128)(2,1)} %get-tuple-element.194), channel_id=1, source_target_pairs={{0,12},{4,0},{8,4},{12,8},{16,28},{20,16},{24,20},{28,24},{32,44},... | collective-permute-start | bytes 4423688 | tf_op jit(solution)/shard_map/ppermute | solution.py:779
  270.1 19.1 %all-to-all-start.3 = ((bf16[32,24,128]{2,1,0:T(8,128)(2,1)}), bf16[32,24,128]{2,1,0:T(8,128)(2,1)}, u32[]{:S(2)}, u32[]{:S(2)}) async-start(bf16[32,24,128]{2,1,0:T(8,128)(2,1)} %copy-done.43), calls=%async_computation.3 | async-start | bytes 393216 | tf_op jit(solution)/shard_map/all_to_all | solution.py:754
  283.7 35.4 %collective-permute-start.41 = (bf16[192,1920]{1,0:T(8,128)(2,1)}, bf16[192,1920]{1,0:T(8,128)(2,1)}, u32[]{:S(2)}, u32[]{:S(2)}) collective-permute-start(bf16[192,1920]{1,0:T(8,128)(2,1)} %get-tuple-element.197.refs_12_), channel_id=1, source_target_pairs={{0,32},{4,36},{8,40},{12,44},{16,48},{20,52},{24,56},{28,60},{32,6... | collective-permute-start | bytes 2211848 | tf_op jit(solution)/shard_map/ppermute | solution.py:779
  284.8 35.2 %collective-permute-start.42 = (bf16[192,1920]{1,0:T(8,128)(2,1)}, bf16[192,1920]{1,0:T(8,128)(2,1)}, u32[]{:S(2)}, u32[]{:S(2)}) collective-permute-start(bf16[192,1920]{1,0:T(8,128)(2,1)} %get-tuple-element.198.refs_13_), channel_id=1, source_target_pairs={{0,96},{4,100},{8,104},{12,108},{16,112},{20,116},{24,120},{28,124... | collective-permute-start | bytes 2211848 | tf_op jit(solution)/shard_map/ppermute | solution.py:779
  286.5 33.4 %collective-permute-start.43 = (bf16[192,1920]{1,0:T(8,128)(2,1)}, bf16[192,1920]{1,0:T(8,128)(2,1)}, u32[]{:S(2)}, u32[]{:S(2)}) collective-permute-start(bf16[192,1920]{1,0:T(8,128)(2,1)} %get-tuple-element.199.refs_14_), channel_id=1, source_target_pairs={{0,4},{4,8},{8,12},{12,0},{16,20},{20,24},{24,28},{28,16},{32,36},... | collective-permute-start | bytes 2211848 | tf_op jit(solution)/shard_map/ppermute | solution.py:779
  287.6 32.4 %collective-permute-start.44 = (bf16[192,1920]{1,0:T(8,128)(2,1)}, bf16[192,1920]{1,0:T(8,128)(2,1)}, u32[]{:S(2)}, u32[]{:S(2)}) collective-permute-start(bf16[192,1920]{1,0:T(8,128)(2,1)} %get-tuple-element.200.refs_15_), channel_id=1, source_target_pairs={{0,12},{4,0},{8,4},{12,8},{16,28},{20,16},{24,20},{28,24},{32,44},... | collective-permute-start | bytes 2211848 | tf_op jit(solution)/shard_map/ppermute | solution.py:779
  319.1 26.5 %collective-permute-start.29 = (bf16[128,1536]{1,0:T(8,128)(2,1)}, bf16[128,1536]{1,0:T(8,128)(2,1)S(1)}, u32[]{:S(2)}, u32[]{:S(2)}) collective-permute-start(bf16[128,1536]{1,0:T(8,128)(2,1)} %get-tuple-element.167), channel_id=1, source_target_pairs={{0,1},{1,0},{2,3},{3,2},{4,5},{5,4},{6,7},{7,6},{8,9},{9,8},{10,11... | collective-permute-start | bytes 1179656 | tf_op jit(solution)/shard_map/ppermute | solution.py:760
  334.0 29.7 %collective-permute-start.47 = (bf16[384,1280]{1,0:T(8,128)(2,1)}, bf16[384,1280]{1,0:T(8,128)(2,1)S(1)}, u32[]{:S(2)}, u32[]{:S(2)}) collective-permute-start(bf16[384,1280]{1,0:T(8,128)(2,1)} %get-tuple-element.225), channel_id=1, source_target_pairs={{0,32},{4,36},{8,40},{12,44},{16,48},{20,52},{24,56},{28,60},{32,6... | collective-permute-start | bytes 2949128 | tf_op jit(solution)/shard_map/ppermute | solution.py:779
  335.4 28.3 %collective-permute-start.48 = (bf16[384,1280]{1,0:T(8,128)(2,1)}, bf16[384,1280]{1,0:T(8,128)(2,1)S(1)}, u32[]{:S(2)}, u32[]{:S(2)}) collective-permute-start(bf16[384,1280]{1,0:T(8,128)(2,1)} %get-tuple-element.226), channel_id=1, source_target_pairs={{0,96},{4,100},{8,104},{12,108},{16,112},{20,116},{24,120},{28,124... | collective-permute-start | bytes 2949128 | tf_op jit(solution)/shard_map/ppermute | solution.py:779
  336.7 27.0 %collective-permute-start.49 = (bf16[384,1280]{1,0:T(8,128)(2,1)}, bf16[384,1280]{1,0:T(8,128)(2,1)S(1)}, u32[]{:S(2)}, u32[]{:S(2)}) collective-permute-start(bf16[384,1280]{1,0:T(8,128)(2,1)} %get-tuple-element.229), channel_id=1, source_target_pairs={{0,4},{4,8},{8,12},{12,0},{16,20},{20,24},{24,28},{28,16},{32,36},... | collective-permute-start | bytes 2949128 | tf_op jit(solution)/shard_map/ppermute | solution.py:779
  336.8 26.9 %collective-permute-start.50 = (bf16[384,1280]{1,0:T(8,128)(2,1)}, bf16[384,1280]{1,0:T(8,128)(2,1)S(1)}, u32[]{:S(2)}, u32[]{:S(2)}) collective-permute-start(bf16[384,1280]{1,0:T(8,128)(2,1)} %get-tuple-element.230), channel_id=1, source_target_pairs={{0,12},{4,0},{8,4},{12,8},{16,28},{20,16},{24,20},{28,24},{32,44},... | collective-permute-start | bytes 2949128 | tf_op jit(solution)/shard_map/ppermute | solution.py:779
  385.5 27.6 %collective-permute-start.55 = (bf16[96,3200]{1,0:T(8,128)(2,1)S(1)}, bf16[96,3200]{1,0:T(8,128)(2,1)S(1)}, u32[]{:S(2)}, u32[]{:S(2)}) collective-permute-start(bf16[96,3200]{1,0:T(8,128)(2,1)S(1)} %get-tuple-element.239), channel_id=1, source_target_pairs={{0,4},{4,8},{8,12},{12,0},{16,20},{20,24},{24,28},{28,16},{32,36},... | collective-permute-start | bytes 1843208 | tf_op jit(solution)/shard_map/ppermute | solution.py:779
  386.0 27.2 %collective-permute-start.56 = (bf16[96,3200]{1,0:T(8,128)(2,1)S(1)}, bf16[96,3200]{1,0:T(8,128)(2,1)S(1)}, u32[]{:S(2)}, u32[]{:S(2)}) collective-permute-start(bf16[96,3200]{1,0:T(8,128)(2,1)S(1)} %get-tuple-element.240), channel_id=1, source_target_pairs={{0,12},{4,0},{8,4},{12,8},{16,28},{20,16},{24,20},{28,24},{32,44},... | collective-permute-start | bytes 1843208 | tf_op jit(solution)/shard_map/ppermute | solution.py:779
  388.3 24.9 %collective-permute-start.57 = (bf16[96,3200]{1,0:T(8,128)(2,1)S(1)}, bf16[96,3200]{1,0:T(8,128)(2,1)S(1)}, u32[]{:S(2)}, u32[]{:S(2)}) collective-permute-start(bf16[96,3200]{1,0:T(8,128)(2,1)S(1)} %get-tuple-element.243), channel_id=1, source_target_pairs={{0,32},{4,36},{8,40},{12,44},{16,48},{20,52},{24,56},{28,60},{32,6... | collective-permute-start | bytes 1843208 | tf_op jit(solution)/shard_map/ppermute | solution.py:779
  388.6 24.6 %collective-permute-start.58 = (bf16[96,3200]{1,0:T(8,128)(2,1)S(1)}, bf16[96,3200]{1,0:T(8,128)(2,1)S(1)}, u32[]{:S(2)}, u32[]{:S(2)}) collective-permute-start(bf16[96,3200]{1,0:T(8,128)(2,1)S(1)} %get-tuple-element.244), channel_id=1, source_target_pairs={{0,96},{4,100},{8,104},{12,108},{16,112},{20,116},{24,120},{28,124... | collective-permute-start | bytes 1843208 | tf_op jit(solution)/shard_map/ppermute | solution.py:779
  (146 other events, 1764.0 us)
